TPU v7x, 256 devices: a whole 4x4x8 slice. The times are simulated.
256 devices in a mesh: gx: 8 (over z), gy: 4 (over x), gz: 8 (over y, core).
Axes of the slice: x: 4, y: 4, z: 8, core: 2. Of those that a mesh axis runs over, the one named last changes fastest.
Arguments:
- source: float32 [128, 64, 1024], P('gz', 'gy', 'gx'), may hold values from -6 to 6
- fraction: float32 [128, 64, 1024], P('gz', 'gy', 'gx'), may hold values from 0.35 to 1
Outputs:
- pressure: float32 [128, 64, 1024], P('gz', 'gy', 'gx')
- residual: float32 [128, 64, 1024], P('gz', 'gy', 'gx')
All inputs are finite; a program needn't handle non-finite values.
Results may differ from a plain program's by a relative error of at most 0.0003.
Values sent between devices are 32-bit elements; how exact they have to be, the bound alone decides.
No kernel may reach another device: no remote copies, remote signals or barrier semaphores. Data moves between devices by JAX's collectives and lax.ppermute only.
A program may use at most 128 MiB of HBM per device.

v0:
```python
import jax
import jax.numpy as jnp
from jax import lax
from jax.sharding import PartitionSpec as P

LEVELS = 5


RELAXATION = 0.8


def extended_2(shard, sides, width):
    for axis, dim in sides:
        size, length = (lax.axis_size(axis), shard.shape[dim])
        up = [(i, (i + 1) % size) for i in range(size - 1)]
        down = [(j, i) for i, j in up]
        last = lax.slice_in_dim(shard, length - width, length, axis=dim)
        leading = lax.slice_in_dim(shard, 0, width, axis=dim)
        before = lax.ppermute(last, axis, up)
        after = lax.ppermute(leading, axis, down)
        shard = jnp.concatenate([before, shard, after], axis=dim)
    return shard


def coarsen(values):
    extent_z, extent_y, extent_x = values.shape
    return values.reshape(extent_z // 2, 2, extent_y // 2, 2, extent_x // 2, 2).mean(axis=(1, 3, 5))


def refine(values):
    return jnp.repeat(jnp.repeat(jnp.repeat(values, 2, axis=0), 2, axis=1), 2, axis=2)


def face_weights(padded, weight_scale):
    centre = padded[1:-1, 1:-1, 1:-1]
    below_z = weight_scale * 0.5 * (centre + padded[:-2, 1:-1, 1:-1])
    above_z = weight_scale * 0.5 * (centre + padded[2:, 1:-1, 1:-1])
    below_y = weight_scale * 0.5 * (centre + padded[1:-1, :-2, 1:-1])
    above_y = weight_scale * 0.5 * (centre + padded[1:-1, 2:, 1:-1])
    below_x = weight_scale * 0.5 * (centre + padded[1:-1, 1:-1, :-2])
    above_x = weight_scale * 0.5 * (centre + padded[1:-1, 1:-1, 2:])
    diagonal = below_z + above_z + below_y + above_y + below_x + above_x
    return (below_z, above_z, below_y, above_y, below_x, above_x, diagonal)


def operate(extended, weights):
    below_z, above_z, below_y, above_y, below_x, above_x, diagonal = weights
    neighbours = below_z * extended[:-2, 1:-1, 1:-1] + above_z * extended[2:, 1:-1, 1:-1]
    neighbours = (
        neighbours + below_y * extended[1:-1, :-2, 1:-1] + above_y * extended[1:-1, 2:, 1:-1]
    )
    neighbours = (
        neighbours + below_x * extended[1:-1, 1:-1, :-2] + above_x * extended[1:-1, 1:-1, 2:]
    )
    return diagonal * extended[1:-1, 1:-1, 1:-1] - neighbours


def interior(weights):
    return tuple((member[1:-1, 1:-1, 1:-1] for member in weights))


def inside_mask(shape_now, starts, totals):
    markers = []
    for axis_pos in range(3):
        position = starts[axis_pos] - 1 + jnp.arange(shape_now[axis_pos] + 2, dtype=jnp.int32)
        markers.append(
            jnp.where((position >= 0) & (position < totals[axis_pos]), 1.0, 0.0).astype(jnp.float32)
        )
    return markers[0][:, None, None] * markers[1][None, :, None] * markers[2][None, None, :]


def near_rim(values, spread):
    if spread:
        return extended_2(values, (("gx", 2), ("gy", 1), ("gz", 0)), 1)
    return jnp.pad(values, 1)


def prepare_level(fraction_now, weight_scale, spread, starts, totals):
    if spread:
        rimmed = extended_2(fraction_now, (("gx", 2), ("gy", 1), ("gz", 0)), 2)
    else:
        rimmed = jnp.pad(fraction_now, 2)
    weights = face_weights(rimmed, weight_scale)
    inside = inside_mask(fraction_now.shape, starts, totals)
    safe_diag = jnp.where(inside > 0.5, weights[6], 1.0)
    return (weights, interior(weights), inside, safe_diag)


def relax_down(source_now, level_data, spread):
    weights, weights_in, inside, safe_diag = level_data
    diagonal = weights_in[6]
    first_sweep = RELAXATION * source_now / diagonal
    first_rim = near_rim(first_sweep, spread)
    second = first_sweep + RELAXATION * (source_now - operate(first_rim, weights_in)) / diagonal
    residue = source_now - operate(near_rim(second, spread), weights_in)
    return (second, residue, source_now)


def relax_up(pressure, source_now, level_data, spread):
    weights, weights_in, inside, safe_diag = level_data
    diagonal = weights_in[6]
    first_sweep = (
        pressure
        + RELAXATION * (source_now - operate(near_rim(pressure, spread), weights_in)) / diagonal
    )
    first_rim = near_rim(first_sweep, spread)
    first_sweep = first_rim[1:-1, 1:-1, 1:-1]
    return first_sweep + RELAXATION * (source_now - operate(first_rim, weights_in)) / diagonal


def assemble(pieces, counts):
    count_z, count_y, count_x = counts
    brick_z, brick_y, brick_x = pieces.shape[1:]
    blocks = pieces.reshape(count_x, count_y, count_z, brick_z, brick_y, brick_x)
    blocks = blocks.transpose(2, 3, 1, 4, 0, 5)
    return blocks.reshape(count_z * brick_z, count_y * brick_y, count_x * brick_x)


def bottom_matrix(fraction_now, weight_scale, count):
    extent_z, extent_y, extent_x = fraction_now.shape
    order_size = extent_z * extent_y * extent_x
    plane_size = extent_y * extent_x
    flat_fraction = fraction_now.reshape(order_size)
    diagonal = face_weights(jnp.pad(fraction_now, 1), weight_scale)[6].reshape(order_size)
    row_index = jnp.arange(order_size, dtype=jnp.int32)[:, None]
    col_index = jnp.arange(count, dtype=jnp.int32)[None, :]
    apart = (
        jnp.abs(row_index // plane_size - col_index // plane_size)
        + jnp.abs(row_index // extent_x % extent_y - col_index // extent_x % extent_y)
        + jnp.abs(row_index % extent_x - col_index % extent_x)
    )
    linked = -weight_scale * 0.5 * (flat_fraction[:, None] + flat_fraction[None, :])
    return jnp.where(apart == 0, diagonal[:, None], jnp.where(apart == 1, linked, 0.0))


def bottom_solve(fraction_low, source_low, weight_scale):
    order_size = fraction_low.size
    factor = jnp.linalg.cholesky(bottom_matrix(fraction_low, weight_scale, order_size))
    solved = jax.scipy.linalg.cho_solve((factor, True), source_low.reshape(order_size))
    return solved.reshape(fraction_low.shape)


def local(source, fraction):
    gather_at = 3
    counts = (lax.axis_size("gz"), lax.axis_size("gy"), lax.axis_size("gx"))
    places = (lax.axis_index("gz"), lax.axis_index("gy"), lax.axis_index("gx"))
    fractions = [fraction]
    for level_index in range(gather_at):
        fractions.append(coarsen(fractions[-1]))
    prepared = []
    sources = []
    pressures = []
    source_rims = []
    source_now = source
    local_shape = source.shape
    for level_index in range(LEVELS):
        if level_index == gather_at:
            local_shape = source_now.shape
            gathered = (
                lax.all_gather(source_now[None], ("gx", "gy", "gz"), axis=0, tiled=True),
                lax.all_gather(fractions[gather_at][None], ("gx", "gy", "gz"), axis=0, tiled=True),
            )
            source_now = assemble(gathered[0], counts)
            fractions[gather_at] = assemble(gathered[1], counts)
        spread = level_index < gather_at
        fraction_now = fractions[level_index]
        if spread:
            starts = tuple(
                (places[axis_pos] * fraction_now.shape[axis_pos] for axis_pos in range(3))
            )
            totals = tuple(
                (counts[axis_pos] * fraction_now.shape[axis_pos] for axis_pos in range(3))
            )
        else:
            starts = (0, 0, 0)
            totals = fraction_now.shape
        level_data = prepare_level(fraction_now, 0.25**level_index, spread, starts, totals)
        pressure, residue, source_rim = relax_down(source_now, level_data, spread)
        prepared.append(level_data)
        sources.append(source_now)
        pressures.append(pressure)
        source_rims.append(source_rim)
        if level_index >= gather_at:
            fractions.append(coarsen(fraction_now))
        source_now = coarsen(residue)
    pressure = bottom_solve(fractions[LEVELS], source_now, 0.25**LEVELS)
    for level_index in reversed(range(LEVELS)):
        if level_index == gather_at - 1:
            corner = tuple((places[axis_pos] * local_shape[axis_pos] for axis_pos in range(3)))
            pressure = lax.dynamic_slice(pressure, corner, local_shape)
        pressure = pressures[level_index] + refine(pressure)
        pressure = relax_up(
            pressure, sources[level_index], prepared[level_index], level_index < gather_at
        )
    residue = source - operate(near_rim(pressure, True), prepared[0][1])
    return (pressure, residue)


def solution(mesh):
    return jax.shard_map(
        local,
        mesh=mesh,
        in_specs=(P("gz", "gy", "gx"), P("gz", "gy", "gx")),
        out_specs=(P("gz", "gy", "gx"), P("gz", "gy", "gx")),
        check_vma=False,
    )
```

profile of v0, /device:TPU:142, one launch (start us, length us, event | category | flops | bytes accessed | tf_op | source)
XLA Modules:
  0.0 657.1 jit_solution(6898633250614371456)
XLA Ops:
  3.7 3.8 collective-permute-start
  7.6 10.5 %reshape.382 = f32[8,2,8,2,64,2]{5,4,3,2,1,0:T(8,128)} reshape(f32[16,16,128]{2,1,0:T(8,128)} %param.3) | data formatting | bytes 262144 | tf_op jit(solution)/shard_map/reshape | solution.py:27
  18.1 4.0 reduce_sum.98
  22.2 3.2 collective-permute-start.19
  29.4 4.4 collective-permute-start.37
  34.0 66.3 %all-gather.1 = f32[512,2,16]{2,1,0:T(2,128)S(1)} all-gather(f32[2,2,16]{2,1,0:T(2,128)S(1)} %broadcast_multiply_fusion.5), channel_id=3, replica_groups=mesh['gx'=8,'gy'=4,'gz'=8] {'gx','gy','gz'}, dimensions={0}, use_global_device_ids=true | all-gather | bytes 65792 | tf_op jit(solution)/shard_map/all_gather | solution.py:161
  102.8 11.7 %cholesky.49 = f32[128,128]{1,0:T(8,128)S(1)} custom-call(f32[128,128]{1,0:T(8,128)S(1)} %cholesky.115), custom_call_target="Cholesky" | custom-call | tf_op jit(solution)/shard_map/jit(cholesky)/cholesky | solution.py:138
  114.6 9.8 %custom-call.18 = f32[1,128,128]{1,2,0:T(8,128)S(1)} custom-call(f32[1,128,128]{2,1,0:T(8,128)S(1)} %get-tuple-element.107), custom_call_target="InvertDiagBlocksLowerTriangular" | custom-call | tf_op jit(solution)/shard_map/jit(cholesky)/cholesky | solution.py:138
  124.9 11.9 %cholesky.103 = f32[128,128]{1,0:T(8,128)S(1)} custom-call(f32[128,128]{1,0:T(8,128)S(1)} %convolution_subtract_fusion), custom_call_target="Cholesky" | custom-call | tf_op jit(solution)/shard_map/jit(cholesky)/cholesky | solution.py:138
  144.5 6.8 %while.1 = (s32[]{:T(128)}, f32[256,256]{1,0:T(8,128)}, s32[2,2]{1,0:T(2,128)S(1)}, f32[2,128,128]{2,1,0:T(8,128)}, s32[]{:T(128)}) while((s32[]{:T(128)}, f32[256,256]{1,0:T(8,128)}, s32[2,2]{1,0:T(2,128)S(1)}, f32[2,128,128]{2,1,0:T(8,128)}, s32[]{:T(128)}) %tuple.106), condition=%wide.while_cond, body=%wide.while_body.sunk | while | flops 2 | bytes 132205 | solution.py:139
  145.1 2.8 bitcast_dynamic-update-slice_fusion.2
  156.5 3.6 collective-permute-start.5
  163.8 5.1 collective-permute-start.7
  172.5 5.3 collective-permute-done.6
  178.0 4.5 collective-permute-start.9
  184.0 4.5 collective-permute-start.21
  196.5 3.6 collective-permute-start.23
  202.8 3.9 collective-permute-start.12
  207.7 3.1 collective-permute-done.12
  211.0 4.5 collective-permute-start.15
  217.2 4.0 collective-permute-done.14
  229.0 9.8 %reshape.381 = f32[8,2,8,2,64,2]{5,4,3,2,1,0:T(8,128)} reshape(f32[16,16,128]{2,1,0:T(8,128)S(1)} %fusion.76) | data formatting | bytes 262144 | tf_op jit(solution)/shard_map/reshape | solution.py:27
  238.8 4.0 reduce_sum.97
  244.9 3.9 collective-permute-start.24
  248.8 3.0 collective-permute-start.39
  253.3 4.5 collective-permute-start.27
  259.3 4.1 collective-permute-done.26
  270.5 2.9 collective-permute-start.41
  273.7 3.1 collective-permute-start.31
  279.7 4.2 collective-permute-done.30
  284.0 3.1 collective-permute-start.33
  289.2 3.4 collective-permute-done.32
  306.0 4.1 collective-permute-start.42
  310.1 2.8 collective-permute-done.42
  316.3 3.4 fusion.13
  326.9 21.1 %custom-call.19 = f32[2,128,128]{1,2,0:T(8,128)} custom-call(f32[2,128,128]{2,1,0:T(8,128)} %get-tuple-element.9), custom_call_target="InvertDiagBlocksLowerTriangular" | custom-call | tf_op jit(solution)/shard_map/jit(_cho_solve)/triangular_solve | solution.py:139
  351.0 3.9 collective-permute-start.48
  354.9 2.8 collective-permute-done.48
  357.8 3.8 collective-permute-start.51
  362.9 4.2 collective-permute-done.50
  375.2 65.6 %all-gather = f32[512,2,16]{2,1,0:T(2,128)S(1)} all-gather(f32[2,2,16]{2,1,0:T(2,128)S(1)} %broadcast_multiply_fusion.6), channel_id=2, replica_groups=mesh['gx'=8,'gy'=4,'gz'=8] {'gx','gy','gz'}, dimensions={0}, use_global_device_ids=true | all-gather | bytes 65792 | tf_op jit(solution)/shard_map/all_gather | solution.py:160
  446.0 5.5 reshape.389
  469.3 3.1 collective-permute-start.55
  475.1 4.0 collective-permute-done.54
  483.3 4.2 collective-permute-done.56
  497.4 3.9 collective-permute-start.60
  501.3 2.8 collective-permute-done.60
  508.1 4.2 collective-permute-done.62
  522.5 3.9 collective-permute-start.66
  526.4 3.1 collective-permute-done.66
  529.6 3.9 collective-permute-start.69
  534.8 4.2 collective-permute-done.68
  549.2 3.9 collective-permute-start.72
  553.2 3.1 collective-permute-done.72
  559.6 4.2 collective-permute-done.74
  578.3 3.9 collective-permute-start.78
  583.2 3.1 collective-permute-done.78
  589.9 4.2 collective-permute-done.80
  604.9 3.9 collective-permute-start.84
  609.9 3.1 collective-permute-done.84
  616.6 4.2 collective-permute-done.86
  631.6 3.9 collective-permute-start.90
  636.5 3.1 collective-permute-done.90
  643.2 4.2 collective-permute-done.92
  (396 shorter events, 236.2 us)
Async XLA Ops:
  1.7 138.4 %collective-permute-start.1 = (f32[16,16,2]{2,1,0:T(8,128)S(1)}, f32[16,16,2]{2,1,0:T(8,128)S(1)}, u32[]{:S(2)}, u32[]{:S(2)}) collective-permute-start(f32[16,16,2]{2,1,0:T(8,128)S(1)} %get-tuple-element.77), channel_id=1, source_target_pairs={{32,0},{64,32},{96,64},{128,96},{160,128},{192,160},{224,192},{33,... | collective-permute-start | bytes 6152 | tf_op jit(solution)/shard_map/ppermute | solution.py:20
  3.7 136.4 %collective-permute-start = (f32[16,16,2]{2,1,0:T(8,128)S(1)}, f32[16,16,2]{2,1,0:T(8,128)S(1)}, u32[]{:S(2)}, u32[]{:S(2)}) collective-permute-start(f32[16,16,2]{2,1,0:T(8,128)S(1)} %get-tuple-element.76), channel_id=1, source_target_pairs={{0,32},{32,64},{64,96},{96,128},{128,160},{160,192},{192,224},{1,3... | collective-permute-start | bytes 6152 | tf_op jit(solution)/shard_map/ppermute | solution.py:19
  22.2 161.7 %collective-permute-start.19 = (f32[8,8,2]{2,1,0:T(8,128)S(1)}, f32[8,8,2]{2,1,0:T(8,128)S(1)}, u32[]{:S(2)}, u32[]{:S(2)}) collective-permute-start(f32[8,8,2]{2,1,0:T(8,128)S(1)} %get-tuple-element.129), channel_id=1, source_target_pairs={{32,0},{64,32},{96,64},{128,96},{160,128},{192,160},{224,192},{33,... | collective-permute-start | bytes 1544 | tf_op jit(solution)/shard_map/ppermute | solution.py:20
  25.4 158.5 %collective-permute-start.18 = (f32[8,8,2]{2,1,0:T(8,128)S(1)}, f32[8,8,2]{2,1,0:T(8,128)S(1)}, u32[]{:S(2)}, u32[]{:S(2)}) collective-permute-start(f32[8,8,2]{2,1,0:T(8,128)S(1)} %get-tuple-element.128), channel_id=1, source_target_pairs={{0,32},{32,64},{64,96},{96,128},{128,160},{160,192},{192,224},{1,3... | collective-permute-start | bytes 1544 | tf_op jit(solution)/shard_map/ppermute | solution.py:19
  29.4 127.1 %collective-permute-start.37 = (f32[4,4,2]{2,1,0:T(4,128)S(1)}, f32[4,4,2]{2,1,0:T(4,128)S(1)}, u32[]{:S(2)}, u32[]{:S(2)}) collective-permute-start(f32[4,4,2]{2,1,0:T(4,128)S(1)} %get-tuple-element.165), channel_id=1, source_target_pairs={{32,0},{64,32},{96,64},{128,96},{160,128},{192,160},{224,192},{33,... | collective-permute-start | bytes 392 | tf_op jit(solution)/shard_map/ppermute | solution.py:20
  140.4 12.0 %collective-permute-start.3 = (f32[16,2,132]{2,0,1:T(8,128)S(1)}, f32[16,2,132]{2,0,1:T(8,128)S(1)}, u32[]{:S(2)}, u32[]{:S(2)}) collective-permute-start(f32[16,2,132]{2,0,1:T(8,128)S(1)} %copy.1153), channel_id=1, source_target_pairs={{8,0},{16,8},{24,16},{9,1},{17,9},{25,17},{10,2},{18,10},{26,18},{... | collective-permute-start | bytes 50696 | tf_op jit(solution)/shard_map/ppermute | solution.py:20
  143.1 11.3 %collective-permute-start.2 = (f32[16,2,132]{2,0,1:T(8,128)S(1)}, f32[16,2,132]{2,0,1:T(8,128)S(1)}, u32[]{:S(2)}, u32[]{:S(2)}) collective-permute-start(f32[16,2,132]{2,0,1:T(8,128)S(1)} %copy.1152), channel_id=1, source_target_pairs={{0,8},{8,16},{16,24},{1,9},{9,17},{17,25},{2,10},{10,18},{18,26},{... | collective-permute-start | bytes 50696 | tf_op jit(solution)/shard_map/ppermute | solution.py:19
  152.4 7.7 %collective-permute-start.36 = (f32[4,4,2]{2,1,0:T(4,128)S(1)}, f32[4,4,2]{2,1,0:T(4,128)S(1)}, u32[]{:S(2)}, u32[]{:S(2)}) collective-permute-start(f32[4,4,2]{2,1,0:T(4,128)S(1)} %get-tuple-element.164), channel_id=1, source_target_pairs={{0,32},{32,64},{64,96},{96,128},{128,160},{160,192},{192,224},{1,3... | collective-permute-start | bytes 392 | tf_op jit(solution)/shard_map/ppermute | solution.py:19
  154.5 5.7 collective-permute-start.4
  163.8 8.8 %collective-permute-start.7 = (f32[16,16,1]{2,1,0:T(8,128)S(1)}, f32[16,16,1]{2,1,0:T(8,128)S(1)}, u32[]{:S(2)}, u32[]{:S(2)}) collective-permute-start(f32[16,16,1]{2,1,0:T(8,128)S(1)} %get-tuple-element.75), channel_id=1, source_target_pairs={{32,0},{64,32},{96,64},{128,96},{160,128},{192,160},{224,192},{33,... | collective-permute-start | bytes 3080 | tf_op jit(solution)/shard_map/ppermute | solution.py:20
  168.9 9.0 %collective-permute-start.6 = (f32[16,16,1]{2,1,0:T(8,128)S(1)}, f32[16,16,1]{2,1,0:T(8,128)S(1)}, u32[]{:S(2)}, u32[]{:S(2)}) collective-permute-start(f32[16,16,1]{2,1,0:T(8,128)S(1)} %get-tuple-element.74), channel_id=1, source_target_pairs={{0,32},{32,64},{64,96},{96,128},{128,160},{160,192},{192,224},{1,3... | collective-permute-start | bytes 3080 | tf_op jit(solution)/shard_map/ppermute | solution.py:19
  178.0 11.9 %collective-permute-start.9 = (f32[16,1,130]{2,0,1:T(8,128)S(1)}, f32[16,1,130]{2,0,1:T(8,128)S(1)}, u32[]{:S(2)}, u32[]{:S(2)}) collective-permute-start(f32[16,1,130]{2,0,1:T(8,128)S(1)} %copy.1098), channel_id=1, source_target_pairs={{8,0},{16,8},{24,16},{9,1},{17,9},{25,17},{10,2},{18,10},{26,18},{... | collective-permute-start | bytes 24968 | tf_op jit(solution)/shard_map/ppermute | solution.py:20
  182.6 7.3 %collective-permute-start.8 = (f32[16,1,130]{2,0,1:T(8,128)S(1)}, f32[16,1,130]{2,0,1:T(8,128)S(1)}, u32[]{:S(2)}, u32[]{:S(2)}) collective-permute-start(f32[16,1,130]{2,0,1:T(8,128)S(1)} %copy.1097), channel_id=1, source_target_pairs={{0,8},{8,16},{16,24},{1,9},{9,17},{17,25},{2,10},{10,18},{18,26},{... | collective-permute-start | bytes 24968 | tf_op jit(solution)/shard_map/ppermute | solution.py:19
  184.0 10.4 %collective-permute-start.21 = (f32[8,2,68]{2,1,0:T(2,128)S(1)}, f32[8,2,68]{2,1,0:T(2,128)S(1)}, u32[]{:S(2)}, u32[]{:S(2)}) collective-permute-start(f32[8,2,68]{2,1,0:T(2,128)S(1)} %get-tuple-element.101), channel_id=1, source_target_pairs={{8,0},{16,8},{24,16},{9,1},{17,9},{25,17},{10,2},{18,10},{26,18},{... | collective-permute-start | bytes 13064 | tf_op jit(solution)/shard_map/ppermute | solution.py:20
  188.6 5.8 collective-permute-start.20
  190.1 10.0 %collective-permute-start.11 = (f32[1,18,130]{2,1,0:T(8,128)S(1)}, f32[1,18,130]{2,1,0:T(8,128)S(1)}, u32[]{:S(2)}, u32[]{:S(2)}) collective-permute-start(f32[1,18,130]{2,1,0:T(8,128)S(1)} %get-tuple-element.51), channel_id=1, source_target_pairs={{1,0},{2,1},{3,2},{4,3},{5,4},{6,5},{7,6},{9,8},{10,9},{11,10},{12... | collective-permute-start | bytes 28088 | tf_op jit(solution)/shard_map/ppermute | solution.py:20
  192.0 8.1 %collective-permute-start.10 = (f32[1,18,130]{2,1,0:T(8,128)S(1)}, f32[1,18,130]{2,1,0:T(8,128)S(1)}, u32[]{:S(2)}, u32[]{:S(2)}) collective-permute-start(f32[1,18,130]{2,1,0:T(8,128)S(1)} %get-tuple-element.50), channel_id=1, source_target_pairs={{0,1},{1,2},{2,3},{3,4},{4,5},{5,6},{6,7},{8,9},{9,10},{10,11},{11... | collective-permute-start | bytes 28088 | tf_op jit(solution)/shard_map/ppermute | solution.py:19
  194.5 12.2 %collective-permute-start.22 = (f32[2,12,68]{2,1,0:T(8,128)S(1)}, f32[2,12,68]{2,1,0:T(8,128)S(1)}, u32[]{:S(2)}, u32[]{:S(2)}) collective-permute-start(f32[2,12,68]{2,1,0:T(8,128)S(1)} %get-tuple-element.78), channel_id=1, source_target_pairs={{0,1},{1,2},{2,3},{3,4},{4,5},{5,6},{6,7},{8,9},{9,10},{10,11},{11... | collective-permute-start | bytes 19592 | tf_op jit(solution)/shard_map/ppermute | solution.py:19
  196.5 10.2 %collective-permute-start.23 = (f32[2,12,68]{2,1,0:T(8,128)S(1)}, f32[2,12,68]{2,1,0:T(8,128)S(1)}, u32[]{:S(2)}, u32[]{:S(2)}) collective-permute-start(f32[2,12,68]{2,1,0:T(8,128)S(1)} %get-tuple-element.79), channel_id=1, source_target_pairs={{1,0},{2,1},{3,2},{4,3},{5,4},{6,5},{7,6},{9,8},{10,9},{11,10},{12... | collective-permute-start | bytes 19592 | tf_op jit(solution)/shard_map/ppermute | solution.py:20
  200.8 6.9 %collective-permute-start.13 = (f32[16,16,1]{2,1,0:T(8,128)S(1)}, f32[16,16,1]{2,1,0:T(8,128)S(1)}, u32[]{:S(2)}, u32[]{:S(2)}) collective-permute-start(f32[16,16,1]{2,1,0:T(8,128)S(1)} %get-tuple-element.73), channel_id=1, source_target_pairs={{32,0},{64,32},{96,64},{128,96},{160,128},{192,160},{224,192},{33,... | collective-permute-start | bytes 3080 | tf_op jit(solution)/shard_map/ppermute | solution.py:20
  202.8 8.1 %collective-permute-start.12 = (f32[16,16,1]{2,1,0:T(8,128)S(1)}, f32[16,16,1]{2,1,0:T(8,128)S(1)}, u32[]{:S(2)}, u32[]{:S(2)}) collective-permute-start(f32[16,16,1]{2,1,0:T(8,128)S(1)} %get-tuple-element.72), channel_id=1, source_target_pairs={{0,32},{32,64},{64,96},{96,128},{128,160},{160,192},{192,224},{1,3... | collective-permute-start | bytes 3080 | tf_op jit(solution)/shard_map/ppermute | solution.py:19
  211.0 6.2 collective-permute-start.15
  215.6 5.6 collective-permute-start.14
  243.0 10.2 %collective-permute-start.25 = (f32[8,8,1]{2,1,0:T(8,128)S(1)}, f32[8,8,1]{2,1,0:T(8,128)S(1)}, u32[]{:S(2)}, u32[]{:S(2)}) collective-permute-start(f32[8,8,1]{2,1,0:T(8,128)S(1)} %get-tuple-element.127), channel_id=1, source_target_pairs={{32,0},{64,32},{96,64},{128,96},{160,128},{192,160},{224,192},{33,... | collective-permute-start | bytes 776 | tf_op jit(solution)/shard_map/ppermute | solution.py:20
  244.9 8.3 %collective-permute-start.24 = (f32[8,8,1]{2,1,0:T(8,128)S(1)}, f32[8,8,1]{2,1,0:T(8,128)S(1)}, u32[]{:S(2)}, u32[]{:S(2)}) collective-permute-start(f32[8,8,1]{2,1,0:T(8,128)S(1)} %get-tuple-element.126), channel_id=1, source_target_pairs={{0,32},{32,64},{64,96},{96,128},{128,160},{160,192},{192,224},{1,3... | collective-permute-start | bytes 776 | tf_op jit(solution)/shard_map/ppermute | solution.py:19
  248.8 10.3 %collective-permute-start.39 = (f32[4,2,36]{2,1,0:T(2,128)S(1)}, f32[4,2,36]{2,1,0:T(2,128)S(1)}, u32[]{:S(2)}, u32[]{:S(2)}) collective-permute-start(f32[4,2,36]{2,1,0:T(2,128)S(1)} %get-tuple-element.163), channel_id=1, source_target_pairs={{8,0},{16,8},{24,16},{9,1},{17,9},{25,17},{10,2},{18,10},{26,18},{... | collective-permute-start | bytes 3464 | tf_op jit(solution)/shard_map/ppermute | solution.py:20
  251.9 7.3 %collective-permute-start.38 = (f32[4,2,36]{2,1,0:T(2,128)S(1)}, f32[4,2,36]{2,1,0:T(2,128)S(1)}, u32[]{:S(2)}, u32[]{:S(2)}) collective-permute-start(f32[4,2,36]{2,1,0:T(2,128)S(1)} %get-tuple-element.162), channel_id=1, source_target_pairs={{0,8},{8,16},{16,24},{1,9},{9,17},{17,25},{2,10},{10,18},{18,26},{... | collective-permute-start | bytes 3464 | tf_op jit(solution)/shard_map/ppermute | solution.py:19
  253.3 6.0 collective-permute-start.27
  257.9 5.5 collective-permute-start.26
  263.4 9.9 %collective-permute-start.29 = (f32[1,10,66]{2,1,0:T(8,128)S(1)}, f32[1,10,66]{2,1,0:T(8,128)S(1)}, u32[]{:S(2)}, u32[]{:S(2)}) collective-permute-start(f32[1,10,66]{2,1,0:T(8,128)S(1)} %get-tuple-element.87), channel_id=1, source_target_pairs={{1,0},{2,1},{3,2},{4,3},{5,4},{6,5},{7,6},{9,8},{10,9},{11,10},{12... | collective-permute-start | bytes 7928 | tf_op jit(solution)/shard_map/ppermute | solution.py:20
  265.4 8.0 %collective-permute-start.28 = (f32[1,10,66]{2,1,0:T(8,128)S(1)}, f32[1,10,66]{2,1,0:T(8,128)S(1)}, u32[]{:S(2)}, u32[]{:S(2)}) collective-permute-start(f32[1,10,66]{2,1,0:T(8,128)S(1)} %get-tuple-element.86), channel_id=1, source_target_pairs={{0,1},{1,2},{2,3},{3,4},{4,5},{5,6},{6,7},{8,9},{9,10},{10,11},{11... | collective-permute-start | bytes 7928 | tf_op jit(solution)/shard_map/ppermute | solution.py:19
  267.8 11.8 %collective-permute-start.40 = (f32[2,8,36]{2,1,0:T(8,128)S(1)}, f32[2,8,36]{2,1,0:T(8,128)S(1)}, u32[]{:S(2)}, u32[]{:S(2)}) collective-permute-start(f32[2,8,36]{2,1,0:T(8,128)S(1)} %get-tuple-element.152), channel_id=1, source_target_pairs={{0,1},{1,2},{2,3},{3,4},{4,5},{5,6},{6,7},{8,9},{9,10},{10,11},{11... | collective-permute-start | bytes 6920 | tf_op jit(solution)/shard_map/ppermute | solution.py:19
  270.5 9.1 %collective-permute-start.41 = (f32[2,8,36]{2,1,0:T(8,128)S(1)}, f32[2,8,36]{2,1,0:T(8,128)S(1)}, u32[]{:S(2)}, u32[]{:S(2)}) collective-permute-start(f32[2,8,36]{2,1,0:T(8,128)S(1)} %get-tuple-element.153), channel_id=1, source_target_pairs={{1,0},{2,1},{3,2},{4,3},{5,4},{6,5},{7,6},{9,8},{10,9},{11,10},{12... | collective-permute-start | bytes 6920 | tf_op jit(solution)/shard_map/ppermute | solution.py:20
  273.7 6.0 collective-permute-start.31
  276.9 7.0 %collective-permute-start.30 = (f32[8,8,1]{2,1,0:T(8,128)S(1)}, f32[8,8,1]{2,1,0:T(8,128)S(1)}, u32[]{:S(2)}, u32[]{:S(2)}) collective-permute-start(f32[8,8,1]{2,1,0:T(8,128)S(1)} %get-tuple-element.124), channel_id=1, source_target_pairs={{0,32},{32,64},{64,96},{96,128},{128,160},{160,192},{192,224},{1,3... | collective-permute-start | bytes 776 | tf_op jit(solution)/shard_map/ppermute | solution.py:19
  287.1 5.5 collective-permute-start.32
  304.1 6.1 collective-permute-start.43
  306.0 7.0 %collective-permute-start.42 = (f32[4,4,1]{2,1,0:T(4,128)S(1)}, f32[4,4,1]{2,1,0:T(4,128)S(1)}, u32[]{:S(2)}, u32[]{:S(2)}) collective-permute-start(f32[4,4,1]{2,1,0:T(4,128)S(1)} %get-tuple-element.160), channel_id=1, source_target_pairs={{0,32},{32,64},{64,96},{96,128},{128,160},{160,192},{192,224},{1,3... | collective-permute-start | bytes 200 | tf_op jit(solution)/shard_map/ppermute | solution.py:19
  313.0 6.6 %collective-permute-start.45 = (f32[4,1,34]{2,1,0:T(1,128)S(1)}, f32[4,1,34]{2,1,0:T(1,128)S(1)}, u32[]{:S(2)}, u32[]{:S(2)}) collective-permute-start(f32[4,1,34]{2,1,0:T(1,128)S(1)} %get-tuple-element.145), channel_id=1, source_target_pairs={{8,0},{16,8},{24,16},{9,1},{17,9},{25,17},{10,2},{18,10},{26,18},{... | collective-permute-start | bytes 1640 | tf_op jit(solution)/shard_map/ppermute | solution.py:20
  320.5 27.5 %collective-permute-start.47 = (f32[1,6,34]{2,1,0:T(8,128)S(1)}, f32[1,6,34]{2,1,0:T(8,128)S(1)}, u32[]{:S(2)}, u32[]{:S(2)}) collective-permute-start(f32[1,6,34]{2,1,0:T(8,128)S(1)} %get-tuple-element.137), channel_id=1, source_target_pairs={{1,0},{2,1},{3,2},{4,3},{5,4},{6,5},{7,6},{9,8},{10,9},{11,10},{12... | collective-permute-start | bytes 2456 | tf_op jit(solution)/shard_map/ppermute | solution.py:20
  322.4 25.6 %collective-permute-start.46 = (f32[1,6,34]{2,1,0:T(8,128)S(1)}, f32[1,6,34]{2,1,0:T(8,128)S(1)}, u32[]{:S(2)}, u32[]{:S(2)}) collective-permute-start(f32[1,6,34]{2,1,0:T(8,128)S(1)} %get-tuple-element.136), channel_id=1, source_target_pairs={{0,1},{1,2},{2,3},{3,4},{4,5},{5,6},{6,7},{8,9},{9,10},{10,11},{11... | collective-permute-start | bytes 2456 | tf_op jit(solution)/shard_map/ppermute | solution.py:19
  349.1 5.9 collective-permute-start.49
  351.0 6.8 %collective-permute-start.48 = (f32[4,4,1]{2,1,0:T(4,128)S(1)}, f32[4,4,1]{2,1,0:T(4,128)S(1)}, u32[]{:S(2)}, u32[]{:S(2)}) collective-permute-start(f32[4,4,1]{2,1,0:T(4,128)S(1)} %get-tuple-element.158), channel_id=1, source_target_pairs={{0,32},{32,64},{64,96},{96,128},{128,160},{160,192},{192,224},{1,3... | collective-permute-start | bytes 200 | tf_op jit(solution)/shard_map/ppermute | solution.py:19
  469.3 5.9 collective-permute-start.55
  472.4 6.8 %collective-permute-start.54 = (f32[4,4,1]{2,1,0:T(4,128)S(1)}, f32[4,4,1]{2,1,0:T(4,128)S(1)}, u32[]{:S(2)}, u32[]{:S(2)}) collective-permute-start(f32[4,4,1]{2,1,0:T(4,128)S(1)} %get-tuple-element.156), channel_id=1, source_target_pairs={{0,32},{32,64},{64,96},{96,128},{128,160},{160,192},{192,224},{1,3... | collective-permute-start | bytes 200 | tf_op jit(solution)/shard_map/ppermute | solution.py:19
  482.0 5.5 collective-permute-start.56
  495.4 5.9 collective-permute-start.61
  497.4 6.8 %collective-permute-start.60 = (f32[4,4,1]{2,1,0:T(4,128)S(1)}, f32[4,4,1]{2,1,0:T(4,128)S(1)}, u32[]{:S(2)}, u32[]{:S(2)}) collective-permute-start(f32[4,4,1]{2,1,0:T(4,128)S(1)} %get-tuple-element.154), channel_id=1, source_target_pairs={{0,32},{32,64},{64,96},{96,128},{128,160},{160,192},{192,224},{1,3... | collective-permute-start | bytes 200 | tf_op jit(solution)/shard_map/ppermute | solution.py:19
  506.7 5.5 collective-permute-start.62
  520.5 5.9 collective-permute-start.67
  522.5 7.0 %collective-permute-start.66 = (f32[8,8,1]{2,1,0:T(8,128)S(1)}, f32[8,8,1]{2,1,0:T(8,128)S(1)}, u32[]{:S(2)}, u32[]{:S(2)}) collective-permute-start(f32[8,8,1]{2,1,0:T(8,128)S(1)} %get-tuple-element.118), channel_id=1, source_target_pairs={{0,32},{32,64},{64,96},{96,128},{128,160},{160,192},{192,224},{1,3... | collective-permute-start | bytes 776 | tf_op jit(solution)/shard_map/ppermute | solution.py:19
  533.5 5.5 collective-permute-start.68
  547.3 5.9 collective-permute-start.73
  549.2 7.0 %collective-permute-start.72 = (f32[8,8,1]{2,1,0:T(8,128)S(1)}, f32[8,8,1]{2,1,0:T(8,128)S(1)}, u32[]{:S(2)}, u32[]{:S(2)}) collective-permute-start(f32[8,8,1]{2,1,0:T(8,128)S(1)} %get-tuple-element.116), channel_id=1, source_target_pairs={{0,32},{32,64},{64,96},{96,128},{128,160},{160,192},{192,224},{1,3... | collective-permute-start | bytes 776 | tf_op jit(solution)/shard_map/ppermute | solution.py:19
  558.3 5.5 collective-permute-start.74
  576.4 6.9 %collective-permute-start.79 = (f32[16,16,1]{2,1,0:T(8,128)S(1)}, f32[16,16,1]{2,1,0:T(8,128)S(1)}, u32[]{:S(2)}, u32[]{:S(2)}) collective-permute-start(f32[16,16,1]{2,1,0:T(8,128)S(1)} %get-tuple-element.71), channel_id=1, source_target_pairs={{32,0},{64,32},{96,64},{128,96},{160,128},{192,160},{224,192},{33,... | collective-permute-start | bytes 3080 | tf_op jit(solution)/shard_map/ppermute | solution.py:20
  578.3 8.1 %collective-permute-start.78 = (f32[16,16,1]{2,1,0:T(8,128)S(1)}, f32[16,16,1]{2,1,0:T(8,128)S(1)}, u32[]{:S(2)}, u32[]{:S(2)}) collective-permute-start(f32[16,16,1]{2,1,0:T(8,128)S(1)} %get-tuple-element.70), channel_id=1, source_target_pairs={{0,32},{32,64},{64,96},{96,128},{128,160},{160,192},{192,224},{1,3... | collective-permute-start | bytes 3080 | tf_op jit(solution)/shard_map/ppermute | solution.py:19
  588.5 5.6 collective-permute-start.80
  603.0 6.9 %collective-permute-start.85 = (f32[16,16,1]{2,1,0:T(8,128)S(1)}, f32[16,16,1]{2,1,0:T(8,128)S(1)}, u32[]{:S(2)}, u32[]{:S(2)}) collective-permute-start(f32[16,16,1]{2,1,0:T(8,128)S(1)} %get-tuple-element.69), channel_id=1, source_target_pairs={{32,0},{64,32},{96,64},{128,96},{160,128},{192,160},{224,192},{33,... | collective-permute-start | bytes 3080 | tf_op jit(solution)/shard_map/ppermute | solution.py:20
  604.9 8.1 %collective-permute-start.84 = (f32[16,16,1]{2,1,0:T(8,128)S(1)}, f32[16,16,1]{2,1,0:T(8,128)S(1)}, u32[]{:S(2)}, u32[]{:S(2)}) collective-permute-start(f32[16,16,1]{2,1,0:T(8,128)S(1)} %get-tuple-element.68), channel_id=1, source_target_pairs={{0,32},{32,64},{64,96},{96,128},{128,160},{160,192},{192,224},{1,3... | collective-permute-start | bytes 3080 | tf_op jit(solution)/shard_map/ppermute | solution.py:19
  615.1 5.6 collective-permute-start.86
  629.7 6.9 %collective-permute-start.91 = (f32[16,16,1]{2,1,0:T(8,128)S(1)}, f32[16,16,1]{2,1,0:T(8,128)S(1)}, u32[]{:S(2)}, u32[]{:S(2)}) collective-permute-start(f32[16,16,1]{2,1,0:T(8,128)S(1)} %get-tuple-element.67), channel_id=1, source_target_pairs={{32,0},{64,32},{96,64},{128,96},{160,128},{192,160},{224,192},{33,... | collective-permute-start | bytes 3080 | tf_op jit(solution)/shard_map/ppermute | solution.py:20
  631.6 8.1 %collective-permute-start.90 = (f32[16,16,1]{2,1,0:T(8,128)S(1)}, f32[16,16,1]{2,1,0:T(8,128)S(1)}, u32[]{:S(2)}, u32[]{:S(2)}) collective-permute-start(f32[16,16,1]{2,1,0:T(8,128)S(1)} %get-tuple-element.66), channel_id=1, source_target_pairs={{0,32},{32,64},{64,96},{96,128},{128,160},{160,192},{192,224},{1,3... | collective-permute-start | bytes 3080 | tf_op jit(solution)/shard_map/ppermute | solution.py:19
  641.8 5.6 collective-permute-start.92
  (53 other events, 1164.2 us)
where the time goes:
time: 665 us; the launch traced here: 657 us
  starting transfers between devices  239 us (36%)
  blocking collectives  132 us (20%)
  waiting for transfers between devices  119 us (18%)
  other arithmetic  110 us (17%)
  local copies, waits for them, and re-layouts  46.3 us (7%)
    ppermute x48, starting transfers between devices, extended_2(): after = lax.ppermute(leading, axis, down)  125 us
    ppermute x48, starting transfers between devices, extended_2(): before = lax.ppermute(last, axis, up)  114 us
    ppermute x48, waiting for transfers between devices, extended_2(): before = lax.ppermute(last, axis, up)  111 us
    all_gather x1, blocking collectives, local(): lax.all_gather(fractions[gather_at][None], ('gx', 'gy', 'gz'), axis=0, ti...  66.3 us
    all_gather x1, blocking collectives, local(): lax.all_gather(source_now[None], ('gx', 'gy', 'gz'), axis=0, tiled=True)  65.6 us
    another operation x7, other arithmetic, bottom_solve(): jnp.linalg.cholesky(bottom_matrix(fraction_low, weight_scale, order_size))  34.7 us
    reshape x6, local copies, waits for them, and re-layouts, coarsen(): values.reshape(extent_z // 2, 2, extent_y // 2, 2, extent_x // 2, 2)  28.2 us
    another operation x4, other arithmetic, bottom_solve(): jax.scipy.linalg.cho_solve((factor, True), source_low.reshape(order_size))  21.9 us
  transfers between devices with their start and end apart: 96, of which 43 were waited for; matrix products, arithmetic and copies ran while one was open for 14% of the time, Pallas kernels for 0%

commit v1 on v0

v1 whole, which is shorter than its diff:
```python
import jax
import jax.numpy as jnp
from jax import lax
from jax.experimental import pallas as pl
from jax.experimental.pallas import tpu as pltpu
from jax.sharding import PartitionSpec as P

RELAXATION = 0.8
F32 = jnp.float32
VMEM_LIMIT = 56 * 1024 * 1024
CENTRE = (0, 0)
AROUND = tuple((oz, oy) for oz in (-1, 0, 1) for oy in (-1, 0, 1) if (oz, oy) != CENTRE)


def turn(v, shift, axis):
    size = v.shape[axis]
    shift = shift % size
    return v if shift == 0 else pltpu.roll(v, shift, axis)


def ahead(v, axis):
    return turn(v, -1, axis)


def behind(v, axis):
    return turn(v, 1, axis)


def index_of(shape, axis):
    return lax.broadcasted_iota(jnp.int32, shape, axis)


def matmul(a, b):
    return lax.dot_general(
        a, b, (((1,), (0,)), ((), ())), precision=lax.Precision.HIGHEST, preferred_element_type=F32
    )


def planes(lo, hi, body, unroll=2):
    trips = (hi - lo) // unroll
    if trips > 1:

        def step(i, carry):
            for k in range(unroll):
                body(lo + i * unroll + k)
            return carry

        lax.fori_loop(0, trips, step, 0)
    else:
        trips = 0
    for p in range(lo + trips * unroll, hi):
        body(p)


class Level:
    def __init__(self, refs):
        self.wx, self.wy, self.wz, self.diag, self.inv = refs

    def build(self, frac, scale, lo, hi, wraps, unroll=2):
        half = 0.5 * scale
        self.wz[lo - 1] = half * (frac[lo - 1] + frac[lo])

        def plane(p):
            c, up, down = frac[p], frac[p + 1], frac[p - 1]
            total = 6.0 * c + up + down
            for axis, keep in ((1, self.wx), (0, self.wy)):
                after, before = ahead(c, axis), behind(c, axis)
                weight = half * (c + after)
                if wraps[axis]:
                    at = index_of(c.shape, axis)
                    last = at == c.shape[axis] - 1
                    weight = jnp.where(last, 0.0, weight)
                    after = jnp.where(last, 0.0, after)
                    before = jnp.where(at == 0, 0.0, before)
                keep[p] = weight
                total = total + after + before
            self.wz[p] = half * (c + up)
            diag = half * total
            self.diag[p] = diag
            self.inv[p] = jnp.where(c > 0.0, RELAXATION / jnp.where(c > 0.0, diag, 1.0), 0.0)

        planes(lo, hi, plane, unroll)

    def apply(self, q, p):
        c, wx, wy = q[p], self.wx[p], self.wy[p]
        near = wx * ahead(c, 1) + behind(wx * c, 1) + wy * ahead(c, 0) + behind(wy * c, 0)
        near = near + self.wz[p] * q[p + 1] + self.wz[p - 1] * q[p - 1]
        return c, self.diag[p] * c - near

    def first(self, rhs, out, lo, hi, unroll=2):
        def plane(p):
            out[p] = self.inv[p] * rhs[p]

        planes(lo, hi, plane, unroll)

    def sweep(self, q, rhs, out, lo, hi, unroll=2):
        def plane(p):
            c, applied = self.apply(q, p)
            out[p] = c + self.inv[p] * (rhs[p] - applied)

        planes(lo, hi, plane, unroll)

    def halved_residual(self, q, rhs, out, lo, hi, unroll=1):
        def pair(j):
            _, one = self.apply(q, lo + 2 * j)
            _, two = self.apply(q, lo + 2 * j + 1)
            out[j] = (rhs[lo + 2 * j] - one) + (rhs[lo + 2 * j + 1] - two)

        planes(0, (hi - lo) // 2, pair, unroll)


def halved(values, out, lo, hi):
    def pair(j):
        out[j] = values[lo + 2 * j] + values[lo + 2 * j + 1]

    planes(0, (hi - lo) // 2, pair)


def rows_of(ref, count):
    _, rows, lanes = ref.shape
    return ref[0:count].reshape(count * rows, lanes)


def gather_pairs(lanes, out_lanes, first, place, count):
    at, to = index_of((lanes, out_lanes), 0), index_of((lanes, out_lanes), 1) - place
    pair = jnp.remainder(at - first, lanes)
    hit = (pair >= 2 * to) & (pair <= 2 * to + 1) & (to >= 0) & (to < count)
    return jnp.where(hit, 0.125, 0.0).astype(F32)


def spread_pairs(lanes, out_lanes, first, start, count):
    at, to = index_of((lanes, out_lanes), 0) - first, index_of((lanes, out_lanes), 1)
    pair = jnp.remainder(to - start, out_lanes)
    hit = (pair >= 2 * at) & (pair <= 2 * at + 1) & (at >= 0) & (at < count)
    return jnp.where(hit, 1.0, 0.0).astype(F32)


def pack_x_kernel(s, f, to_left, to_right):
    lane = index_of((16, 128), 1)
    for z in range(8):
        a, b, c, d = s[z], s[z + 8], f[z], f[z + 8]
        to_left[z] = jnp.where(
            lane < 32,
            a,
            jnp.where(lane < 64, turn(b, 32, 1), jnp.where(lane < 96, turn(c, 64, 1), turn(d, 96, 1))),
        )
        to_right[z] = jnp.where(
            lane >= 96,
            a,
            jnp.where(lane >= 64, turn(b, 96, 1), jnp.where(lane >= 32, turn(c, 64, 1), turn(d, 32, 1))),
        )


def z_range(oz, corner):
    depth = 5 if corner else 7
    return {-1: (16 - depth, 16), 0: (0, 16), 1: (0, depth)}[oz]


def y_range(oy):
    return {-1: (8, 16), 0: (0, 16), 1: (0, 8)}[oy]


def piece_shape(oz, oy):
    (za, zb), (ya, yb) = z_range(oz, oy != 0), y_range(oy)
    return (3, zb - za, yb - ya, 128)


def pack_yz_kernel(s, f, from_right, from_left, halo, *outs):
    ix = lax.axis_index("gx")
    left = jnp.where(ix > 0, 1.0, 0.0).astype(F32)
    right = jnp.where(ix < lax.axis_size("gx") - 1, 1.0, 0.0).astype(F32)
    lane = index_of((16, 128), 1)
    is_right = (lane < 32) | ((lane >= 64) & (lane < 96))
    for z in range(8):
        r, l = from_right[z] * right, from_left[z] * left
        halo[z] = jnp.where(is_right, r, l)
        halo[z + 8] = jnp.where(is_right, turn(r, 96, 1), turn(l, 32, 1))
    for (oz, oy), out in zip(AROUND, outs):
        (za, zb), (ya, yb) = z_range(oz, oy != 0), y_range(oy)
        for k, ref in enumerate((s, f, halo)):
            out[k] = ref[za:zb, ya:yb, :]


def down_kernel(s, f, halo, *refs):
    pieces, refs = refs[:8], refs[8:]
    S, D0, *w0 = refs[:7]
    own1, payload = refs[7:9]
    F, Q, T, U, V, f1, F1, q1, d1, *w1 = refs[9:]
    iz, iy = lax.axis_index("gz"), lax.axis_index("gy")
    nz, ny = lax.axis_size("gz"), lax.axis_size("gy")
    for p in (0, 1, 2, 29, 30, 31):
        S[p] = jnp.zeros((32, 256), F32)
        F[p] = jnp.zeros((32, 256), F32)

    def put(z0, y0, depth, height, inside, plane):
        edge = index_of((height, 128), 1)
        edge = (edge < 32) | (edge >= 96)

        def body(k):
            a, b, h = plane(k)
            if inside is not None:
                a, b, h = a * inside, b * inside, h * inside
            rows = pl.ds(y0, height)
            S[z0 + k, rows, 0:128] = a
            F[z0 + k, rows, 0:128] = b
            S[z0 + k, rows, 128:256] = jnp.where(edge, h, 0.0)
            F[z0 + k, rows, 128:256] = jnp.where(edge, turn(h, 64, 1), 0.0)

        planes(0, depth, body, 4)

    put(8, 8, 16, 16, None, lambda k: (s[k], f[k], halo[k]))
    for (oz, oy), piece in zip(AROUND, pieces):
        _, depth, height, _ = piece.shape
        okay = (iz + oz >= 0) & (iz + oz < nz) & (iy + oy >= 0) & (iy + oy < ny)
        z0 = {-1: 8 - depth, 0: 8, 1: 24}[oz]
        y0 = {-1: 0, 0: 8, 1: 24}[oy]
        inside = jnp.where(okay, 1.0, 0.0).astype(F32)
        put(z0, y0, depth, height, inside, lambda k, piece=piece: (piece[0, k], piece[1, k], piece[2, k]))

    level = Level(w0)
    level.build(F, 1.0, 2, 30, (False, False))
    level.first(S, Q, 2, 30)
    level.sweep(Q, S, D0, 3, 29)
    level.halved_residual(D0, S, T, 4, 28)
    C = gather_pairs(256, 128, 0, 0, 128)

    def coarse(count, out, start):
        U[0:count] = matmul(rows_of(T, count), C).reshape(count, 32, 128)
        for j in range(count):
            out[start + j] = U[j, pl.ds(0, 16, 2), :] + U[j, pl.ds(1, 16, 2), :]

    coarse(12, f1, 1)
    halved(F, T, 2, 30)
    coarse(14, F1, 0)
    for j in range(8):
        own1[0, j] = f1[3 + j, 4:12, :]
        own1[1, j] = F1[3 + j, 4:12, :]

    level = Level(w1)
    level.build(F1, 0.25, 1, 13, (False, False))
    level.first(f1, q1, 1, 13)
    level.sweep(q1, f1, d1, 2, 12)
    level.halved_residual(d1, f1, V, 3, 11)
    first = matmul(rows_of(V, 4), gather_pairs(128, 128, 112, 0, 48))
    halved(F1, V, 3, 11)
    both = first + matmul(rows_of(V, 4), gather_pairs(128, 128, 112, 64, 48))
    V[0:4] = both.reshape(4, 16, 128)
    for j in range(4):
        rows = V[j, pl.ds(4, 4, 2), :] + V[j, pl.ds(5, 4, 2), :]
        for d in range(32):
            payload[d, 4 * j : 4 * j + 4, :] = rows


def middle_kernel(got, own1, y_low, y_high, to_z, payload, f2, F2, d2, *refs):
    q2, T, U, *w2 = refs
    iy, ny = lax.axis_index("gy"), lax.axis_size("gy")
    low = jnp.where(iy > 0, 1.0, 0.0).astype(F32)
    high = jnp.where(iy < ny - 1, 1.0, 0.0).astype(F32)
    for k in range(2):
        for z in range(8):
            to_z[k, z, 0:8, :] = y_low[k, z] * low
            to_z[k, z, 8:16, :] = own1[k, z]
            to_z[k, z, 16:24, :] = y_high[k, z] * high
    keep = index_of((16, 128), 1) < 48
    zero = jnp.zeros((16, 128), F32)
    for ref in (f2, F2, q2, d2):
        ref[0] = zero
        ref[33] = zero
    for gy in range(4):
        for gz in range(8):
            block = got[gy * 8 + gz]
            rhs, frac = jnp.where(keep, block, 0.0), jnp.where(keep, turn(block, 64, 1), 0.0)
            for j in range(4):
                f2[1 + gz * 4 + j, 4 * gy : 4 * gy + 4, :] = rhs[4 * j : 4 * j + 4]
                F2[1 + gz * 4 + j, 4 * gy : 4 * gy + 4, :] = frac[4 * j : 4 * j + 4]
    level = Level(w2)
    level.build(F2, 0.25**2, 1, 33, (True, False), 4)
    level.first(f2, q2, 1, 33, 4)
    level.sweep(q2, f2, d2, 1, 33, 4)
    C = gather_pairs(128, 128, 8, 0, 16)
    for field in range(2):
        if field == 0:
            level.halved_residual(d2, f2, T, 1, 33, 2)
        else:
            halved(F2, T, 1, 33)
        U[...] = matmul(rows_of(T, 16), C).reshape(16, 16, 128)
        for zh in range(2):
            total = None
            for zl in range(8):
                z = zh * 8 + zl
                part = U[z, pl.ds(0, 8, 2), :] + U[z, pl.ds(1, 8, 2), :]
                part = turn(part, 16 * zl, 1)
                total = part if total is None else total + part
            for d in range(8):
                payload[d, 2 * field + zh] = total


def bottom(frac, rhs, half):
    shape = (8, 128)
    row, lane = index_of(shape, 0), index_of(shape, 1)
    used = lane < 32
    odd = jnp.remainder(row, 2) == 1
    y_near = jnp.where(odd, behind(frac, 0), ahead(frac, 0))
    z_up = jnp.where(row >= 6, 0.0, turn(frac, -2, 0))
    z_down = jnp.where(row < 2, 0.0, turn(frac, 2, 0))
    x_up = jnp.where(lane < 31, ahead(frac, 1), 0.0)
    x_down = jnp.where(lane > 0, behind(frac, 1), 0.0)
    diag = half * (6.0 * frac + y_near + z_up + z_down + x_up + x_down)
    after = jnp.where(lane < 31, -half * (frac + x_up), 0.0)
    before = jnp.where((lane > 0) & used, -half * (frac + x_down), 0.0)
    A, C, D, g = [], [], [], []
    for i in range(8):
        here = row == i
        z, y = i // 2, i % 2
        linked = (row == 2 * z + 1 - y) | (row == i - 2) | (row == i + 2)
        mine = jnp.broadcast_to(frac[i : i + 1], shape)
        block = jnp.where(here, diag, jnp.where(linked, -half * (mine + frac), 0.0))
        D.append(jnp.where(used, block, jnp.where(here, 1.0, 0.0)))
        A.append(jnp.where(here, before, 0.0))
        C.append(jnp.where(here, after, 0.0))
        g.append(jnp.broadcast_to(jnp.where(used[:1], rhs[i : i + 1], 0.0), shape))

    def pick(v, k):
        return jnp.broadcast_to(v[k : k + 1], shape)

    def divide(D, others):
        D, others = list(D), [list(o) for o in others]
        for k in range(8):
            inverse = 1.0 / pick(D[k], k)
            D[k] = D[k] * inverse
            for o in others:
                o[k] = o[k] * inverse
            for i in range(8):
                if i != k:
                    factor = pick(D[i], k)
                    D[i] = D[i] - factor * D[k]
                    for o in others:
                        o[i] = o[i] - factor * o[k]
        return others

    step = 1
    while step < 32:
        X, Y, h = divide(D, (A, C, g))
        Xl, Yl, hl = [[turn(v, step, 1) for v in o] for o in (X, Y, h)]
        Xr, Yr, hr = [[turn(v, -step, 1) for v in o] for o in (X, Y, h)]
        nA, nC, nD, ng = [], [], [], []
        for i in range(8):
            d, a, c, r = D[i], None, None, g[i]
            for k in range(8):
                pa, pc = pick(A[i], k), pick(C[i], k)
                d = d - (pa * Yl[k] + pc * Xr[k])
                r = r - (pa * hl[k] + pc * hr[k])
                a = -pa * Xl[k] if a is None else a - pa * Xl[k]
                c = -pc * Yr[k] if c is None else c - pc * Yr[k]
            nA.append(a)
            nC.append(c)
            nD.append(d)
            ng.append(r)
        A, C, D, g = nA, nC, nD, ng
        step *= 2
    (u,) = divide(D, (g,))
    out = jnp.zeros(shape, F32)
    for i in range(8):
        out = jnp.where((row == i) & used, u[i], out)
    return out


def up_kernel(got, to_z, z_low, z_high, f2, F2, d2, S, D0, wx0, wy0, wz0, g0, i0, pressure, residual, *refs):
    f3, F3, q3, d3, f4, F4, q4, d4 = refs[:8]
    w3, w4, w2, w1 = refs[8:13], refs[13:18], refs[18:23], refs[23:28]
    T3, g5, F5, qa2, qb2, T2, f1, F1, qa1, qb1, T1, U1, T0, U0, qa0, qb0 = refs[28:]
    iz, iy, ix = lax.axis_index("gz"), lax.axis_index("gy"), lax.axis_index("gx")
    nz = lax.axis_size("gz")
    lane = index_of((8, 128), 1)
    row = index_of((8, 128), 0)
    zero = jnp.zeros((8, 128), F32)

    for ref in (f3, F3, q3, d3):
        ref[0] = zero
        ref[17] = zero
    for ref in (f4, F4, q4, d4):
        ref[0] = zero
        ref[9] = zero
    for field, ref in enumerate((f3, F3)):
        for zh in range(2):
            blocks = [got[d, 2 * field + zh] for d in range(8)]
            for zl in range(8):
                total = turn(blocks[0], -16 * zl, 1)
                for d in range(1, 8):
                    total = jnp.where(lane >= 16 * d, turn(blocks[d], 16 * (d - zl), 1), total)
                ref[1 + zh * 8 + zl] = total

    three, four = Level(w3), Level(w4)
    three.build(F3, 0.25**3, 1, 17, (True, True), 16)
    three.first(f3, q3, 1, 17, 16)
    three.sweep(q3, f3, d3, 1, 17, 16)
    C = gather_pairs(128, 128, 0, 0, 64)
    for field in range(2):
        if field == 0:
            three.halved_residual(d3, f3, T3, 1, 17, 8)
        else:
            halved(F3, T3, 1, 17)
        T3[0:8] = matmul(rows_of(T3, 8), C).reshape(8, 8, 128)
        out = (f4, F4)[field]
        for j in range(8):
            out[1 + j] = zero
            out[1 + j, 0:4, :] = T3[j, pl.ds(0, 4, 2), :] + T3[j, pl.ds(1, 4, 2), :]
    four.build(F4, 0.25**4, 1, 9, (False, False), 8)
    four.first(f4, q4, 1, 9, 8)
    four.sweep(q4, f4, d4, 1, 9, 8)
    for field in range(2):
        if field == 0:
            four.halved_residual(d4, f4, T3, 1, 9, 4)
        else:
            halved(F4, T3, 1, 9)
        T3[0:4] = matmul(rows_of(T3, 4), C).reshape(4, 8, 128)
        out = (g5, F5)[field]
        for j in range(4):
            out[2 * j : 2 * j + 2, :] = T3[j, pl.ds(0, 2, 2), :] + T3[j, pl.ds(1, 2, 2), :]
    corr5 = bottom(F5[...], g5[...], 0.5 * 0.25**5)

    double = spread_pairs(128, 128, 0, 0, 64)
    wide = matmul(corr5, double)
    for z in range(4):
        plane = jnp.where(row < 2, wide[2 * z : 2 * z + 1], jnp.where(row < 4, wide[2 * z + 1 : 2 * z + 2], 0.0))
        for k in (0, 1):
            p = 1 + 2 * z + k
            q4[p] = d4[p] + jnp.where(F4[p] > 0.0, plane, 0.0)
    four.sweep(q4, f4, d4, 1, 9, 8)
    four.sweep(d4, f4, q4, 1, 9, 8)

    T3[0:8] = matmul(rows_of(q4.at[1:9], 8), double).reshape(8, 8, 128)
    for j in range(8):
        part = T3[j, 0:4, :]
        T3[8, pl.ds(0, 4, 2), :] = part
        T3[8, pl.ds(1, 4, 2), :] = part
        plane = T3[8]
        for k in (0, 1):
            p = 1 + 2 * j + k
            q3[p] = d3[p] + plane
    three.sweep(q3, f3, d3, 1, 17, 16)
    three.sweep(d3, f3, q3, 1, 17, 16)

    two = Level(w2)
    two.build(F2, 0.25**2, 1, 33, (True, False), 4)
    shift = jnp.remainder(4 - 16 * ix, 128)
    for j in range(16):
        T2[0, j] = pltpu.roll(q3[1 + j], shift, 1)
    T2[1] = matmul(T2[0].reshape(128, 128), spread_pairs(128, 128, 0, 0, 24)).reshape(16, 8, 128)
    zero2 = jnp.zeros((16, 128), F32)
    for ref in (qa2, qb2):
        ref[0] = zero2
        ref[33] = zero2
    for j in range(16):
        part = T2[1, j]
        qb2[1, pl.ds(0, 8, 2), :] = part
        qb2[1, pl.ds(1, 8, 2), :] = part
        plane = qb2[1]
        for k in (0, 1):
            p = 1 + 2 * j + k
            qa2[p] = d2[p] + jnp.where(F2[p] > 0.0, plane, 0.0)
    two.sweep(qa2, f2, qb2, 1, 33, 4)
    two.sweep(qb2, f2, qa2, 1, 33, 4)

    low = jnp.where(iz > 0, 1.0, 0.0).astype(F32)
    high = jnp.where(iz < nz - 1, 1.0, 0.0).astype(F32)
    for k, ref in enumerate((f1, F1)):
        for z in range(8):
            ref[z] = z_low[k, z] * low
            ref[8 + z] = to_z[k, z]
            ref[16 + z] = z_high[k, z] * high
    one = Level(w1)
    one.build(F1, 0.25, 3, 21, (False, False))
    one.first(f1, qa1, 3, 21)
    one.sweep(qa1, f1, qb1, 4, 20)
    shift = jnp.remainder(4 - 4 * iy, 16)
    for j in range(8):
        at = jnp.clip(4 * iz - 2 + j, 0, 31)
        U1[j] = pltpu.roll(qa2[1 + at], shift, 0)
    U1[...] = matmul(rows_of(U1, 8), spread_pairs(128, 128, 0, 112, 48)).reshape(8, 16, 128)
    for j in range(8):
        part = U1[j, 0:12, :]
        T1[pl.ds(0, 12, 2), :] = part
        T1[pl.ds(1, 12, 2), :] = part
        plane = T1[...]
        for k in (0, 1):
            p = 4 + 2 * j + k
            qa1[p] = qb1[p] + jnp.where(F1[p] > 0.0, plane, 0.0)
    one.sweep(qa1, f1, qb1, 5, 19)
    one.sweep(qb1, f1, qa1, 6, 18)

    zero_level = Level((wx0, wy0, wz0, g0, i0))
    T0[...] = matmul(qa1[6:18].reshape(288, 128), spread_pairs(128, 256, 0, 0, 128)).reshape(12, 24, 256)

    def refine(j):
        for half in (0, 1):
            part = T0[j, 4:20, 128 * half : 128 * half + 128]
            U0[half, pl.ds(0, 16, 2), :] = part
            U0[half, pl.ds(1, 16, 2), :] = part
        plane = jnp.concatenate([U0[0], U0[1]], axis=1)
        for k in (0, 1):
            p = 4 + 2 * j + k
            qa0[p] = D0[p] + jnp.where(i0[p] > 0.0, plane, 0.0)

    planes(0, 12, refine, 1)
    zero_level.sweep(qa0, S, qb0, 6, 26)
    zero_level.sweep(qb0, S, qa0, 7, 25)

    def finish(p):
        c, applied = zero_level.apply(qa0, p)
        pressure[p - 8] = c[8:24, 0:128]
        residual[p - 8] = (S[p] - applied)[8:24, 0:128]

    planes(8, 24, finish)


def call(kernel, name, out_shapes, scratch=()):
    spec = pl.BlockSpec(memory_space=pltpu.VMEM)

    def run(*args):
        return pl.pallas_call(
            kernel,
            out_shape=[jax.ShapeDtypeStruct(shape, F32) for shape in out_shapes],
            in_specs=[spec] * len(args),
            out_specs=[spec] * len(out_shapes),
            scratch_shapes=[pltpu.VMEM(shape, F32) for shape in scratch],
            compiler_params=pltpu.CompilerParams(vmem_limit_bytes=VMEM_LIMIT),
            name=name,
        )(*args)

    return run


def ring(axis, step):
    size = lax.axis_size(axis)
    return [(i, (i + step) % size) for i in range(size)]


def around(oz, oy):
    nz, ny = lax.axis_size("gz"), lax.axis_size("gy")
    return [
        (y * nz + z, (y - oy) % ny * nz + (z - oz) % nz) for y in range(ny) for z in range(nz)
    ]


BIG, MID, MID2 = (32, 32, 256), (14, 16, 128), (34, 16, 128)
WIDE1 = (24, 24, 128)


def local(source, fraction):
    block = (8, 16, 128)
    to_left, to_right = call(pack_x_kernel, "pack_x", [block, block])(source, fraction)
    from_right = lax.ppermute(to_left, "gx", ring("gx", -1))
    from_left = lax.ppermute(to_right, "gx", ring("gx", 1))
    halo, *sends = call(
        pack_yz_kernel, "pack_yz", [(16, 16, 128)] + [piece_shape(oz, oy) for oz, oy in AROUND]
    )(source, fraction, from_right, from_left)
    pieces = [
        lax.ppermute(piece, ("gy", "gz"), around(oz, oy)) for (oz, oy), piece in zip(AROUND, sends)
    ]
    *fine, own1, payload = call(
        down_kernel,
        "down",
        [BIG] * 7 + [(2, 8, 8, 128), (32, 16, 128)],
        [BIG, BIG, (14, 32, 256), (14, 32, 128), (4, 16, 128)] + [MID] * 9,
    )(source, fraction, halo, *pieces)
    y_low = lax.ppermute(own1, "gy", ring("gy", 1))
    y_high = lax.ppermute(own1, "gy", ring("gy", -1))
    got = lax.all_to_all(payload, ("gy", "gz"), 0, 0)
    to_z, payload, f2, F2, d2 = call(
        middle_kernel,
        "middle",
        [(2, 8, 24, 128), (8, 4, 8, 128), MID2, MID2, MID2],
        [MID2, (16, 16, 128), (16, 16, 128)] + [MID2] * 5,
    )(got, own1, y_low, y_high)
    z_low = lax.ppermute(to_z, "gz", ring("gz", 1))
    z_high = lax.ppermute(to_z, "gz", ring("gz", -1))
    got = lax.all_to_all(payload, "gx", 0, 0)
    three, four = (18, 8, 128), (10, 8, 128)
    pressure, residual = call(
        up_kernel,
        "up",
        [(16, 16, 128)] * 2,
        [three] * 4
        + [four] * 4
        + [three] * 5
        + [four] * 5
        + [MID2] * 5
        + [WIDE1] * 5
        + [(9, 8, 128), (8, 128), (8, 128), MID2, MID2, (2, 16, 8, 128)]
        + [WIDE1] * 4
        + [(24, 128), (8, 16, 128), (12, 24, 256), (2, 32, 128), BIG, BIG],
    )(got, to_z, z_low, z_high, f2, F2, d2, *fine)
    return (pressure, residual)


def solution(mesh):
    spec = P("gz", "gy", "gx")
    return jax.shard_map(
        local, mesh=mesh, in_specs=(spec, spec), out_specs=(spec, spec), check_vma=False
    )
```

time: 665 us -> 110 us (0.17)
  the two profiles are of different devices: /device:TPU:142 before, /device:TPU:1 now
where the time goes in v1:
time: 110 us
  starting transfers between devices  40.4 us (37%)
  Pallas kernels  40 us (36%)
  waiting for transfers between devices  25.5 us (23%)
  local copies, waits for them, and re-layouts  2.89 us (3%)
    pallas_call x5, Pallas kernels, run(): pl.pallas_call(kernel, out_shape=[jax.ShapeDtypeStruct(shape, F32) for sh...  40 us
    ppermute x8, starting transfers between devices, local(): lax.ppermute(piece, ('gy', 'gz'), around(oz, oy))  16.6 us
    all_to_all x1, starting transfers between devices, local(): got = lax.all_to_all(payload, ('gy', 'gz'), 0, 0)  9.25 us
    ppermute x8, waiting for transfers between devices, local(): lax.ppermute(piece, ('gy', 'gz'), around(oz, oy))  7.23 us
    ppermute x1, starting transfers between devices, local(): from_right = lax.ppermute(to_left, 'gx', ring('gx', -1))  6.41 us
    ppermute x1, waiting for transfers between devices, local(): y_high = lax.ppermute(own1, 'gy', ring('gy', -1))  3.73 us
    all_to_all x1, starting transfers between devices, local(): got = lax.all_to_all(payload, 'gx', 0, 0)  3.68 us
    ppermute x1, waiting for transfers between devices, local(): z_high = lax.ppermute(to_z, 'gz', ring('gz', -1))  3.64 us
  transfers between devices with their start and end apart: 16, of which 10 were waited for; matrix products, arithmetic and copies ran while one was open for 0% of the time, Pallas kernels for 0%

profile of v1, /device:TPU:1, one launch (start us, length us, event | category | flops | bytes accessed | tf_op | source)
XLA Modules:
  0.0 109.5 jit_solution(14455406588347917623)
XLA Ops:
  0.6 1.8 %pack_x.1 = (f32[8,16,128]{2,1,0:T(8,128)}, f32[8,16,128]{2,1,0:T(8,128)}) custom-call(f32[16,16,128]{2,1,0:T(8,128)} %s.5, f32[16,16,128]{2,1,0:T(8,128)} %f.5), custom_call_target="tpu_custom_call" | custom-call | tf_op jit(solution)/shard_map/pack_x/pallas_call | solution.py:521
  2.4 6.4 %collective-permute-start = (f32[8,16,128]{2,1,0:T(8,128)}, f32[8,16,128]{2,1,0:T(8,128)S(1)}, u32[]{:S(2)}, u32[]{:S(2)}) collective-permute-start(f32[8,16,128]{2,1,0:T(8,128)} %get-tuple-element.27), channel_id=1, source_target_pairs={{0,224},{32,0},{64,32},{96,64},{128,96},{160,128},{192,160},{224,1... | collective-permute-start | bytes 196616 | tf_op jit(solution)/shard_map/ppermute | solution.py:553
  8.8 0.0 collective-permute-start.1
  8.8 1.6 %collective-permute-done.from_right = f32[8,16,128]{2,1,0:T(8,128)S(1)} collective-permute-done((f32[8,16,128]{2,1,0:T(8,128)}, f32[8,16,128]{2,1,0:T(8,128)S(1)}, u32[]{:S(2)}, u32[]{:S(2)}) %collective-permute-start) | collective-permute-done | bytes 65568 | tf_op jit(solution)/shard_map/ppermute | solution.py:553
  10.5 0.0 copy-start.12
  10.5 2.9 %collective-permute-done.1.from_left = f32[8,16,128]{2,1,0:T(8,128)S(1)} collective-permute-done((f32[8,16,128]{2,1,0:T(8,128)}, f32[8,16,128]{2,1,0:T(8,128)S(1)}, u32[]{:S(2)}, u32[]{:S(2)}) %collective-permute-start.1) | collective-permute-done | bytes 65568 | tf_op jit(solution)/shard_map/ppermute | solution.py:554
  13.3 0.0 copy-done.12
  13.3 0.0 copy-start.13
  13.3 0.6 copy-done.13
  14.0 2.0 %pack_yz.1 = (f32[16,16,128]{2,1,0:T(8,128)}, f32[3,5,8,128]{3,2,1,0:T(8,128)}, f32[3,7,16,128]{3,2,1,0:T(8,128)}, f32[3,5,8,128]{3,2,1,0:T(8,128)}, f32[3,16,8,...) custom-call(f32[16,16,128]{2,1,0:T(8,128)} %s.5, ...), custom_call_target="tpu_custom_call" | custom-call | tf_op jit(solution)/shard_map/pack_yz/pallas_call | solution.py:521
  16.0 4.2 %collective-permute-start.2 = (f32[3,5,8,128]{3,2,1,0:T(8,128)}, f32[3,5,8,128]{3,2,1,0:T(8,128)S(1)}, u32[]{:S(2)}, u32[]{:S(2)}) collective-permute-start(f32[3,5,8,128]{3,2,1,0:T(8,128)} %get-tuple-element.30), channel_id=1, source_target_pairs={{0,9},{1,10},{2,11},{3,12},{4,13},{5,14},{6,15},{7,8},{8,17},{9,18... | collective-permute-start | bytes 184328 | tf_op jit(solution)/shard_map/ppermute | solution.py:559
  20.2 1.2 %collective-permute-start.5 = (f32[3,16,8,128]{3,2,1,0:T(8,128)}, f32[3,16,8,128]{3,2,1,0:T(8,128)S(1)}, u32[]{:S(2)}, u32[]{:S(2)}) collective-permute-start(f32[3,16,8,128]{3,2,1,0:T(8,128)} %get-tuple-element.33), channel_id=1, source_target_pairs={{0,8},{1,9},{2,10},{3,11},{4,12},{5,13},{6,14},{7,15},{8,16},{9,17... | collective-permute-start | bytes 589832 | tf_op jit(solution)/shard_map/ppermute | solution.py:559
  21.4 1.5 %collective-permute-start.6 = (f32[3,16,8,128]{3,2,1,0:T(8,128)}, f32[3,16,8,128]{3,2,1,0:T(8,128)S(1)}, u32[]{:S(2)}, u32[]{:S(2)}) collective-permute-start(f32[3,16,8,128]{3,2,1,0:T(8,128)} %get-tuple-element.34), channel_id=1, source_target_pairs={{0,24},{1,25},{2,26},{3,27},{4,28},{5,29},{6,30},{7,31},{8,0},{9,1... | collective-permute-start | bytes 589832 | tf_op jit(solution)/shard_map/ppermute | solution.py:559
  22.9 0.7 collective-permute-start.4
  23.6 1.1 %collective-permute-start.3 = (f32[3,7,16,128]{3,2,1,0:T(8,128)}, f32[3,7,16,128]{3,2,1,0:T(8,128)S(1)}, u32[]{:S(2)}, u32[]{:S(2)}) collective-permute-start(f32[3,7,16,128]{3,2,1,0:T(8,128)} %get-tuple-element.31), channel_id=1, source_target_pairs={{0,1},{1,2},{2,3},{3,4},{4,5},{5,6},{6,7},{7,0},{8,9},{9,10},{10,1... | collective-permute-start | bytes 516104 | tf_op jit(solution)/shard_map/ppermute | solution.py:559
  24.7 0.0 collective-permute-done.2.refs_0_
  24.7 0.9 collective-permute-start.8
  25.6 2.4 %collective-permute-done.4.refs_2_ = f32[3,5,8,128]{3,2,1,0:T(8,128)S(1)} collective-permute-done((f32[3,5,8,128]{3,2,1,0:T(8,128)}, f32[3,5,8,128]{3,2,1,0:T(8,128)S(1)}, u32[]{:S(2)}, u32[]{:S(2)}) %collective-permute-start.4) | collective-permute-done | bytes 61472 | tf_op jit(solution)/shard_map/ppermute | solution.py:559
  28.0 0.0 copy-start.15
  28.0 3.9 %collective-permute-start.7 = (f32[3,5,8,128]{3,2,1,0:T(8,128)}, f32[3,5,8,128]{3,2,1,0:T(8,128)S(1)}, u32[]{:S(2)}, u32[]{:S(2)}) collective-permute-start(f32[3,5,8,128]{3,2,1,0:T(8,128)} %get-tuple-element.35), channel_id=1, source_target_pairs={{0,15},{1,8},{2,9},{3,10},{4,11},{5,12},{6,13},{7,14},{8,23},{9,16... | collective-permute-start | bytes 184328 | tf_op jit(solution)/shard_map/ppermute | solution.py:559
  31.9 3.1 %collective-permute-done.7.refs_5_ = f32[3,5,8,128]{3,2,1,0:T(8,128)S(1)} collective-permute-done((f32[3,5,8,128]{3,2,1,0:T(8,128)}, f32[3,5,8,128]{3,2,1,0:T(8,128)S(1)}, u32[]{:S(2)}, u32[]{:S(2)}) %collective-permute-start.7) | collective-permute-done | bytes 61472 | tf_op jit(solution)/shard_map/ppermute | solution.py:559
  35.0 0.0 copy-start.16
  35.0 3.1 %collective-permute-start.9 = (f32[3,5,8,128]{3,2,1,0:T(8,128)}, f32[3,5,8,128]{3,2,1,0:T(8,128)S(1)}, u32[]{:S(2)}, u32[]{:S(2)}) collective-permute-start(f32[3,5,8,128]{3,2,1,0:T(8,128)} %get-tuple-element.37), channel_id=1, source_target_pairs={{0,31},{1,24},{2,25},{3,26},{4,27},{5,28},{6,29},{7,30},{8,7},{9,0... | collective-permute-start | bytes 184328 | tf_op jit(solution)/shard_map/ppermute | solution.py:559
  38.1 1.7 %collective-permute-done.9.refs_7_ = f32[3,5,8,128]{3,2,1,0:T(8,128)S(1)} collective-permute-done((f32[3,5,8,128]{3,2,1,0:T(8,128)}, f32[3,5,8,128]{3,2,1,0:T(8,128)S(1)}, u32[]{:S(2)}, u32[]{:S(2)}) %collective-permute-start.9) | collective-permute-done | bytes 61472 | tf_op jit(solution)/shard_map/ppermute | solution.py:559
  39.8 0.0 copy-start.17
  39.8 0.0 collective-permute-done.3.refs_1_
  39.8 0.0 copy-start.7
  39.8 0.0 collective-permute-done.8.refs_6_
  39.8 0.0 copy-start.8
  39.8 0.0 collective-permute-done.5.refs_3_
  39.8 0.0 copy-start.2
  39.8 0.0 collective-permute-done.6.refs_4_
  39.9 0.0 copy-start.3
  39.9 0.0 copy-done.14
  39.9 0.0 copy-done.15
  39.9 0.0 copy-done.16
  39.9 0.5 copy-done.17
  40.4 0.1 copy-done.7
  40.5 0.1 copy-done.8
  40.6 0.1 copy-done.2
  40.6 0.1 copy-done.3
  40.7 13.4 %down.1 = (f32[32,32,256]{2,1,0:T(8,128)}, f32[32,32,256]{2,1,0:T(8,128)}, f32[32,32,256]{2,1,0:T(8,128)}, f32[32,32,256]{2,1,0:T(8,128)}, f32[32,32,256]{2,1,0:...) custom-call(f32[16,16,128]{2,1,0:T(8,128)} %s.5, ...), custom_call_target="tpu_custom_call" | custom-call | tf_op jit(solution)/shard_map/down/pallas_call | solution.py:521
  54.2 9.2 %all-to-all-start = ((f32[32,16,128]{2,1,0:T(8,128)}), f32[32,16,128]{2,1,0:T(8,128)S(1)}, u32[]{:S(2)}, u32[]{:S(2)}) async-start(f32[32,16,128]{2,1,0:T(8,128)} %get-tuple-element.38), calls=%async_computation | async-start | bytes 524288 | tf_op jit(solution)/shard_map/all_to_all | solution.py:569
  63.4 0.0 copy-done.9
  63.4 2.7 %collective-permute-start.11 = (f32[2,8,8,128]{3,2,1,0:T(8,128)S(1)}, f32[2,8,8,128]{3,2,1,0:T(8,128)S(1)}, u32[]{:S(2)}, u32[]{:S(2)}) collective-permute-start(f32[2,8,8,128]{3,2,1,0:T(8,128)S(1)} %copy-done.9), channel_id=1, source_target_pairs={{0,24},{8,0},{16,8},{24,16},{1,25},{9,1},{17,9},{25,17},{2,26},{10... | collective-permute-start | bytes 196616 | tf_op jit(solution)/shard_map/ppermute | solution.py:568
  66.2 0.0 collective-permute-start.10
  66.2 3.7 %collective-permute-done.11.y_high = f32[2,8,8,128]{3,2,1,0:T(8,128)S(1)} collective-permute-done((f32[2,8,8,128]{3,2,1,0:T(8,128)S(1)}, f32[2,8,8,128]{3,2,1,0:T(8,128)S(1)}, u32[]{:S(2)}, u32[]{:S(2)}) %collective-permute-start.11) | collective-permute-done | bytes 65568 | tf_op jit(solution)/shard_map/ppermute | solution.py:568
  69.9 1.1 %collective-permute-done.10.y_low = f32[2,8,8,128]{3,2,1,0:T(8,128)S(1)} collective-permute-done((f32[2,8,8,128]{3,2,1,0:T(8,128)S(1)}, f32[2,8,8,128]{3,2,1,0:T(8,128)S(1)}, u32[]{:S(2)}, u32[]{:S(2)}) %collective-permute-start.10) | collective-permute-done | bytes 65568 | tf_op jit(solution)/shard_map/ppermute | solution.py:567
  71.1 1.7 %all-to-all-done.got = f32[32,16,128]{2,1,0:T(8,128)S(1)} async-done(((f32[32,16,128]{2,1,0:T(8,128)}), f32[32,16,128]{2,1,0:T(8,128)S(1)}, u32[]{:S(2)}, u32[]{:S(2)}) %all-to-all-start) | async-done | bytes 262176 | tf_op jit(solution)/shard_map/all_to_all | solution.py:569
  72.7 0.0 copy-done.10
  72.7 0.0 copy-done.11
  72.7 0.7 copy-done
  73.5 5.3 %middle.1 = (f32[2,8,24,128]{3,2,1,0:T(8,128)}, f32[8,4,8,128]{3,2,1,0:T(8,128)}, f32[34,16,128]{2,1,0:T(8,128)}, f32[34,16,128]{2,1,0:T(8,128)}, f32[34,16,128]{2,1,0:T(8,128)}) custom-call(f32[32,16,128]{2,1,0:T(8,128)} %copy-done, f32[2,8,8,128]{3,2,1,0:T(8,128)} %get-tuple-element.39.own1, f32[2,8,8,128]{3,2,1,0:T(8,128)} %copy-done.11, ...), custom_call_target="tpu_custom_call" | custom-call | tf_op jit(solution)/shard_map/middle/pallas_call | solution.py:521
  78.7 3.7 %all-to-all-start.1 = ((f32[8,4,8,128]{3,2,1,0:T(8,128)}), f32[8,4,8,128]{3,2,1,0:T(8,128)S(1)}, u32[]{:S(2)}, u32[]{:S(2)}) async-start(f32[8,4,8,128]{3,2,1,0:T(8,128)} %get-tuple-element.40), calls=%async_computation.1 | async-start | bytes 262144 | tf_op jit(solution)/shard_map/all_to_all | solution.py:578
  82.4 0.0 copy-done.4
  82.4 0.2 collective-permute-start.13
  82.6 1.6 %collective-permute-start.12 = (f32[2,8,24,128]{3,2,1,0:T(8,128)S(1)}, f32[2,8,24,128]{3,2,1,0:T(8,128)S(1)}, u32[]{:S(2)}, u32[]{:S(2)}) collective-permute-start(f32[2,8,24,128]{3,2,1,0:T(8,128)S(1)} %copy-done.4), channel_id=1, source_target_pairs={{0,1},{1,2},{2,3},{3,4},{4,5},{5,6},{6,7},{7,0},{8,9},{9,10},{10,1... | collective-permute-start | bytes 589832 | tf_op jit(solution)/shard_map/ppermute | solution.py:576
  84.2 3.6 %collective-permute-done.13.z_high = f32[2,8,24,128]{3,2,1,0:T(8,128)S(1)} collective-permute-done((f32[2,8,24,128]{3,2,1,0:T(8,128)S(1)}, f32[2,8,24,128]{3,2,1,0:T(8,128)S(1)}, u32[]{:S(2)}, u32[]{:S(2)}) %collective-permute-start.13) | collective-permute-done | bytes 196640 | tf_op jit(solution)/shard_map/ppermute | solution.py:577
  87.8 0.0 collective-permute-done.12.z_low
  87.8 3.5 %all-to-all-done.1.got = f32[8,4,8,128]{3,2,1,0:T(8,128)S(1)} async-done(((f32[8,4,8,128]{3,2,1,0:T(8,128)}), f32[8,4,8,128]{3,2,1,0:T(8,128)S(1)}, u32[]{:S(2)}, u32[]{:S(2)}) %all-to-all-start.1) | async-done | bytes 131104 | tf_op jit(solution)/shard_map/all_to_all | solution.py:578
  91.4 0.0 copy-done.5
  91.4 0.0 copy-done.6
  91.4 0.6 copy-done.1
  92.0 17.5 %up.1 = (f32[16,16,128]{2,1,0:T(8,128)}, f32[16,16,128]{2,1,0:T(8,128)}) custom-call(f32[8,4,8,128]{3,2,1,0:T(8,128)} %copy-done.1, f32[2,8,24,128]{3,2,1,0:T(8,128)} %get-tuple-element.41.to_z, f32[2,8,24,128]{3,2,1,0:T(8,128)} %copy-done.6, f32[2,8,24,128]{3,2,1,0:T(8,128)} %copy-done.5, f32[34,16,128]{2,1,0:T(8,128)} %get-tuple-element.42.f2, ...), custom_call_target="tpu_custom_call" | custom-call | tf_op jit(solution)/shard_map/up/pallas_call | solution.py:521
  (9 shorter events, 0.0 us)
Async XLA Ops:
  2.4 8.1 %collective-permute-start = (f32[8,16,128]{2,1,0:T(8,128)}, f32[8,16,128]{2,1,0:T(8,128)S(1)}, u32[]{:S(2)}, u32[]{:S(2)}) collective-permute-start(f32[8,16,128]{2,1,0:T(8,128)} %get-tuple-element.27), channel_id=1, source_target_pairs={{0,224},{32,0},{64,32},{96,64},{128,96},{160,128},{192,160},{224,1... | collective-permute-start | bytes 196616 | tf_op jit(solution)/shard_map/ppermute | solution.py:553
  8.8 4.5 %collective-permute-start.1 = (f32[8,16,128]{2,1,0:T(8,128)}, f32[8,16,128]{2,1,0:T(8,128)S(1)}, u32[]{:S(2)}, u32[]{:S(2)}) collective-permute-start(f32[8,16,128]{2,1,0:T(8,128)} %get-tuple-element.28), channel_id=1, source_target_pairs={{0,32},{32,64},{64,96},{96,128},{128,160},{160,192},{192,224},{224... | collective-permute-start | bytes 196616 | tf_op jit(solution)/shard_map/ppermute | solution.py:554
  10.5 2.9 %copy-start.12 = (f32[8,16,128]{2,1,0:T(8,128)}, f32[8,16,128]{2,1,0:T(8,128)S(1)}, u32[]{:S(2)}) copy-start(f32[8,16,128]{2,1,0:T(8,128)S(1)} %collective-permute-done.from_right) | copy-start | bytes 196612
  13.3 0.6 copy-start.13
  16.0 8.7 %collective-permute-start.2 = (f32[3,5,8,128]{3,2,1,0:T(8,128)}, f32[3,5,8,128]{3,2,1,0:T(8,128)S(1)}, u32[]{:S(2)}, u32[]{:S(2)}) collective-permute-start(f32[3,5,8,128]{3,2,1,0:T(8,128)} %get-tuple-element.30), channel_id=1, source_target_pairs={{0,9},{1,10},{2,11},{3,12},{4,13},{5,14},{6,15},{7,8},{8,17},{9,18... | collective-permute-start | bytes 184328 | tf_op jit(solution)/shard_map/ppermute | solution.py:559
  20.2 19.6 %collective-permute-start.5 = (f32[3,16,8,128]{3,2,1,0:T(8,128)}, f32[3,16,8,128]{3,2,1,0:T(8,128)S(1)}, u32[]{:S(2)}, u32[]{:S(2)}) collective-permute-start(f32[3,16,8,128]{3,2,1,0:T(8,128)} %get-tuple-element.33), channel_id=1, source_target_pairs={{0,8},{1,9},{2,10},{3,11},{4,12},{5,13},{6,14},{7,15},{8,16},{9,17... | collective-permute-start | bytes 589832 | tf_op jit(solution)/shard_map/ppermute | solution.py:559
  21.4 18.4 %collective-permute-start.6 = (f32[3,16,8,128]{3,2,1,0:T(8,128)}, f32[3,16,8,128]{3,2,1,0:T(8,128)S(1)}, u32[]{:S(2)}, u32[]{:S(2)}) collective-permute-start(f32[3,16,8,128]{3,2,1,0:T(8,128)} %get-tuple-element.34), channel_id=1, source_target_pairs={{0,24},{1,25},{2,26},{3,27},{4,28},{5,29},{6,30},{7,31},{8,0},{9,1... | collective-permute-start | bytes 589832 | tf_op jit(solution)/shard_map/ppermute | solution.py:559
  22.9 5.1 %collective-permute-start.4 = (f32[3,5,8,128]{3,2,1,0:T(8,128)}, f32[3,5,8,128]{3,2,1,0:T(8,128)S(1)}, u32[]{:S(2)}, u32[]{:S(2)}) collective-permute-start(f32[3,5,8,128]{3,2,1,0:T(8,128)} %get-tuple-element.32), channel_id=1, source_target_pairs={{0,25},{1,26},{2,27},{3,28},{4,29},{5,30},{6,31},{7,24},{8,1},{9,2... | collective-permute-start | bytes 184328 | tf_op jit(solution)/shard_map/ppermute | solution.py:559
  23.6 16.2 %collective-permute-start.3 = (f32[3,7,16,128]{3,2,1,0:T(8,128)}, f32[3,7,16,128]{3,2,1,0:T(8,128)S(1)}, u32[]{:S(2)}, u32[]{:S(2)}) collective-permute-start(f32[3,7,16,128]{3,2,1,0:T(8,128)} %get-tuple-element.31), channel_id=1, source_target_pairs={{0,1},{1,2},{2,3},{3,4},{4,5},{5,6},{6,7},{7,0},{8,9},{9,10},{10,1... | collective-permute-start | bytes 516104 | tf_op jit(solution)/shard_map/ppermute | solution.py:559
  24.7 15.1 %copy-start.14 = (f32[3,5,8,128]{3,2,1,0:T(8,128)}, f32[3,5,8,128]{3,2,1,0:T(8,128)S(1)}, u32[]{:S(2)}) copy-start(f32[3,5,8,128]{3,2,1,0:T(8,128)S(1)} %collective-permute-done.2.refs_0_) | copy-start | bytes 184324
  24.7 15.1 %collective-permute-start.8 = (f32[3,7,16,128]{3,2,1,0:T(8,128)}, f32[3,7,16,128]{3,2,1,0:T(8,128)S(1)}, u32[]{:S(2)}, u32[]{:S(2)}) collective-permute-start(f32[3,7,16,128]{3,2,1,0:T(8,128)} %get-tuple-element.36), channel_id=1, source_target_pairs={{0,7},{1,0},{2,1},{3,2},{4,3},{5,4},{6,5},{7,6},{8,15},{9,8},{10,9... | collective-permute-start | bytes 516104 | tf_op jit(solution)/shard_map/ppermute | solution.py:559
  28.0 11.9 %copy-start.15 = (f32[3,5,8,128]{3,2,1,0:T(8,128)}, f32[3,5,8,128]{3,2,1,0:T(8,128)S(1)}, u32[]{:S(2)}) copy-start(f32[3,5,8,128]{3,2,1,0:T(8,128)S(1)} %collective-permute-done.4.refs_2_) | copy-start | bytes 184324
  28.0 7.1 %collective-permute-start.7 = (f32[3,5,8,128]{3,2,1,0:T(8,128)}, f32[3,5,8,128]{3,2,1,0:T(8,128)S(1)}, u32[]{:S(2)}, u32[]{:S(2)}) collective-permute-start(f32[3,5,8,128]{3,2,1,0:T(8,128)} %get-tuple-element.35), channel_id=1, source_target_pairs={{0,15},{1,8},{2,9},{3,10},{4,11},{5,12},{6,13},{7,14},{8,23},{9,16... | collective-permute-start | bytes 184328 | tf_op jit(solution)/shard_map/ppermute | solution.py:559
  35.0 4.8 %copy-start.16 = (f32[3,5,8,128]{3,2,1,0:T(8,128)}, f32[3,5,8,128]{3,2,1,0:T(8,128)S(1)}, u32[]{:S(2)}) copy-start(f32[3,5,8,128]{3,2,1,0:T(8,128)S(1)} %collective-permute-done.7.refs_5_) | copy-start | bytes 184324
  35.0 4.8 %collective-permute-start.9 = (f32[3,5,8,128]{3,2,1,0:T(8,128)}, f32[3,5,8,128]{3,2,1,0:T(8,128)S(1)}, u32[]{:S(2)}, u32[]{:S(2)}) collective-permute-start(f32[3,5,8,128]{3,2,1,0:T(8,128)} %get-tuple-element.37), channel_id=1, source_target_pairs={{0,31},{1,24},{2,25},{3,26},{4,27},{5,28},{6,29},{7,30},{8,7},{9,0... | collective-permute-start | bytes 184328 | tf_op jit(solution)/shard_map/ppermute | solution.py:559
  39.8 0.6 copy-start.17
  39.8 0.7 copy-start.7
  39.8 0.8 copy-start.8
  39.8 0.8 copy-start.2
  39.9 0.9 copy-start.3
  54.2 9.3 %copy-start.9 = (f32[2,8,8,128]{3,2,1,0:T(8,128)S(1)}, f32[2,8,8,128]{3,2,1,0:T(8,128)}, u32[]{:S(2)}) copy-start(f32[2,8,8,128]{3,2,1,0:T(8,128)} %get-tuple-element.39.own1) | copy-start | bytes 196612
  54.2 18.5 %all-to-all-start = ((f32[32,16,128]{2,1,0:T(8,128)}), f32[32,16,128]{2,1,0:T(8,128)S(1)}, u32[]{:S(2)}, u32[]{:S(2)}) async-start(f32[32,16,128]{2,1,0:T(8,128)} %get-tuple-element.38), calls=%async_computation | async-start | bytes 524288 | tf_op jit(solution)/shard_map/all_to_all | solution.py:569
  63.4 6.5 %collective-permute-start.11 = (f32[2,8,8,128]{3,2,1,0:T(8,128)S(1)}, f32[2,8,8,128]{3,2,1,0:T(8,128)S(1)}, u32[]{:S(2)}, u32[]{:S(2)}) collective-permute-start(f32[2,8,8,128]{3,2,1,0:T(8,128)S(1)} %copy-done.9), channel_id=1, source_target_pairs={{0,24},{8,0},{16,8},{24,16},{1,25},{9,1},{17,9},{25,17},{2,26},{10... | collective-permute-start | bytes 196616 | tf_op jit(solution)/shard_map/ppermute | solution.py:568
  66.2 4.9 %collective-permute-start.10 = (f32[2,8,8,128]{3,2,1,0:T(8,128)S(1)}, f32[2,8,8,128]{3,2,1,0:T(8,128)S(1)}, u32[]{:S(2)}, u32[]{:S(2)}) collective-permute-start(f32[2,8,8,128]{3,2,1,0:T(8,128)S(1)} %copy-done.9), channel_id=1, source_target_pairs={{0,8},{8,16},{16,24},{24,0},{1,9},{9,17},{17,25},{25,1},{2,10},{10... | collective-permute-start | bytes 196616 | tf_op jit(solution)/shard_map/ppermute | solution.py:567
  69.9 2.8 %copy-start.10 = (f32[2,8,8,128]{3,2,1,0:T(8,128)}, f32[2,8,8,128]{3,2,1,0:T(8,128)S(1)}, u32[]{:S(2)}) copy-start(f32[2,8,8,128]{3,2,1,0:T(8,128)S(1)} %collective-permute-done.11.y_high) | copy-start | bytes 196612
  71.0 1.7 %copy-start.11 = (f32[2,8,8,128]{3,2,1,0:T(8,128)}, f32[2,8,8,128]{3,2,1,0:T(8,128)S(1)}, u32[]{:S(2)}) copy-start(f32[2,8,8,128]{3,2,1,0:T(8,128)S(1)} %collective-permute-done.10.y_low) | copy-start | bytes 196612
  72.7 0.7 copy-start
  78.7 3.7 %copy-start.4 = (f32[2,8,24,128]{3,2,1,0:T(8,128)S(1)}, f32[2,8,24,128]{3,2,1,0:T(8,128)}, u32[]{:S(2)}) copy-start(f32[2,8,24,128]{3,2,1,0:T(8,128)} %get-tuple-element.41.to_z) | copy-start | bytes 589828
  78.7 12.6 %all-to-all-start.1 = ((f32[8,4,8,128]{3,2,1,0:T(8,128)}), f32[8,4,8,128]{3,2,1,0:T(8,128)S(1)}, u32[]{:S(2)}, u32[]{:S(2)}) async-start(f32[8,4,8,128]{3,2,1,0:T(8,128)} %get-tuple-element.40), calls=%async_computation.1 | async-start | bytes 262144 | tf_op jit(solution)/shard_map/all_to_all | solution.py:578
  82.4 5.4 %collective-permute-start.13 = (f32[2,8,24,128]{3,2,1,0:T(8,128)S(1)}, f32[2,8,24,128]{3,2,1,0:T(8,128)S(1)}, u32[]{:S(2)}, u32[]{:S(2)}) collective-permute-start(f32[2,8,24,128]{3,2,1,0:T(8,128)S(1)} %copy-done.4), channel_id=1, source_target_pairs={{0,7},{1,0},{2,1},{3,2},{4,3},{5,4},{6,5},{7,6},{8,15},{9,8},{10,9... | collective-permute-start | bytes 589832 | tf_op jit(solution)/shard_map/ppermute | solution.py:577
  82.6 5.2 %collective-permute-start.12 = (f32[2,8,24,128]{3,2,1,0:T(8,128)S(1)}, f32[2,8,24,128]{3,2,1,0:T(8,128)S(1)}, u32[]{:S(2)}, u32[]{:S(2)}) collective-permute-start(f32[2,8,24,128]{3,2,1,0:T(8,128)S(1)} %copy-done.4), channel_id=1, source_target_pairs={{0,1},{1,2},{2,3},{3,4},{4,5},{5,6},{6,7},{7,0},{8,9},{9,10},{10,1... | collective-permute-start | bytes 589832 | tf_op jit(solution)/shard_map/ppermute | solution.py:576
  87.8 3.5 %copy-start.5 = (f32[2,8,24,128]{3,2,1,0:T(8,128)}, f32[2,8,24,128]{3,2,1,0:T(8,128)S(1)}, u32[]{:S(2)}) copy-start(f32[2,8,24,128]{3,2,1,0:T(8,128)S(1)} %collective-permute-done.13.z_high) | copy-start | bytes 589828
  87.8 3.5 %copy-start.6 = (f32[2,8,24,128]{3,2,1,0:T(8,128)}, f32[2,8,24,128]{3,2,1,0:T(8,128)S(1)}, u32[]{:S(2)}) copy-start(f32[2,8,24,128]{3,2,1,0:T(8,128)S(1)} %collective-permute-done.12.z_low) | copy-start | bytes 589828
  91.4 0.7 copy-start.1

commit v2 on v1

--- a/solution.py
+++ b/solution.py
@@ -7,9 +7,7 @@
 
 RELAXATION = 0.8
 F32 = jnp.float32
-VMEM_LIMIT = 56 * 1024 * 1024
-CENTRE = (0, 0)
-AROUND = tuple((oz, oy) for oz in (-1, 0, 1) for oy in (-1, 0, 1) if (oz, oy) != CENTRE)
+VMEM_LIMIT = 32 * 1024 * 1024
 
 
 def turn(v, shift, axis):
@@ -135,7 +133,20 @@
     return jnp.where(hit, 1.0, 0.0).astype(F32)
 
 
-def pack_x_kernel(s, f, to_left, to_right):
+def inside(okay):
+    return jnp.where(okay, 1.0, 0.0).astype(F32)
+
+
+def copies(pairs, sems):
+    started = [pltpu.make_async_copy(a, b, sems.at[i]) for i, (a, b) in enumerate(pairs)]
+    for copy in started:
+        copy.start()
+    return started
+
+
+def pack_x_kernel(source, fraction, s, f, to_left, to_right, sems):
+    for copy in copies(((source, s), (fraction, f)), sems):
+        copy.wait()
     lane = index_of((16, 128), 1)
     for z in range(8):
         a, b, c, d = s[z], s[z + 8], f[z], f[z + 8]
@@ -151,55 +162,52 @@
         )
 
 
-def z_range(oz, corner):
-    depth = 5 if corner else 7
-    return {-1: (16 - depth, 16), 0: (0, 16), 1: (0, depth)}[oz]
-
-
-def y_range(oy):
-    return {-1: (8, 16), 0: (0, 16), 1: (0, 8)}[oy]
-
-
-def piece_shape(oz, oy):
-    (za, zb), (ya, yb) = z_range(oz, oy != 0), y_range(oy)
-    return (3, zb - za, yb - ya, 128)
-
-
-def pack_yz_kernel(s, f, from_right, from_left, halo, *outs):
+def pack_y_kernel(s, f, from_right, from_left, halo, to_low, to_high):
     ix = lax.axis_index("gx")
-    left = jnp.where(ix > 0, 1.0, 0.0).astype(F32)
-    right = jnp.where(ix < lax.axis_size("gx") - 1, 1.0, 0.0).astype(F32)
+    left = inside(ix > 0)
+    right = inside(ix < lax.axis_size("gx") - 1)
     lane = index_of((16, 128), 1)
     is_right = (lane < 32) | ((lane >= 64) & (lane < 96))
     for z in range(8):
         r, l = from_right[z] * right, from_left[z] * left
         halo[z] = jnp.where(is_right, r, l)
         halo[z + 8] = jnp.where(is_right, turn(r, 96, 1), turn(l, 32, 1))
-    for (oz, oy), out in zip(AROUND, outs):
-        (za, zb), (ya, yb) = z_range(oz, oy != 0), y_range(oy)
+    for k, ref in enumerate((s, f, halo)):
+        to_low[k] = ref[:, 0:8, :]
+        to_high[k] = ref[:, 8:16, :]
+
+
+def pack_z_kernel(s, f, halo, y_low, y_high, to_low, to_high):
+    iy, ny = lax.axis_index("gy"), lax.axis_size("gy")
+    low, high = inside(iy > 0), inside(iy < ny - 1)
+    for out, start in ((to_low, 0), (to_high, 9)):
         for k, ref in enumerate((s, f, halo)):
-            out[k] = ref[za:zb, ya:yb, :]
-
-
-def down_kernel(s, f, halo, *refs):
-    pieces, refs = refs[:8], refs[8:]
-    S, D0, *w0 = refs[:7]
-    own1, payload = refs[7:9]
-    F, Q, T, U, V, f1, F1, q1, d1, *w1 = refs[9:]
+            for j in range(7):
+                z = start + j
+                out[k, j, 0:8, :] = y_low[k, z] * low
+                out[k, j, 8:24, :] = ref[z]
+                out[k, j, 24:32, :] = y_high[k, z] * high
+
+
+def down_kernel(s, f, halo, y_low, y_high, z_low, z_high, *refs):
+    kept, own1, message, payload = refs[:7], refs[7], refs[8], refs[9]
+    F, Q, T, U, V, f1, F1, q1, d1, *w1 = refs[10:24]
+    S, D0, *w0 = refs[24:31]
+    sems = refs[31]
     iz, iy = lax.axis_index("gz"), lax.axis_index("gy")
     nz, ny = lax.axis_size("gz"), lax.axis_size("gy")
-    for p in (0, 1, 2, 29, 30, 31):
+    for p in (0, 31):
         S[p] = jnp.zeros((32, 256), F32)
         F[p] = jnp.zeros((32, 256), F32)
 
-    def put(z0, y0, depth, height, inside, plane):
+    def put(z0, y0, depth, height, scale, plane):
         edge = index_of((height, 128), 1)
         edge = (edge < 32) | (edge >= 96)
 
         def body(k):
             a, b, h = plane(k)
-            if inside is not None:
-                a, b, h = a * inside, b * inside, h * inside
+            if scale is not None:
+                a, b, h = a * scale, b * scale, h * scale
             rows = pl.ds(y0, height)
             S[z0 + k, rows, 0:128] = a
             F[z0 + k, rows, 0:128] = b
@@ -209,18 +217,18 @@
         planes(0, depth, body, 4)
 
     put(8, 8, 16, 16, None, lambda k: (s[k], f[k], halo[k]))
-    for (oz, oy), piece in zip(AROUND, pieces):
-        _, depth, height, _ = piece.shape
-        okay = (iz + oz >= 0) & (iz + oz < nz) & (iy + oy >= 0) & (iy + oy < ny)
-        z0 = {-1: 8 - depth, 0: 8, 1: 24}[oz]
-        y0 = {-1: 0, 0: 8, 1: 24}[oy]
-        inside = jnp.where(okay, 1.0, 0.0).astype(F32)
-        put(z0, y0, depth, height, inside, lambda k, piece=piece: (piece[0, k], piece[1, k], piece[2, k]))
-
+    for ref, y0, okay in ((y_low, 0, iy > 0), (y_high, 24, iy < ny - 1)):
+        put(8, y0, 16, 8, inside(okay), lambda k, ref=ref: (ref[0, k], ref[1, k], ref[2, k]))
+    for ref, z0, okay in ((z_low, 1, iz > 0), (z_high, 24, iz < nz - 1)):
+        put(z0, 0, 7, 32, inside(okay), lambda k, ref=ref: (ref[0, k], ref[1, k], ref[2, k]))
+
+    started = copies(((S, kept[0]),), sems)
     level = Level(w0)
     level.build(F, 1.0, 2, 30, (False, False))
+    started += copies(tuple(zip(w0, kept[2:])), sems.at[1:6])
     level.first(S, Q, 2, 30)
     level.sweep(Q, S, D0, 3, 29)
+    started += copies(((D0, kept[1]),), sems.at[6:7])
     level.halved_residual(D0, S, T, 4, 28)
     C = gather_pairs(256, 128, 0, 0, 128)
 
@@ -233,8 +241,9 @@
     halved(F, T, 2, 30)
     coarse(14, F1, 0)
     for j in range(8):
-        own1[0, j] = f1[3 + j, 4:12, :]
-        own1[1, j] = F1[3 + j, 4:12, :]
+        message[j] = f1[3 + j, 4:12, :]
+        message[8 + j] = F1[3 + j, 4:12, :]
+    started += copies(((message.at[0:16], own1),), sems.at[7:8])
 
     level = Level(w1)
     level.build(F1, 0.25, 1, 13, (False, False))
@@ -247,36 +256,59 @@
     V[0:4] = both.reshape(4, 16, 128)
     for j in range(4):
         rows = V[j, pl.ds(4, 4, 2), :] + V[j, pl.ds(5, 4, 2), :]
-        for d in range(32):
-            payload[d, 4 * j : 4 * j + 4, :] = rows
-
-
-def middle_kernel(got, own1, y_low, y_high, to_z, payload, f2, F2, d2, *refs):
-    q2, T, U, *w2 = refs
+        message[16 + j // 2, 4 * (j % 2) : 4 * (j % 2) + 4, :] = rows
+    payload[...] = message[16:18]
+    for copy in started:
+        copy.wait()
+
+
+def spread_y_kernel(message, y_low, y_high, far, to_low, to_high):
     iy, ny = lax.axis_index("gy"), lax.axis_size("gy")
-    low = jnp.where(iy > 0, 1.0, 0.0).astype(F32)
-    high = jnp.where(iy < ny - 1, 1.0, 0.0).astype(F32)
-    for k in range(2):
-        for z in range(8):
-            to_z[k, z, 0:8, :] = y_low[k, z] * low
-            to_z[k, z, 8:16, :] = own1[k, z]
-            to_z[k, z, 16:24, :] = y_high[k, z] * high
-    keep = index_of((16, 128), 1) < 48
+    low, high = inside(iy > 0), inside(iy < ny - 1)
+    for out, start in ((to_low, 0), (to_high, 2)):
+        for k in range(2):
+            for j in range(6):
+                at, z = (6 * k + j) * 3, 8 * k + start + j
+                out[at] = y_low[z] * low
+                out[at + 1] = message[z]
+                out[at + 2] = y_high[z] * high
+        for step, ref, first in ((0, message, 16), (-1, y_low, 16), (1, y_high, 16), (2, far, 0)):
+            at = 36 + 2 * jnp.remainder(iy + step + ny, ny)
+            for k in range(2):
+                out[at + k] = ref[first + k]
+
+
+def spread_z_kernel(own, z_low, z_high, out):
+    for k, ref in enumerate((z_low, own, z_high)):
+        out[8 * k : 8 * k + 8] = ref[36:44]
+
+
+def middle_kernel(own, before, after, payload, f2h, F2h, d2h, *refs):
+    f2, F2, d2, q2, T, U, *w2, sems = refs
+    iz, nz = lax.axis_index("gz"), lax.axis_size("gz")
+    lane = index_of((8, 128), 1)
+    keep = lane < 48
     zero = jnp.zeros((16, 128), F32)
     for ref in (f2, F2, q2, d2):
         ref[0] = zero
         ref[33] = zero
-    for gy in range(4):
-        for gz in range(8):
-            block = got[gy * 8 + gz]
-            rhs, frac = jnp.where(keep, block, 0.0), jnp.where(keep, turn(block, 64, 1), 0.0)
-            for j in range(4):
-                f2[1 + gz * 4 + j, 4 * gy : 4 * gy + 4, :] = rhs[4 * j : 4 * j + 4]
-                F2[1 + gz * 4 + j, 4 * gy : 4 * gy + 4, :] = frac[4 * j : 4 * j + 4]
+    for ref, start in ((before, -4), (own, -1), (after, 2)):
+        for k in range(3):
+            base = 1 + 4 * jnp.remainder(iz + start + k + nz, nz)
+            for gy in range(4):
+                for j in range(2):
+                    block = ref[8 * k + 2 * gy + j]
+                    rhs, frac = jnp.where(keep, block, 0.0), jnp.where(keep, turn(block, 64, 1), 0.0)
+                    for half in range(2):
+                        rows = slice(4 * half, 4 * half + 4)
+                        f2[base + 2 * j + half, 4 * gy : 4 * gy + 4, :] = rhs[rows]
+                        F2[base + 2 * j + half, 4 * gy : 4 * gy + 4, :] = frac[rows]
+    started = copies(((f2, f2h), (F2, F2h)), sems)
     level = Level(w2)
     level.build(F2, 0.25**2, 1, 33, (True, False), 4)
     level.first(f2, q2, 1, 33, 4)
     level.sweep(q2, f2, d2, 1, 33, 4)
+    started += copies(((d2, d2h),), sems.at[2:3])
     C = gather_pairs(128, 128, 8, 0, 16)
     for field in range(2):
         if field == 0:
@@ -293,6 +325,8 @@
                 total = part if total is None else total + part
             for d in range(8):
                 payload[d, 2 * field + zh] = total
+    for copy in started:
+        copy.wait()
 
 
 def bottom(frac, rhs, half):
@@ -365,7 +399,13 @@
     return out
 
 
-def up_kernel(got, to_z, z_low, z_high, f2, F2, d2, S, D0, wx0, wy0, wz0, g0, i0, pressure, residual, *refs):
+def up_kernel(got, *refs):
+    far, refs = refs[:15], refs[15:]
+    pressure, residual, refs = refs[0], refs[1], refs[2:]
+    near, sems = refs[:15], refs[15]
+    started = copies(tuple(zip(far, near)), sems)
+    own1, y_low, y_high, z_low, z_high, f2, F2, d2, S, D0, wx0, wy0, wz0, g0, i0 = near
+    refs = refs[16:]
     f3, F3, q3, d3, f4, F4, q4, d4 = refs[:8]
     w3, w4, w2, w1 = refs[8:13], refs[13:18], refs[18:23], refs[23:28]
     T3, g5, F5, qa2, qb2, T2, f1, F1, qa1, qb1, T1, U1, T0, U0, qa0, qb0 = refs[28:]
@@ -441,6 +481,8 @@
     three.sweep(q3, f3, d3, 1, 17, 16)
     three.sweep(d3, f3, q3, 1, 17, 16)
 
+    for copy in started[5:8]:
+        copy.wait()
     two = Level(w2)
     two.build(F2, 0.25**2, 1, 33, (True, False), 4)
     shift = jnp.remainder(4 - 16 * ix, 128)
@@ -462,13 +504,20 @@
     two.sweep(qa2, f2, qb2, 1, 33, 4)
     two.sweep(qb2, f2, qa2, 1, 33, 4)
 
-    low = jnp.where(iz > 0, 1.0, 0.0).astype(F32)
-    high = jnp.where(iz < nz - 1, 1.0, 0.0).astype(F32)
+    for copy in started[:5]:
+        copy.wait()
+    iy, ny = lax.axis_index("gy"), lax.axis_size("gy")
+    low, high, under, over = inside(iy > 0), inside(iy < ny - 1), inside(iz > 0), inside(iz < nz - 1)
     for k, ref in enumerate((f1, F1)):
         for z in range(8):
-            ref[z] = z_low[k, z] * low
-            ref[8 + z] = to_z[k, z]
-            ref[16 + z] = z_high[k, z] * high
+            ref[8 + z, 0:8, :] = y_low[8 * k + z] * low
+            ref[8 + z, 8:16, :] = own1[8 * k + z]
+            ref[8 + z, 16:24, :] = y_high[8 * k + z] * high
+        for j in range(6):
+            for t in range(3):
+                at = (6 * k + j) * 3 + t
+                ref[2 + j, 8 * t : 8 * t + 8, :] = z_low[at] * under
+                ref[16 + j, 8 * t : 8 * t + 8, :] = z_high[at] * over
     one = Level(w1)
     one.build(F1, 0.25, 3, 21, (False, False))
     one.first(f1, qa1, 3, 21)
@@ -489,6 +538,8 @@
     one.sweep(qa1, f1, qb1, 5, 19)
     one.sweep(qb1, f1, qa1, 6, 18)
 
+    for copy in started[8:]:
+        copy.wait()
     zero_level = Level((wx0, wy0, wz0, g0, i0))
     T0[...] = matmul(qa1[6:18].reshape(288, 128), spread_pairs(128, 256, 0, 0, 128)).reshape(12, 24, 256)
 
@@ -514,16 +565,20 @@
     planes(8, 24, finish)
 
 
-def call(kernel, name, out_shapes, scratch=()):
-    spec = pl.BlockSpec(memory_space=pltpu.VMEM)
+def call(kernel, name, ins, outs, scratch=()):
+    anywhere = pl.BlockSpec(memory_space=pl.ANY)
+    spec = {"v": pl.BlockSpec(memory_space=pltpu.VMEM), "n": pl.BlockSpec(memory_space=pltpu.VMEM), "h": anywhere}
+    kind = {"v": pltpu.VMEM, "h": pltpu.HBM, "n": jax.ShapeDtypeStruct}
+    space = {"v": pltpu.VMEM, "h": pltpu.HBM}
 
     def run(*args):
+        args = [pltpu.with_memory_space_constraint(a, space[k]) if k in space else a for a, k in zip(args, ins)]
         return pl.pallas_call(
             kernel,
-            out_shape=[jax.ShapeDtypeStruct(shape, F32) for shape in out_shapes],
-            in_specs=[spec] * len(args),
-            out_specs=[spec] * len(out_shapes),
-            scratch_shapes=[pltpu.VMEM(shape, F32) for shape in scratch],
+            out_shape=[kind[k](shape, F32) for k, shape in outs],
+            in_specs=[spec[k] for k in ins],
+            out_specs=[spec[k] for k, _ in outs],
+            scratch_shapes=[pltpu.VMEM(shape, F32) if isinstance(shape, tuple) else shape for shape in scratch],
             compiler_params=pltpu.CompilerParams(vmem_limit_bytes=VMEM_LIMIT),
             name=name,
         )(*args)
@@ -536,61 +591,76 @@
     return [(i, (i + step) % size) for i in range(size)]
 
 
-def around(oz, oy):
-    nz, ny = lax.axis_size("gz"), lax.axis_size("gy")
-    return [
-        (y * nz + z, (y - oy) % ny * nz + (z - oz) % nz) for y in range(ny) for z in range(nz)
-    ]
-
-
-BIG, MID, MID2 = (32, 32, 256), (14, 16, 128), (34, 16, 128)
-WIDE1 = (24, 24, 128)
+def exchange(to_low, to_high, axis, reach=1):
+    return lax.ppermute(to_high, axis, ring(axis, reach)), lax.ppermute(to_low, axis, ring(axis, -reach))
+
+
+BIG, MID, MID2, WIDE1 = (32, 32, 256), (14, 16, 128), (34, 16, 128), (24, 24, 128)
+THREE, FOUR = (18, 8, 128), (10, 8, 128)
 
 
 def local(source, fraction):
-    block = (8, 16, 128)
-    to_left, to_right = call(pack_x_kernel, "pack_x", [block, block])(source, fraction)
-    from_right = lax.ppermute(to_left, "gx", ring("gx", -1))
-    from_left = lax.ppermute(to_right, "gx", ring("gx", 1))
-    halo, *sends = call(
-        pack_yz_kernel, "pack_yz", [(16, 16, 128)] + [piece_shape(oz, oy) for oz, oy in AROUND]
-    )(source, fraction, from_right, from_left)
-    pieces = [
-        lax.ppermute(piece, ("gy", "gz"), around(oz, oy)) for (oz, oy), piece in zip(AROUND, sends)
-    ]
-    *fine, own1, payload = call(
+    def dma(count):
+        return pltpu.SemaphoreType.DMA((count,))
+
+    own, strip = (16, 16, 128), (8, 16, 128)
+    s, f, to_left, to_right = call(
+        pack_x_kernel, "pack_x", "hh", [("v", own)] * 2 + [("v", strip)] * 2, [dma(2)]
+    )(source, fraction)
+    from_left, from_right = exchange(to_left, to_right, "gx")
+    rows = (3, 16, 8, 128)
+    halo, to_low, to_high = call(pack_y_kernel, "pack_y", "vvvv", [("v", own), ("v", rows), ("v", rows)])(
+        s, f, from_right, from_left
+    )
+    y_low, y_high = exchange(to_low, to_high, "gy")
+    layers = (3, 7, 32, 128)
+    to_low, to_high = call(pack_z_kernel, "pack_z", "vvvvv", [("v", layers)] * 2)(s, f, halo, y_low, y_high)
+    z_low, z_high = exchange(to_low, to_high, "gz")
+    *fine, own1, message, payload = call(
         down_kernel,
         "down",
-        [BIG] * 7 + [(2, 8, 8, 128), (32, 16, 128)],
-        [BIG, BIG, (14, 32, 256), (14, 32, 128), (4, 16, 128)] + [MID] * 9,
-    )(source, fraction, halo, *pieces)
-    y_low = lax.ppermute(own1, "gy", ring("gy", 1))
-    y_high = lax.ppermute(own1, "gy", ring("gy", -1))
-    got = lax.all_to_all(payload, ("gy", "gz"), 0, 0)
-    to_z, payload, f2, F2, d2 = call(
+        "vvvvvvv",
+        [("h", BIG)] * 7 + [("h", (16, 8, 128)), ("v", (18, 8, 128)), ("v", (2, 8, 128))],
+        [BIG, BIG, (14, 32, 256), (14, 32, 128), (4, 16, 128)] + [MID] * 9 + [BIG] * 7 + [dma(8)],
+    )(s, f, halo, y_low, y_high, z_low, z_high)
+
+    y_low, y_high = exchange(message, message, "gy")
+    opposite = lax.ppermute(payload, "gy", ring("gy", 2))
+    layers = (44, 8, 128)
+    to_low, to_high = call(spread_y_kernel, "spread_y", "vvvv", [("v", layers)] * 2)(message, y_low, y_high, opposite)
+    z_low, z_high = exchange(to_low, to_high, "gz")
+    (near,) = call(spread_z_kernel, "spread_z", "vvv", [("v", (24, 8, 128))])(to_low, z_low, z_high)
+    before, after = exchange(near, near, "gz", 3)
+    payload, f2, F2, d2 = call(
         middle_kernel,
         "middle",
-        [(2, 8, 24, 128), (8, 4, 8, 128), MID2, MID2, MID2],
-        [MID2, (16, 16, 128), (16, 16, 128)] + [MID2] * 5,
-    )(got, own1, y_low, y_high)
-    z_low = lax.ppermute(to_z, "gz", ring("gz", 1))
-    z_high = lax.ppermute(to_z, "gz", ring("gz", -1))
+        "vvv",
+        [("v", (8, 4, 8, 128))] + [("h", MID2)] * 3,
+        [MID2] * 4 + [(16, 16, 128), (16, 16, 128)] + [MID2] * 5 + [dma(3)],
+    )(near, before, after)
     got = lax.all_to_all(payload, "gx", 0, 0)
-    three, four = (18, 8, 128), (10, 8, 128)
+    kept = [own1, y_low, y_high, z_low, z_high, f2, F2, d2, *fine]
     pressure, residual = call(
         up_kernel,
         "up",
-        [(16, 16, 128)] * 2,
-        [three] * 4
-        + [four] * 4
-        + [three] * 5
-        + [four] * 5
+        "v" + "h" * 15,
+        [("n", own)] * 2,
+        [(16, 8, 128)]
+        + [(18, 8, 128)] * 2
+        + [(44, 8, 128)] * 2
+        + [MID2] * 3
+        + [BIG] * 7
+        + [dma(15)]
+        + [THREE] * 4
+        + [FOUR] * 4
+        + [THREE] * 5
+        + [FOUR] * 5
         + [MID2] * 5
         + [WIDE1] * 5
         + [(9, 8, 128), (8, 128), (8, 128), MID2, MID2, (2, 16, 8, 128)]
         + [WIDE1] * 4
         + [(24, 128), (8, 16, 128), (12, 24, 256), (2, 32, 128), BIG, BIG],
-    )(got, to_z, z_low, z_high, f2, F2, d2, *fine)
+    )(got, *kept)
     return (pressure, residual)
 
 

time: 110 us -> 91.2 us (0.83)
  starting transfers between devices: 40.4 us -> 22.8 us
  Pallas kernels: 40 us -> 27.9 us
  blocking collectives: 0 us -> 10.3 us
  local copies, waits for them, and re-layouts: 2.89 us -> 1.24 us
  waiting for transfers between devices: 25.5 us -> 26.6 us
    all_to_all x2 -> x0, starting transfers between devices: 12.9 us -> none  [the longest x1 9.25 us: local(): got = lax.all_to_all(payload, ('gy', 'gz'), 0, 0)]
    pallas_call x5 -> x8, Pallas kernels: 40 us -> 27.9 us  [run(): pl.pallas_call(kernel, out_shape=[kind[k](shape, F32) for k, shape in out...]
    all_to_all x0 -> x1, blocking collectives: none -> 10.3 us  [local(): got = lax.all_to_all(payload, 'gx', 0, 0)]
    ppermute x14 -> x13, waiting for transfers between devices: 20.3 us -> 26.6 us  [the longest x6 14.9 us: exchange(): lax.ppermute(to_high, axis, ring(axis, reach))]
    all_to_all x2 -> x0, waiting for transfers between devices: 5.19 us -> none  [the longest x1 3.51 us: local(): got = lax.all_to_all(payload, 'gx', 0, 0)]
    ppermute x14 -> x13, starting transfers between devices: 27.4 us -> 22.8 us  [the longest x6 12 us: exchange(): lax.ppermute(to_low, axis, ring(axis, -reach))]
    unnamed x36 -> x8, local copies, waits for them, and re-layouts: 2.89 us -> 1.24 us
  transfers between devices with their start and end apart: 16 -> 13, of which waited for: 10 -> 11; matrix products, arithmetic and copies ran while one was open for 0% -> 0% of each run, Pallas kernels for 0% -> 0%
where the time goes in v2:
time: 91.2 us; the launch traced here: 89.8 us
  Pallas kernels  27.9 us (31%)
  waiting for transfers between devices  26.6 us (29%)
  starting transfers between devices  22.8 us (25%)
  blocking collectives  10.3 us (11%)
  local copies, waits for them, and re-layouts  1.24 us (1%)
    pallas_call x8, Pallas kernels, run(): pl.pallas_call(kernel, out_shape=[kind[k](shape, F32) for k, shape in out...  27.9 us
    ppermute x6, waiting for transfers between devices, exchange(): lax.ppermute(to_high, axis, ring(axis, reach))  14.9 us
    ppermute x6, starting transfers between devices, exchange(): lax.ppermute(to_low, axis, ring(axis, -reach))  12 us
    all_to_all x1, blocking collectives, local(): got = lax.all_to_all(payload, 'gx', 0, 0)  10.3 us
    ppermute x6, starting transfers between devices, exchange(): lax.ppermute(to_high, axis, ring(axis, reach))  9.56 us
    ppermute x6, waiting for transfers between devices, exchange(): lax.ppermute(to_low, axis, ring(axis, -reach))  8.89 us
    ppermute x1, waiting for transfers between devices, local(): opposite = lax.ppermute(payload, 'gy', ring('gy', 2))  2.84 us
  transfers between devices with their start and end apart: 13, of which 11 were waited for; matrix products, arithmetic and copies ran while one was open for 0% of the time, Pallas kernels for 0%

profile of v2, /device:TPU:1, one launch (start us, length us, event | category | flops | bytes accessed | tf_op | source)
XLA Modules:
  0.0 89.8 jit_solution(5882707890542039277)
XLA Ops:
  0.6 1.1 %pack_x.1 = (f32[16,16,128]{2,1,0:T(8,128)S(1)}, f32[16,16,128]{2,1,0:T(8,128)S(1)}, f32[8,16,128]{2,1,0:T(8,128)S(1)}, f32[8,16,128]{2,1,0:T(8,128)S(1)}) custom-call(f32[16,16,128]{2,1,0:T(8,128)} %source.1, f32[16,16,128]{2,1,0:T(8,128)} %fraction.1), custom_call_target="tpu_custom_call" | custom-call | tf_op jit(solution)/shard_map/pack_x/pallas_call | solution.py:576
  1.8 6.5 %collective-permute-start = (f32[8,16,128]{2,1,0:T(8,128)S(1)}, f32[8,16,128]{2,1,0:T(8,128)S(1)}, u32[]{:S(2)}, u32[]{:S(2)}) collective-permute-start(f32[8,16,128]{2,1,0:T(8,128)S(1)} %get-tuple-element.29), channel_id=1, source_target_pairs={{0,224},{32,0},{64,32},{96,64},{128,96},{160,128},{192,160},{224,1... | collective-permute-start | bytes 196616 | tf_op jit(solution)/shard_map/ppermute | solution.py:595
  8.3 0.0 collective-permute-start.1
  8.3 1.3 %collective-permute-done.from_right = f32[8,16,128]{2,1,0:T(8,128)S(1)} collective-permute-done((f32[8,16,128]{2,1,0:T(8,128)S(1)}, f32[8,16,128]{2,1,0:T(8,128)S(1)}, u32[]{:S(2)}, u32[]{:S(2)}) %collective-permute-start) | collective-permute-done | bytes 65568 | tf_op jit(solution)/shard_map/ppermute | solution.py:595
  9.6 3.0 %collective-permute-done.1.from_left = f32[8,16,128]{2,1,0:T(8,128)S(1)} collective-permute-done((f32[8,16,128]{2,1,0:T(8,128)S(1)}, f32[8,16,128]{2,1,0:T(8,128)S(1)}, u32[]{:S(2)}, u32[]{:S(2)}) %collective-permute-start.1) | collective-permute-done | bytes 65568 | tf_op jit(solution)/shard_map/ppermute | solution.py:595
  12.6 0.1 pack_y.1
  12.7 1.3 %collective-permute-start.2 = (f32[3,16,8,128]{3,2,1,0:T(8,128)S(1)}, f32[3,16,8,128]{3,2,1,0:T(8,128)S(1)}, u32[]{:S(2)}, u32[]{:S(2)}) collective-permute-start(f32[3,16,8,128]{3,2,1,0:T(8,128)S(1)} %get-tuple-element.32), channel_id=1, source_target_pairs={{0,8},{8,16},{16,24},{24,0},{1,9},{9,17},{17,25},{25,1},{2,10},{10... | collective-permute-start | bytes 589832 | tf_op jit(solution)/shard_map/ppermute | solution.py:595
  14.0 1.5 %collective-permute-start.3 = (f32[3,16,8,128]{3,2,1,0:T(8,128)S(1)}, f32[3,16,8,128]{3,2,1,0:T(8,128)S(1)}, u32[]{:S(2)}, u32[]{:S(2)}) collective-permute-start(f32[3,16,8,128]{3,2,1,0:T(8,128)S(1)} %get-tuple-element.33), channel_id=1, source_target_pairs={{0,24},{8,0},{16,8},{24,16},{1,25},{9,1},{17,9},{25,17},{2,26},{10... | collective-permute-start | bytes 589832 | tf_op jit(solution)/shard_map/ppermute | solution.py:595
  15.5 3.1 %collective-permute-done.2.y_low = f32[3,16,8,128]{3,2,1,0:T(8,128)S(1)} collective-permute-done((f32[3,16,8,128]{3,2,1,0:T(8,128)S(1)}, f32[3,16,8,128]{3,2,1,0:T(8,128)S(1)}, u32[]{:S(2)}, u32[]{:S(2)}) %collective-permute-start.2) | collective-permute-done | bytes 196640 | tf_op jit(solution)/shard_map/ppermute | solution.py:595
  18.5 0.0 collective-permute-done.3.y_high
  18.6 4.7 %collective-permute-start.4 = (f32[3,7,32,128]{3,2,1,0:T(8,128)S(1)}, f32[3,7,32,128]{3,2,1,0:T(8,128)S(1)}, u32[]{:S(2)}, u32[]{:S(2)}) collective-permute-start(f32[3,7,32,128]{3,2,1,0:T(8,128)S(1)} %get-tuple-element.34), channel_id=1, source_target_pairs={{0,1},{1,2},{2,3},{3,4},{4,5},{5,6},{6,7},{7,0},{8,9},{9,10},{10,1... | collective-permute-start | bytes 1032200 | tf_op jit(solution)/shard_map/ppermute | solution.py:595
  23.3 0.0 collective-permute-start.5
  23.3 4.2 %collective-permute-done.4.z_low = f32[3,7,32,128]{3,2,1,0:T(8,128)S(1)} collective-permute-done((f32[3,7,32,128]{3,2,1,0:T(8,128)S(1)}, f32[3,7,32,128]{3,2,1,0:T(8,128)S(1)}, u32[]{:S(2)}, u32[]{:S(2)}) %collective-permute-start.4) | collective-permute-done | bytes 344096 | tf_op jit(solution)/shard_map/ppermute | solution.py:595
  27.5 2.5 %collective-permute-done.5.z_high = f32[3,7,32,128]{3,2,1,0:T(8,128)S(1)} collective-permute-done((f32[3,7,32,128]{3,2,1,0:T(8,128)S(1)}, f32[3,7,32,128]{3,2,1,0:T(8,128)S(1)}, u32[]{:S(2)}, u32[]{:S(2)}) %collective-permute-start.5) | collective-permute-done | bytes 344096 | tf_op jit(solution)/shard_map/ppermute | solution.py:595
  30.0 9.3 %down.1 = (f32[32,32,256]{2,1,0:T(8,128)}, f32[32,32,256]{2,1,0:T(8,128)}, f32[32,32,256]{2,1,0:T(8,128)}, f32[32,32,256]{2,1,0:T(8,128)}, f32[32,32,256]{2,1,0:...) custom-call(f32[16,16,128]{2,1,0:T(8,128)S(1)} %get-tuple-element.27, ...), custom_call_target="tpu_custom_call" | custom-call | tf_op jit(solution)/shard_map/down/pallas_call | solution.py:576
  39.3 2.8 %collective-permute-start.7 = (f32[18,8,128]{2,1,0:T(8,128)S(1)}, f32[18,8,128]{2,1,0:T(8,128)S(1)}, u32[]{:S(2)}, u32[]{:S(2)}) collective-permute-start(f32[18,8,128]{2,1,0:T(8,128)S(1)} %get-tuple-element.36.message), channel_id=1, source_target_pairs={{0,24},{8,0},{16,8},{24,16},{1,25},{9,1},{17,9},{25,17},{2,26},{10... | collective-permute-start | bytes 221192 | tf_op jit(solution)/shard_map/ppermute | solution.py:595
  42.0 0.0 collective-permute-start.6
  42.0 1.3 %collective-permute-start.8 = (f32[2,8,128]{2,1,0:T(8,128)S(1)}, f32[2,8,128]{2,1,0:T(8,128)S(1)}, u32[]{:S(2)}, u32[]{:S(2)}) collective-permute-start(f32[2,8,128]{2,1,0:T(8,128)S(1)} %get-tuple-element.37), channel_id=1, source_target_pairs={{0,16},{8,24},{16,0},{24,8},{1,17},{9,25},{17,1},{25,9},{2,18},{10... | collective-permute-start | bytes 24584 | tf_op jit(solution)/shard_map/ppermute | solution.py:628
  43.3 2.8 %collective-permute-done.8.far = f32[2,8,128]{2,1,0:T(8,128)S(1)} collective-permute-done((f32[2,8,128]{2,1,0:T(8,128)S(1)}, f32[2,8,128]{2,1,0:T(8,128)S(1)}, u32[]{:S(2)}, u32[]{:S(2)}) %collective-permute-start.8) | collective-permute-done | bytes 8224 | tf_op jit(solution)/shard_map/ppermute | solution.py:628
  46.1 0.0 collective-permute-done.7.y_high.refs_2_
  46.1 0.0 copy-start.2
  46.1 0.8 collective-permute-done.6.y_low.refs_1_
  46.9 0.0 copy-start.3
  47.0 0.0 copy-done.2
  47.0 0.6 copy-done.3
  47.6 1.6 %collective-permute-start.9 = (f32[44,8,128]{2,1,0:T(8,128)S(1)}, f32[44,8,128]{2,1,0:T(8,128)S(1)}, u32[]{:S(2)}, u32[]{:S(2)}) collective-permute-start(f32[44,8,128]{2,1,0:T(8,128)S(1)} %get-tuple-element.39), channel_id=1, source_target_pairs={{0,1},{1,2},{2,3},{3,4},{4,5},{5,6},{6,7},{7,0},{8,9},{9,10},{10,1... | collective-permute-start | bytes 540680 | tf_op jit(solution)/shard_map/ppermute | solution.py:595
  49.1 0.0 collective-permute-start.10
  49.1 2.4 %collective-permute-done.9.z_low.refs_3_ = f32[44,8,128]{2,1,0:T(8,128)S(1)} collective-permute-done((f32[44,8,128]{2,1,0:T(8,128)S(1)}, f32[44,8,128]{2,1,0:T(8,128)S(1)}, u32[]{:S(2)}, u32[]{:S(2)}) %collective-permute-start.9) | collective-permute-done | bytes 180256 | tf_op jit(solution)/shard_map/ppermute | solution.py:595
  51.6 0.0 copy-start
  51.6 2.8 %collective-permute-done.10.z_high.refs_4_ = f32[44,8,128]{2,1,0:T(8,128)S(1)} collective-permute-done((f32[44,8,128]{2,1,0:T(8,128)S(1)}, f32[44,8,128]{2,1,0:T(8,128)S(1)}, u32[]{:S(2)}, u32[]{:S(2)}) %collective-permute-start.10) | collective-permute-done | bytes 180256 | tf_op jit(solution)/shard_map/ppermute | solution.py:595
  54.4 0.0 copy-start.1
  54.4 0.0 copy-done
  54.4 0.6 copy-done.1
  55.0 1.3 %collective-permute-start.12 = (f32[24,8,128]{2,1,0:T(8,128)S(1)}, f32[24,8,128]{2,1,0:T(8,128)S(1)}, u32[]{:S(2)}, u32[]{:S(2)}) collective-permute-start(f32[24,8,128]{2,1,0:T(8,128)S(1)} %spread_z.1.own), channel_id=1, source_target_pairs={{0,5},{1,6},{2,7},{3,0},{4,1},{5,2},{6,3},{7,4},{8,13},{9,14},{10,... | collective-permute-start | bytes 294920 | tf_op jit(solution)/shard_map/ppermute | solution.py:595
  56.3 2.0 %collective-permute-start.11 = (f32[24,8,128]{2,1,0:T(8,128)S(1)}, f32[24,8,128]{2,1,0:T(8,128)S(1)}, u32[]{:S(2)}, u32[]{:S(2)}) collective-permute-start(f32[24,8,128]{2,1,0:T(8,128)S(1)} %spread_z.1.own), channel_id=1, source_target_pairs={{0,3},{1,4},{2,5},{3,6},{4,7},{5,0},{6,1},{7,2},{8,11},{9,12},{10,... | collective-permute-start | bytes 294920 | tf_op jit(solution)/shard_map/ppermute | solution.py:595
  58.3 2.3 %collective-permute-done.12.after = f32[24,8,128]{2,1,0:T(8,128)S(1)} collective-permute-done((f32[24,8,128]{2,1,0:T(8,128)S(1)}, f32[24,8,128]{2,1,0:T(8,128)S(1)}, u32[]{:S(2)}, u32[]{:S(2)}) %collective-permute-start.12) | collective-permute-done | bytes 98336 | tf_op jit(solution)/shard_map/ppermute | solution.py:595
  60.6 1.4 %collective-permute-done.11.before = f32[24,8,128]{2,1,0:T(8,128)S(1)} collective-permute-done((f32[24,8,128]{2,1,0:T(8,128)S(1)}, f32[24,8,128]{2,1,0:T(8,128)S(1)}, u32[]{:S(2)}, u32[]{:S(2)}) %collective-permute-start.11) | collective-permute-done | bytes 98336 | tf_op jit(solution)/shard_map/ppermute | solution.py:595
  62.0 3.4 %middle.1 = (f32[8,4,8,128]{3,2,1,0:T(8,128)S(1)}, f32[34,16,128]{2,1,0:T(8,128)}, f32[34,16,128]{2,1,0:T(8,128)}, f32[34,16,128]{2,1,0:T(8,128)}) custom-call(f32[24,8,128]{2,1,0:T(8,128)S(1)} %spread_z.1.own, f32[24,8,128]{2,1,0:T(8,128)S(1)} %collective-permute-done.11.before, f32[24,8,128]{2,1,0:T(8,128)S(1)} %collective-permute-done.12.after), custom_call_target="tpu_custom_call" | custom-call | tf_op jit(solution)/shard_map/middle/pallas_call | solution.py:576
  65.4 10.3 %all_to_all.5.got = f32[8,4,8,128]{3,2,1,0:T(8,128)S(1)} all-to-all(f32[8,4,8,128]{3,2,1,0:T(8,128)S(1)} %get-tuple-element.40), channel_id=1, replica_groups=mesh['gx'=8,'gy'=4,'gz'=8] {'gx'}, dimensions={0} | all-to-all | bytes 262144 | tf_op jit(solution)/shard_map/all_to_all | solution.py:641
  75.7 13.9 %up.1 = (f32[16,16,128]{2,1,0:T(8,128)}, f32[16,16,128]{2,1,0:T(8,128)}) custom-call(f32[8,4,8,128]{3,2,1,0:T(8,128)S(1)} %all_to_all.5.got, f32[16,8,128]{2,1,0:T(8,128)} %get-tuple-element.41.refs_0_, f32[18,8,128]{2,1,0:T(8,128)} %copy-done.3, f32[18,8,128]{2,1,0:T(8,128)} %copy-done.2, f32[44,8,128]{2,1,0:T(8,128)} %copy-done, f32[44,8,128]{2,1,0:T(8,128)} %copy-done.1, ...), custom_call_target="tpu_custom_call" | custom-call | tf_op jit(solution)/shard_map/up/pallas_call | solution.py:576
  (3 shorter events, 0.1 us)
Async XLA Ops:
  1.8 7.8 %collective-permute-start = (f32[8,16,128]{2,1,0:T(8,128)S(1)}, f32[8,16,128]{2,1,0:T(8,128)S(1)}, u32[]{:S(2)}, u32[]{:S(2)}) collective-permute-start(f32[8,16,128]{2,1,0:T(8,128)S(1)} %get-tuple-element.29), channel_id=1, source_target_pairs={{0,224},{32,0},{64,32},{96,64},{128,96},{160,128},{192,160},{224,1... | collective-permute-start | bytes 196616 | tf_op jit(solution)/shard_map/ppermute | solution.py:595
  8.3 4.3 %collective-permute-start.1 = (f32[8,16,128]{2,1,0:T(8,128)S(1)}, f32[8,16,128]{2,1,0:T(8,128)S(1)}, u32[]{:S(2)}, u32[]{:S(2)}) collective-permute-start(f32[8,16,128]{2,1,0:T(8,128)S(1)} %get-tuple-element.30), channel_id=1, source_target_pairs={{0,32},{32,64},{64,96},{96,128},{128,160},{160,192},{192,224},{224... | collective-permute-start | bytes 196616 | tf_op jit(solution)/shard_map/ppermute | solution.py:595
  12.7 5.8 %collective-permute-start.2 = (f32[3,16,8,128]{3,2,1,0:T(8,128)S(1)}, f32[3,16,8,128]{3,2,1,0:T(8,128)S(1)}, u32[]{:S(2)}, u32[]{:S(2)}) collective-permute-start(f32[3,16,8,128]{3,2,1,0:T(8,128)S(1)} %get-tuple-element.32), channel_id=1, source_target_pairs={{0,8},{8,16},{16,24},{24,0},{1,9},{9,17},{17,25},{25,1},{2,10},{10... | collective-permute-start | bytes 589832 | tf_op jit(solution)/shard_map/ppermute | solution.py:595
  14.0 4.5 %collective-permute-start.3 = (f32[3,16,8,128]{3,2,1,0:T(8,128)S(1)}, f32[3,16,8,128]{3,2,1,0:T(8,128)S(1)}, u32[]{:S(2)}, u32[]{:S(2)}) collective-permute-start(f32[3,16,8,128]{3,2,1,0:T(8,128)S(1)} %get-tuple-element.33), channel_id=1, source_target_pairs={{0,24},{8,0},{16,8},{24,16},{1,25},{9,1},{17,9},{25,17},{2,26},{10... | collective-permute-start | bytes 589832 | tf_op jit(solution)/shard_map/ppermute | solution.py:595
  18.6 8.9 %collective-permute-start.4 = (f32[3,7,32,128]{3,2,1,0:T(8,128)S(1)}, f32[3,7,32,128]{3,2,1,0:T(8,128)S(1)}, u32[]{:S(2)}, u32[]{:S(2)}) collective-permute-start(f32[3,7,32,128]{3,2,1,0:T(8,128)S(1)} %get-tuple-element.34), channel_id=1, source_target_pairs={{0,1},{1,2},{2,3},{3,4},{4,5},{5,6},{6,7},{7,0},{8,9},{9,10},{10,1... | collective-permute-start | bytes 1032200 | tf_op jit(solution)/shard_map/ppermute | solution.py:595
  23.3 6.7 %collective-permute-start.5 = (f32[3,7,32,128]{3,2,1,0:T(8,128)S(1)}, f32[3,7,32,128]{3,2,1,0:T(8,128)S(1)}, u32[]{:S(2)}, u32[]{:S(2)}) collective-permute-start(f32[3,7,32,128]{3,2,1,0:T(8,128)S(1)} %get-tuple-element.35), channel_id=1, source_target_pairs={{0,7},{1,0},{2,1},{3,2},{4,3},{5,4},{6,5},{7,6},{8,15},{9,8},{10,9... | collective-permute-start | bytes 1032200 | tf_op jit(solution)/shard_map/ppermute | solution.py:595
  39.3 6.9 %collective-permute-start.7 = (f32[18,8,128]{2,1,0:T(8,128)S(1)}, f32[18,8,128]{2,1,0:T(8,128)S(1)}, u32[]{:S(2)}, u32[]{:S(2)}) collective-permute-start(f32[18,8,128]{2,1,0:T(8,128)S(1)} %get-tuple-element.36.message), channel_id=1, source_target_pairs={{0,24},{8,0},{16,8},{24,16},{1,25},{9,1},{17,9},{25,17},{2,26},{10... | collective-permute-start | bytes 221192 | tf_op jit(solution)/shard_map/ppermute | solution.py:595
  42.0 4.9 %collective-permute-start.6 = (f32[18,8,128]{2,1,0:T(8,128)S(1)}, f32[18,8,128]{2,1,0:T(8,128)S(1)}, u32[]{:S(2)}, u32[]{:S(2)}) collective-permute-start(f32[18,8,128]{2,1,0:T(8,128)S(1)} %get-tuple-element.36.message), channel_id=1, source_target_pairs={{0,8},{8,16},{16,24},{24,0},{1,9},{9,17},{17,25},{25,1},{2,10},{10... | collective-permute-start | bytes 221192 | tf_op jit(solution)/shard_map/ppermute | solution.py:595
  42.0 4.1 %collective-permute-start.8 = (f32[2,8,128]{2,1,0:T(8,128)S(1)}, f32[2,8,128]{2,1,0:T(8,128)S(1)}, u32[]{:S(2)}, u32[]{:S(2)}) collective-permute-start(f32[2,8,128]{2,1,0:T(8,128)S(1)} %get-tuple-element.37), channel_id=1, source_target_pairs={{0,16},{8,24},{16,0},{24,8},{1,17},{9,25},{17,1},{25,9},{2,18},{10... | collective-permute-start | bytes 24584 | tf_op jit(solution)/shard_map/ppermute | solution.py:628
  46.1 0.9 copy-start.2
  46.9 0.6 copy-start.3
  47.6 4.0 %collective-permute-start.9 = (f32[44,8,128]{2,1,0:T(8,128)S(1)}, f32[44,8,128]{2,1,0:T(8,128)S(1)}, u32[]{:S(2)}, u32[]{:S(2)}) collective-permute-start(f32[44,8,128]{2,1,0:T(8,128)S(1)} %get-tuple-element.39), channel_id=1, source_target_pairs={{0,1},{1,2},{2,3},{3,4},{4,5},{5,6},{6,7},{7,0},{8,9},{9,10},{10,1... | collective-permute-start | bytes 540680 | tf_op jit(solution)/shard_map/ppermute | solution.py:595
  49.1 5.2 %collective-permute-start.10 = (f32[44,8,128]{2,1,0:T(8,128)S(1)}, f32[44,8,128]{2,1,0:T(8,128)S(1)}, u32[]{:S(2)}, u32[]{:S(2)}) collective-permute-start(f32[44,8,128]{2,1,0:T(8,128)S(1)} %get-tuple-element.38.own), channel_id=1, source_target_pairs={{0,7},{1,0},{2,1},{3,2},{4,3},{5,4},{6,5},{7,6},{8,15},{9,8},{10,9... | collective-permute-start | bytes 540680 | tf_op jit(solution)/shard_map/ppermute | solution.py:595
  51.6 2.8 %copy-start = (f32[44,8,128]{2,1,0:T(8,128)}, f32[44,8,128]{2,1,0:T(8,128)S(1)}, u32[]{:S(2)}) copy-start(f32[44,8,128]{2,1,0:T(8,128)S(1)} %collective-permute-done.9.z_low.refs_3_) | copy-start | bytes 540676
  54.4 0.7 copy-start.1
  55.0 5.6 %collective-permute-start.12 = (f32[24,8,128]{2,1,0:T(8,128)S(1)}, f32[24,8,128]{2,1,0:T(8,128)S(1)}, u32[]{:S(2)}, u32[]{:S(2)}) collective-permute-start(f32[24,8,128]{2,1,0:T(8,128)S(1)} %spread_z.1.own), channel_id=1, source_target_pairs={{0,5},{1,6},{2,7},{3,0},{4,1},{5,2},{6,3},{7,4},{8,13},{9,14},{10,... | collective-permute-start | bytes 294920 | tf_op jit(solution)/shard_map/ppermute | solution.py:595
  56.3 5.7 %collective-permute-start.11 = (f32[24,8,128]{2,1,0:T(8,128)S(1)}, f32[24,8,128]{2,1,0:T(8,128)S(1)}, u32[]{:S(2)}, u32[]{:S(2)}) collective-permute-start(f32[24,8,128]{2,1,0:T(8,128)S(1)} %spread_z.1.own), channel_id=1, source_target_pairs={{0,3},{1,4},{2,5},{3,6},{4,7},{5,0},{6,1},{7,2},{8,11},{9,12},{10,... | collective-permute-start | bytes 294920 | tf_op jit(solution)/shard_map/ppermute | solution.py:595

commit v3 on v2

--- a/solution.py
+++ b/solution.py
@@ -29,12 +29,18 @@
 
 
 def matmul(a, b):
-    return lax.dot_general(
-        a, b, (((1,), (0,)), ((), ())), precision=lax.Precision.HIGHEST, preferred_element_type=F32
-    )
-
-
-def planes(lo, hi, body, unroll=2):
+    b = b.astype(jnp.bfloat16)
+    total = None
+    for part in range(3):
+        piece = a.astype(jnp.bfloat16)
+        product = lax.dot_general(piece, b, (((1,), (0,)), ((), ())), preferred_element_type=F32)
+        total = product if total is None else total + product
+        if part < 2:
+            a = a - piece.astype(F32)
+    return total
+
+
+def planes(lo, hi, body, unroll=10):
     trips = (hi - lo) // unroll
     if trips > 1:
 
@@ -54,7 +60,7 @@
     def __init__(self, refs):
         self.wx, self.wy, self.wz, self.diag, self.inv = refs
 
-    def build(self, frac, scale, lo, hi, wraps, unroll=2):
+    def build(self, frac, scale, lo, hi, wraps, unroll=10):
         half = 0.5 * scale
         self.wz[lo - 1] = half * (frac[lo - 1] + frac[lo])
 
@@ -85,20 +91,20 @@
         near = near + self.wz[p] * q[p + 1] + self.wz[p - 1] * q[p - 1]
         return c, self.diag[p] * c - near
 
-    def first(self, rhs, out, lo, hi, unroll=2):
+    def first(self, rhs, out, lo, hi, unroll=10):
         def plane(p):
             out[p] = self.inv[p] * rhs[p]
 
         planes(lo, hi, plane, unroll)
 
-    def sweep(self, q, rhs, out, lo, hi, unroll=2):
+    def sweep(self, q, rhs, out, lo, hi, unroll=10):
         def plane(p):
             c, applied = self.apply(q, p)
             out[p] = c + self.inv[p] * (rhs[p] - applied)
 
         planes(lo, hi, plane, unroll)
 
-    def halved_residual(self, q, rhs, out, lo, hi, unroll=1):
+    def halved_residual(self, q, rhs, out, lo, hi, unroll=4):
         def pair(j):
             _, one = self.apply(q, lo + 2 * j)
             _, two = self.apply(q, lo + 2 * j + 1)
@@ -190,10 +196,8 @@
 
 
 def down_kernel(s, f, halo, y_low, y_high, z_low, z_high, *refs):
-    kept, own1, message, payload = refs[:7], refs[7], refs[8], refs[9]
-    F, Q, T, U, V, f1, F1, q1, d1, *w1 = refs[10:24]
-    S, D0, *w0 = refs[24:31]
-    sems = refs[31]
+    kept, own1, f1, F1 = refs[:7], refs[7], refs[8], refs[9]
+    F, Q, T, U, V, S, D0, *w0, sems = refs[10:]
     iz, iy = lax.axis_index("gz"), lax.axis_index("gy")
     nz, ny = lax.axis_size("gz"), lax.axis_size("gy")
     for p in (0, 31):
@@ -222,29 +226,35 @@
     for ref, z0, okay in ((z_low, 1, iz > 0), (z_high, 24, iz < nz - 1)):
         put(z0, 0, 7, 32, inside(okay), lambda k, ref=ref: (ref[0, k], ref[1, k], ref[2, k]))
 
-    started = copies(((S, kept[0]),), sems)
+    started = copies(((S.at[5:27], kept[0].at[5:27]),), sems)
     level = Level(w0)
     level.build(F, 1.0, 2, 30, (False, False))
-    started += copies(tuple(zip(w0, kept[2:])), sems.at[1:6])
+    started += copies(tuple((a.at[5:27], b.at[5:27]) for a, b in zip(w0, kept[2:])), sems.at[1:6])
     level.first(S, Q, 2, 30)
     level.sweep(Q, S, D0, 3, 29)
-    started += copies(((D0, kept[1]),), sems.at[6:7])
+    started += copies(((D0.at[5:27], kept[1].at[5:27]),), sems.at[6:7])
     level.halved_residual(D0, S, T, 4, 28)
     C = gather_pairs(256, 128, 0, 0, 128)
 
     def coarse(count, out, start):
-        U[0:count] = matmul(rows_of(T, count), C).reshape(count, 32, 128)
         for j in range(count):
-            out[start + j] = U[j, pl.ds(0, 16, 2), :] + U[j, pl.ds(1, 16, 2), :]
+            for half in range(2):
+                lanes = slice(128 * half, 128 * half + 128)
+                V[j, half] = T[j, :, lanes]
+                U[j, :, lanes] = V[j, half, pl.ds(0, 16, 2), :] + V[j, half, pl.ds(1, 16, 2), :]
+        out[start : start + count] = matmul(rows_of(U, count), C).reshape(count, 16, 128)
 
     coarse(12, f1, 1)
     halved(F, T, 2, 30)
     coarse(14, F1, 0)
     for j in range(8):
-        message[j] = f1[3 + j, 4:12, :]
-        message[8 + j] = F1[3 + j, 4:12, :]
-    started += copies(((message.at[0:16], own1),), sems.at[7:8])
-
+        own1[j] = f1[3 + j, 4:12, :]
+        own1[8 + j] = F1[3 + j, 4:12, :]
+    for copy in started:
+        copy.wait()
+
+
+def down_one_kernel(f1, F1, payload, V, q1, d1, *w1):
     level = Level(w1)
     level.build(F1, 0.25, 1, 13, (False, False))
     level.first(f1, q1, 1, 13)
@@ -256,13 +266,11 @@
     V[0:4] = both.reshape(4, 16, 128)
     for j in range(4):
         rows = V[j, pl.ds(4, 4, 2), :] + V[j, pl.ds(5, 4, 2), :]
-        message[16 + j // 2, 4 * (j % 2) : 4 * (j % 2) + 4, :] = rows
-    payload[...] = message[16:18]
-    for copy in started:
-        copy.wait()
-
-
-def spread_y_kernel(message, y_low, y_high, far, to_low, to_high):
+        for d in range(32):
+            payload[d, 4 * j : 4 * j + 4, :] = rows
+
+
+def spread_y_kernel(own, y_low, y_high, to_low, to_high):
     iy, ny = lax.axis_index("gy"), lax.axis_size("gy")
     low, high = inside(iy > 0), inside(iy < ny - 1)
     for out, start in ((to_low, 0), (to_high, 2)):
@@ -270,45 +278,31 @@
             for j in range(6):
                 at, z = (6 * k + j) * 3, 8 * k + start + j
                 out[at] = y_low[z] * low
-                out[at + 1] = message[z]
+                out[at + 1] = own[z]
                 out[at + 2] = y_high[z] * high
-        for step, ref, first in ((0, message, 16), (-1, y_low, 16), (1, y_high, 16), (2, far, 0)):
-            at = 36 + 2 * jnp.remainder(iy + step + ny, ny)
-            for k in range(2):
-                out[at + k] = ref[first + k]
-
-
-def spread_z_kernel(own, z_low, z_high, out):
-    for k, ref in enumerate((z_low, own, z_high)):
-        out[8 * k : 8 * k + 8] = ref[36:44]
-
-
-def middle_kernel(own, before, after, payload, f2h, F2h, d2h, *refs):
+
+
+def middle_kernel(got, own, y_low, y_high, payload, f2h, F2h, d2h, own_h, y_low_h, y_high_h, *refs):
     f2, F2, d2, q2, T, U, *w2, sems = refs
-    iz, nz = lax.axis_index("gz"), lax.axis_size("gz")
-    lane = index_of((8, 128), 1)
-    keep = lane < 48
+    started = copies(((own, own_h), (y_low, y_low_h), (y_high, y_high_h)), sems)
+    keep = index_of((16, 128), 1) < 48
     zero = jnp.zeros((16, 128), F32)
     for ref in (f2, F2, q2, d2):
         ref[0] = zero
         ref[33] = zero
-    for ref, start in ((before, -4), (own, -1), (after, 2)):
-        for k in range(3):
-            base = 1 + 4 * jnp.remainder(iz + start + k + nz, nz)
-            for gy in range(4):
-                for j in range(2):
-                    block = ref[8 * k + 2 * gy + j]
-                    rhs, frac = jnp.where(keep, block, 0.0), jnp.where(keep, turn(block, 64, 1), 0.0)
-                    for half in range(2):
-                        rows = slice(4 * half, 4 * half + 4)
-                        f2[base + 2 * j + half, 4 * gy : 4 * gy + 4, :] = rhs[rows]
-                        F2[base + 2 * j + half, 4 * gy : 4 * gy + 4, :] = frac[rows]
-    started = copies(((f2, f2h), (F2, F2h)), sems)
+    for gy in range(4):
+        for gz in range(8):
+            block = got[gy * 8 + gz]
+            rhs, frac = jnp.where(keep, block, 0.0), jnp.where(keep, turn(block, 64, 1), 0.0)
+            for j in range(4):
+                f2[1 + gz * 4 + j, 4 * gy : 4 * gy + 4, :] = rhs[4 * j : 4 * j + 4]
+                F2[1 + gz * 4 + j, 4 * gy : 4 * gy + 4, :] = frac[4 * j : 4 * j + 4]
+    started += copies(((f2, f2h), (F2, F2h)), sems.at[3:5])
     level = Level(w2)
-    level.build(F2, 0.25**2, 1, 33, (True, False), 4)
-    level.first(f2, q2, 1, 33, 4)
-    level.sweep(q2, f2, d2, 1, 33, 4)
-    started += copies(((d2, d2h),), sems.at[2:3])
+    level.build(F2, 0.25**2, 1, 33, (True, False), 16)
+    level.first(f2, q2, 1, 33, 16)
+    level.sweep(q2, f2, d2, 1, 33, 16)
+    started += copies(((d2, d2h),), sems.at[5:6])
     C = gather_pairs(128, 128, 8, 0, 16)
     for field in range(2):
         if field == 0:
@@ -403,14 +397,23 @@
     far, refs = refs[:15], refs[15:]
     pressure, residual, refs = refs[0], refs[1], refs[2:]
     near, sems = refs[:15], refs[15]
-    started = copies(tuple(zip(far, near)), sems)
+    iz, iy, ix = lax.axis_index("gz"), lax.axis_index("gy"), lax.axis_index("gx")
+    nz, ny = lax.axis_size("gz"), lax.axis_size("gy")
+    start = jnp.clip(4 * iz - 4, 0, 20)
+
+    def part(a, b):
+        if b.shape == BIG:
+            return a.at[5:27], b.at[5:27]
+        if b.shape == WINDOW:
+            return a.at[pl.ds(start, 14)], b
+        return a, b
+
+    started = copies(tuple(part(a, b) for a, b in zip(far, near)), sems)
     own1, y_low, y_high, z_low, z_high, f2, F2, d2, S, D0, wx0, wy0, wz0, g0, i0 = near
     refs = refs[16:]
     f3, F3, q3, d3, f4, F4, q4, d4 = refs[:8]
     w3, w4, w2, w1 = refs[8:13], refs[13:18], refs[18:23], refs[23:28]
-    T3, g5, F5, qa2, qb2, T2, f1, F1, qa1, qb1, T1, U1, T0, U0, qa0, qb0 = refs[28:]
-    iz, iy, ix = lax.axis_index("gz"), lax.axis_index("gy"), lax.axis_index("gx")
-    nz = lax.axis_size("gz")
+    T3, g5, F5, qa2, qb2, T2, T2y, f1, F1, qa1, qb1, T1, U1, T0, U0, qa0, qb0, kept_p, kept_r, out_sems = refs[28:]
     lane = index_of((8, 128), 1)
     row = index_of((8, 128), 0)
     zero = jnp.zeros((8, 128), F32)
@@ -484,29 +487,28 @@
     for copy in started[5:8]:
         copy.wait()
     two = Level(w2)
-    two.build(F2, 0.25**2, 1, 33, (True, False), 4)
+    two.build(F2, 0.25**2, 1, 13, (True, False), 12)
     shift = jnp.remainder(4 - 16 * ix, 128)
-    for j in range(16):
-        T2[0, j] = pltpu.roll(q3[1 + j], shift, 1)
-    T2[1] = matmul(T2[0].reshape(128, 128), spread_pairs(128, 128, 0, 0, 24)).reshape(16, 8, 128)
+    for j in range(6):
+        T2[0, j] = pltpu.roll(q3[1 + start // 2 + j], shift, 1)
+    T2[1] = matmul(T2[0].reshape(48, 128), spread_pairs(128, 128, 0, 0, 24)).reshape(6, 8, 128)
     zero2 = jnp.zeros((16, 128), F32)
     for ref in (qa2, qb2):
         ref[0] = zero2
-        ref[33] = zero2
-    for j in range(16):
-        part = T2[1, j]
-        qb2[1, pl.ds(0, 8, 2), :] = part
-        qb2[1, pl.ds(1, 8, 2), :] = part
-        plane = qb2[1]
+        ref[13] = zero2
+    for j in range(6):
+        rows = T2[1, j]
+        T2y[j, pl.ds(0, 8, 2), :] = rows
+        T2y[j, pl.ds(1, 8, 2), :] = rows
+        plane = T2y[j]
         for k in (0, 1):
             p = 1 + 2 * j + k
             qa2[p] = d2[p] + jnp.where(F2[p] > 0.0, plane, 0.0)
-    two.sweep(qa2, f2, qb2, 1, 33, 4)
-    two.sweep(qb2, f2, qa2, 1, 33, 4)
+    two.sweep(qa2, f2, qb2, 1, 13, 12)
+    two.sweep(qb2, f2, qa2, 1, 13, 12)
 
     for copy in started[:5]:
         copy.wait()
-    iy, ny = lax.axis_index("gy"), lax.axis_size("gy")
     low, high, under, over = inside(iy > 0), inside(iy < ny - 1), inside(iz > 0), inside(iz < nz - 1)
     for k, ref in enumerate((f1, F1)):
         for z in range(8):
@@ -524,14 +526,14 @@
     one.sweep(qa1, f1, qb1, 4, 20)
     shift = jnp.remainder(4 - 4 * iy, 16)
     for j in range(8):
-        at = jnp.clip(4 * iz - 2 + j, 0, 31)
+        at = jnp.clip(4 * iz - 2 + j, 0, 31) - start
         U1[j] = pltpu.roll(qa2[1 + at], shift, 0)
     U1[...] = matmul(rows_of(U1, 8), spread_pairs(128, 128, 0, 112, 48)).reshape(8, 16, 128)
     for j in range(8):
         part = U1[j, 0:12, :]
-        T1[pl.ds(0, 12, 2), :] = part
-        T1[pl.ds(1, 12, 2), :] = part
-        plane = T1[...]
+        T1[j, pl.ds(0, 12, 2), :] = part
+        T1[j, pl.ds(1, 12, 2), :] = part
+        plane = T1[j]
         for k in (0, 1):
             p = 4 + 2 * j + k
             qa1[p] = qb1[p] + jnp.where(F1[p] > 0.0, plane, 0.0)
@@ -546,23 +548,30 @@
     def refine(j):
         for half in (0, 1):
             part = T0[j, 4:20, 128 * half : 128 * half + 128]
-            U0[half, pl.ds(0, 16, 2), :] = part
-            U0[half, pl.ds(1, 16, 2), :] = part
-        plane = jnp.concatenate([U0[0], U0[1]], axis=1)
+            U0[half, j, pl.ds(0, 16, 2), :] = part
+            U0[half, j, pl.ds(1, 16, 2), :] = part
+        plane = jnp.concatenate([U0[0, j], U0[1, j]], axis=1)
         for k in (0, 1):
             p = 4 + 2 * j + k
             qa0[p] = D0[p] + jnp.where(i0[p] > 0.0, plane, 0.0)
 
-    planes(0, 12, refine, 1)
+    planes(0, 12, refine, 4)
     zero_level.sweep(qa0, S, qb0, 6, 26)
     zero_level.sweep(qb0, S, qa0, 7, 25)
 
     def finish(p):
         c, applied = zero_level.apply(qa0, p)
-        pressure[p - 8] = c[8:24, 0:128]
-        residual[p - 8] = (S[p] - applied)[8:24, 0:128]
-
-    planes(8, 24, finish)
+        kept_p[p - 8] = c[8:24, 0:128]
+        kept_r[p - 8] = (S[p] - applied)[8:24, 0:128]
+
+    started = []
+    for k in (0, 8):
+        planes(8 + k, 16 + k, finish, 8)
+        at = slice(k, k + 8)
+        pairs = ((kept_p.at[at], pressure.at[at]), (kept_r.at[at], residual.at[at]))
+        started += copies(pairs, out_sems.at[k // 4 : k // 4 + 2])
+    for copy in started:
+        copy.wait()
 
 
 def call(kernel, name, ins, outs, scratch=()):
@@ -596,6 +605,7 @@
 
 
 BIG, MID, MID2, WIDE1 = (32, 32, 256), (14, 16, 128), (34, 16, 128), (24, 24, 128)
+WINDOW = (14, 16, 128)
 THREE, FOUR = (18, 8, 128), (10, 8, 128)
 
 
@@ -616,50 +626,50 @@
     layers = (3, 7, 32, 128)
     to_low, to_high = call(pack_z_kernel, "pack_z", "vvvvv", [("v", layers)] * 2)(s, f, halo, y_low, y_high)
     z_low, z_high = exchange(to_low, to_high, "gz")
-    *fine, own1, message, payload = call(
+    *fine, own1, f1, F1 = call(
         down_kernel,
         "down",
         "vvvvvvv",
-        [("h", BIG)] * 7 + [("h", (16, 8, 128)), ("v", (18, 8, 128)), ("v", (2, 8, 128))],
-        [BIG, BIG, (14, 32, 256), (14, 32, 128), (4, 16, 128)] + [MID] * 9 + [BIG] * 7 + [dma(8)],
+        [("h", BIG)] * 7 + [("v", (16, 8, 128)), ("v", MID), ("v", MID)],
+        [BIG, BIG, (14, 32, 256), (14, 16, 256), (14, 2, 32, 128)] + [BIG] * 7 + [dma(7)],
     )(s, f, halo, y_low, y_high, z_low, z_high)
-
-    y_low, y_high = exchange(message, message, "gy")
-    opposite = lax.ppermute(payload, "gy", ring("gy", 2))
-    layers = (44, 8, 128)
-    to_low, to_high = call(spread_y_kernel, "spread_y", "vvvv", [("v", layers)] * 2)(message, y_low, y_high, opposite)
+    y_low, y_high = exchange(own1, own1, "gy")
+    (payload,) = call(
+        down_one_kernel, "down_one", "vv", [("v", (32, 16, 128))], [(4, 16, 128)] + [MID] * 7
+    )(f1, F1)
+    got = lax.all_to_all(payload, ("gy", "gz"), 0, 0)
+    layers = (36, 8, 128)
+    to_low, to_high = call(spread_y_kernel, "spread_y", "vvv", [("v", layers)] * 2)(own1, y_low, y_high)
     z_low, z_high = exchange(to_low, to_high, "gz")
-    (near,) = call(spread_z_kernel, "spread_z", "vvv", [("v", (24, 8, 128))])(to_low, z_low, z_high)
-    before, after = exchange(near, near, "gz", 3)
-    payload, f2, F2, d2 = call(
+    payload, *kept = call(
         middle_kernel,
         "middle",
-        "vvv",
-        [("v", (8, 4, 8, 128))] + [("h", MID2)] * 3,
-        [MID2] * 4 + [(16, 16, 128), (16, 16, 128)] + [MID2] * 5 + [dma(3)],
-    )(near, before, after)
+        "vvvv",
+        [("v", (8, 4, 8, 128))] + [("h", MID2)] * 3 + [("h", (16, 8, 128))] * 3,
+        [MID2] * 4 + [(16, 16, 128), (16, 16, 128)] + [MID2] * 5 + [dma(6)],
+    )(got, own1, y_low, y_high)
     got = lax.all_to_all(payload, "gx", 0, 0)
+    f2, F2, d2, own1, y_low, y_high = kept
     kept = [own1, y_low, y_high, z_low, z_high, f2, F2, d2, *fine]
     pressure, residual = call(
         up_kernel,
         "up",
         "v" + "h" * 15,
-        [("n", own)] * 2,
-        [(16, 8, 128)]
-        + [(18, 8, 128)] * 2
-        + [(44, 8, 128)] * 2
-        + [MID2] * 3
+        [("h", own)] * 2,
+        [(16, 8, 128)] * 3
+        + [layers] * 2
+        + [WINDOW] * 3
         + [BIG] * 7
         + [dma(15)]
         + [THREE] * 4
         + [FOUR] * 4
         + [THREE] * 5
         + [FOUR] * 5
-        + [MID2] * 5
+        + [WINDOW] * 5
         + [WIDE1] * 5
-        + [(9, 8, 128), (8, 128), (8, 128), MID2, MID2, (2, 16, 8, 128)]
+        + [(9, 8, 128), (8, 128), (8, 128), WINDOW, WINDOW, (2, 6, 8, 128), (6, 16, 128)]
         + [WIDE1] * 4
-        + [(24, 128), (8, 16, 128), (12, 24, 256), (2, 32, 128), BIG, BIG],
+        + [(8, 24, 128), (8, 16, 128), (12, 24, 256), (2, 12, 32, 128), BIG, BIG, own, own, dma(4)],
     )(got, *kept)
     return (pressure, residual)
 

time: 91.2 us -> 75.6 us (0.83); the launches traced: 89.8 us -> 75.3 us
  blocking collectives: 10.3 us -> 0 us
  Pallas kernels: 27.9 us -> 17.6 us
  starting transfers between devices: 22.8 us -> 27.7 us
  waiting for transfers between devices: 26.6 us -> 29.2 us
  local copies, waits for them, and re-layouts: 1.24 us -> 0.01 us
    all_to_all x0 -> x2, starting transfers between devices: none -> 10.4 us  [the longest x1 6.84 us: local(): got = lax.all_to_all(payload, ('gy', 'gz'), 0, 0)]
    pallas_call x8, Pallas kernels: 27.9 us -> 17.6 us  [run(): pl.pallas_call(kernel, out_shape=[kind[k](shape, F32) for k, shape in out...]
    all_to_all x1 -> x0, blocking collectives: 10.3 us -> none  [local(): got = lax.all_to_all(payload, 'gx', 0, 0)]
    all_to_all x0 -> x2, waiting for transfers between devices: none -> 5.38 us  [the longest x1 3.9 us: local(): got = lax.all_to_all(payload, 'gx', 0, 0)]
    ppermute x1 -> x0, waiting for transfers between devices: 2.84 us -> none  [local(): opposite = lax.ppermute(payload, 'gy', ring('gy', 2))]
    ppermute x6 -> x5, starting transfers between devices: 12 us -> 9.41 us  [exchange(): lax.ppermute(to_low, axis, ring(axis, -reach))]
    ppermute x6 -> x5, waiting for transfers between devices: 8.89 us -> 6.57 us  [exchange(): lax.ppermute(to_low, axis, ring(axis, -reach))]
    ppermute x6 -> x5, waiting for transfers between devices: 14.9 us -> 17.2 us  [exchange(): lax.ppermute(to_high, axis, ring(axis, reach))]
  transfers between devices with their start and end apart: 13 -> 12, of which waited for: 11 -> 10; matrix products, arithmetic and copies ran while one was open for 0% -> 0% of each run, Pallas kernels for 0% -> 0%
where the time goes in v3:
time: 75.6 us; the launch traced here: 75.3 us
  waiting for transfers between devices  29.2 us (39%)
  starting transfers between devices  27.7 us (37%)
  Pallas kernels  17.6 us (23%)
  between operations  0.86 us (1%)
    pallas_call x8, Pallas kernels, run(): pl.pallas_call(kernel, out_shape=[kind[k](shape, F32) for k, shape in out...  17.6 us
    ppermute x5, waiting for transfers between devices, exchange(): lax.ppermute(to_high, axis, ring(axis, reach))  17.2 us
    ppermute x5, starting transfers between devices, exchange(): lax.ppermute(to_low, axis, ring(axis, -reach))  9.41 us
    ppermute x5, starting transfers between devices, exchange(): lax.ppermute(to_high, axis, ring(axis, reach))  7.88 us
    all_to_all x1, starting transfers between devices, local(): got = lax.all_to_all(payload, ('gy', 'gz'), 0, 0)  6.84 us
    ppermute x5, waiting for transfers between devices, exchange(): lax.ppermute(to_low, axis, ring(axis, -reach))  6.57 us
    all_to_all x1, waiting for transfers between devices, local(): got = lax.all_to_all(payload, 'gx', 0, 0)  3.9 us
    all_to_all x1, starting transfers between devices, local(): got = lax.all_to_all(payload, 'gx', 0, 0)  3.56 us
  transfers between devices with their start and end apart: 12, of which 10 were waited for; matrix products, arithmetic and copies ran while one was open for 0% of the time, Pallas kernels for 0%

profile of v3, /device:TPU:1, one launch (start us, length us, event | category | flops | bytes accessed | tf_op | source)
XLA Modules:
  0.0 75.3 jit_solution(1281505005569695059)
XLA Ops:
  0.6 1.1 %pack_x.1 = (f32[16,16,128]{2,1,0:T(8,128)S(1)}, f32[16,16,128]{2,1,0:T(8,128)S(1)}, f32[8,16,128]{2,1,0:T(8,128)S(1)}, f32[8,16,128]{2,1,0:T(8,128)S(1)}) custom-call(f32[16,16,128]{2,1,0:T(8,128)} %source.1, f32[16,16,128]{2,1,0:T(8,128)} %fraction.1), custom_call_target="tpu_custom_call" | custom-call | tf_op jit(solution)/shard_map/pack_x/pallas_call | solution.py:585
  1.8 6.5 %collective-permute-start = (f32[8,16,128]{2,1,0:T(8,128)S(1)}, f32[8,16,128]{2,1,0:T(8,128)S(1)}, u32[]{:S(2)}, u32[]{:S(2)}) collective-permute-start(f32[8,16,128]{2,1,0:T(8,128)S(1)} %get-tuple-element.32), channel_id=1, source_target_pairs={{0,224},{32,0},{64,32},{96,64},{128,96},{160,128},{192,160},{224,1... | collective-permute-start | bytes 196616 | tf_op jit(solution)/shard_map/ppermute | solution.py:604
  8.3 0.0 collective-permute-start.1
  8.3 1.3 %collective-permute-done.from_right = f32[8,16,128]{2,1,0:T(8,128)S(1)} collective-permute-done((f32[8,16,128]{2,1,0:T(8,128)S(1)}, f32[8,16,128]{2,1,0:T(8,128)S(1)}, u32[]{:S(2)}, u32[]{:S(2)}) %collective-permute-start) | collective-permute-done | bytes 65568 | tf_op jit(solution)/shard_map/ppermute | solution.py:604
  9.6 3.0 %collective-permute-done.1.from_left = f32[8,16,128]{2,1,0:T(8,128)S(1)} collective-permute-done((f32[8,16,128]{2,1,0:T(8,128)S(1)}, f32[8,16,128]{2,1,0:T(8,128)S(1)}, u32[]{:S(2)}, u32[]{:S(2)}) %collective-permute-start.1) | collective-permute-done | bytes 65568 | tf_op jit(solution)/shard_map/ppermute | solution.py:604
  12.6 0.1 pack_y.1
  12.7 1.3 %collective-permute-start.2 = (f32[3,16,8,128]{3,2,1,0:T(8,128)S(1)}, f32[3,16,8,128]{3,2,1,0:T(8,128)S(1)}, u32[]{:S(2)}, u32[]{:S(2)}) collective-permute-start(f32[3,16,8,128]{3,2,1,0:T(8,128)S(1)} %get-tuple-element.35), channel_id=1, source_target_pairs={{0,8},{8,16},{16,24},{24,0},{1,9},{9,17},{17,25},{25,1},{2,10},{10... | collective-permute-start | bytes 589832 | tf_op jit(solution)/shard_map/ppermute | solution.py:604
  14.0 1.5 %collective-permute-start.3 = (f32[3,16,8,128]{3,2,1,0:T(8,128)S(1)}, f32[3,16,8,128]{3,2,1,0:T(8,128)S(1)}, u32[]{:S(2)}, u32[]{:S(2)}) collective-permute-start(f32[3,16,8,128]{3,2,1,0:T(8,128)S(1)} %get-tuple-element.36), channel_id=1, source_target_pairs={{0,24},{8,0},{16,8},{24,16},{1,25},{9,1},{17,9},{25,17},{2,26},{10... | collective-permute-start | bytes 589832 | tf_op jit(solution)/shard_map/ppermute | solution.py:604
  15.5 3.1 %collective-permute-done.2.y_low = f32[3,16,8,128]{3,2,1,0:T(8,128)S(1)} collective-permute-done((f32[3,16,8,128]{3,2,1,0:T(8,128)S(1)}, f32[3,16,8,128]{3,2,1,0:T(8,128)S(1)}, u32[]{:S(2)}, u32[]{:S(2)}) %collective-permute-start.2) | collective-permute-done | bytes 196640 | tf_op jit(solution)/shard_map/ppermute | solution.py:604
  18.5 0.0 collective-permute-done.3.y_high
  18.6 4.7 %collective-permute-start.4 = (f32[3,7,32,128]{3,2,1,0:T(8,128)S(1)}, f32[3,7,32,128]{3,2,1,0:T(8,128)S(1)}, u32[]{:S(2)}, u32[]{:S(2)}) collective-permute-start(f32[3,7,32,128]{3,2,1,0:T(8,128)S(1)} %get-tuple-element.37), channel_id=1, source_target_pairs={{0,1},{1,2},{2,3},{3,4},{4,5},{5,6},{6,7},{7,0},{8,9},{9,10},{10,1... | collective-permute-start | bytes 1032200 | tf_op jit(solution)/shard_map/ppermute | solution.py:604
  23.3 0.0 collective-permute-start.5
  23.3 4.2 %collective-permute-done.4.z_low = f32[3,7,32,128]{3,2,1,0:T(8,128)S(1)} collective-permute-done((f32[3,7,32,128]{3,2,1,0:T(8,128)S(1)}, f32[3,7,32,128]{3,2,1,0:T(8,128)S(1)}, u32[]{:S(2)}, u32[]{:S(2)}) %collective-permute-start.4) | collective-permute-done | bytes 344096 | tf_op jit(solution)/shard_map/ppermute | solution.py:604
  27.5 2.5 %collective-permute-done.5.z_high = f32[3,7,32,128]{3,2,1,0:T(8,128)S(1)} collective-permute-done((f32[3,7,32,128]{3,2,1,0:T(8,128)S(1)}, f32[3,7,32,128]{3,2,1,0:T(8,128)S(1)}, u32[]{:S(2)}, u32[]{:S(2)}) %collective-permute-start.5) | collective-permute-done | bytes 344096 | tf_op jit(solution)/shard_map/ppermute | solution.py:604
  30.0 4.1 %down.1 = (f32[32,32,256]{2,1,0:T(8,128)}, f32[32,32,256]{2,1,0:T(8,128)}, f32[32,32,256]{2,1,0:T(8,128)}, f32[32,32,256]{2,1,0:T(8,128)}, f32[32,32,256]{2,1,0:...) custom-call(f32[16,16,128]{2,1,0:T(8,128)S(1)} %get-tuple-element.30, ...), custom_call_target="tpu_custom_call" | custom-call | tf_op jit(solution)/shard_map/down/pallas_call | solution.py:585
  34.1 1.2 %down_one.1 = f32[32,16,128]{2,1,0:T(8,128)} custom-call(f32[14,16,128]{2,1,0:T(8,128)S(1)} %get-tuple-element.39.f1, f32[14,16,128]{2,1,0:T(8,128)S(1)} %get-tuple-element.40.F1), custom_call_target="tpu_custom_call" | custom-call | tf_op jit(solution)/shard_map/down_one/pallas_call | solution.py:585
  35.3 6.8 %all-to-all-start = ((f32[32,16,128]{2,1,0:T(8,128)}), f32[32,16,128]{2,1,0:T(8,128)S(1)}, u32[]{:S(2)}, u32[]{:S(2)}) async-start(f32[32,16,128]{2,1,0:T(8,128)} %down_one.1), calls=%async_computation | async-start | bytes 524288 | tf_op jit(solution)/shard_map/all_to_all | solution.py:640
  42.1 1.5 %collective-permute-start.6 = (f32[16,8,128]{2,1,0:T(8,128)S(1)}, f32[16,8,128]{2,1,0:T(8,128)S(1)}, u32[]{:S(2)}, u32[]{:S(2)}) collective-permute-start(f32[16,8,128]{2,1,0:T(8,128)S(1)} %get-tuple-element.41.own), channel_id=1, source_target_pairs={{0,8},{8,16},{16,24},{24,0},{1,9},{9,17},{17,25},{25,1},{2,10},{10... | collective-permute-start | bytes 196616 | tf_op jit(solution)/shard_map/ppermute | solution.py:604
  43.6 1.3 %collective-permute-start.7 = (f32[16,8,128]{2,1,0:T(8,128)S(1)}, f32[16,8,128]{2,1,0:T(8,128)S(1)}, u32[]{:S(2)}, u32[]{:S(2)}) collective-permute-start(f32[16,8,128]{2,1,0:T(8,128)S(1)} %get-tuple-element.41.own), channel_id=1, source_target_pairs={{0,24},{8,0},{16,8},{24,16},{1,25},{9,1},{17,9},{25,17},{2,26},{10... | collective-permute-start | bytes 196616 | tf_op jit(solution)/shard_map/ppermute | solution.py:604
  44.9 5.0 %collective-permute-done.6.y_low = f32[16,8,128]{2,1,0:T(8,128)S(1)} collective-permute-done((f32[16,8,128]{2,1,0:T(8,128)S(1)}, f32[16,8,128]{2,1,0:T(8,128)S(1)}, u32[]{:S(2)}, u32[]{:S(2)}) %collective-permute-start.6) | collective-permute-done | bytes 65568 | tf_op jit(solution)/shard_map/ppermute | solution.py:604
  49.9 0.0 collective-permute-done.7.y_high
  49.9 1.5 %all-to-all-done.got = f32[32,16,128]{2,1,0:T(8,128)S(1)} async-done(((f32[32,16,128]{2,1,0:T(8,128)}), f32[32,16,128]{2,1,0:T(8,128)S(1)}, u32[]{:S(2)}, u32[]{:S(2)}) %all-to-all-start) | async-done | bytes 262176 | tf_op jit(solution)/shard_map/all_to_all | solution.py:640
  51.4 2.7 %middle.1 = (f32[8,4,8,128]{3,2,1,0:T(8,128)}, f32[34,16,128]{2,1,0:T(8,128)}, f32[34,16,128]{2,1,0:T(8,128)}, f32[34,16,128]{2,1,0:T(8,128)}, f32[16,8,128]{2,1...) custom-call(f32[32,16,128]{2,1,0:T(8,128)S(1)} %all-to-all-done.got, f32[16,8,128]{2,1,0:T(8,128)S(1)} %get-tuple-element.41.own, ...), custom_call_target="tpu_custom_call" | custom-call | tf_op jit(solution)/shard_map/middle/pallas_call | solution.py:585
  54.1 3.6 %all-to-all-start.1 = ((f32[8,4,8,128]{3,2,1,0:T(8,128)}), f32[8,4,8,128]{3,2,1,0:T(8,128)S(1)}, u32[]{:S(2)}, u32[]{:S(2)}) async-start(f32[8,4,8,128]{3,2,1,0:T(8,128)} %get-tuple-element.42), calls=%async_computation.1 | async-start | bytes 262144 | tf_op jit(solution)/shard_map/all_to_all | solution.py:651
  57.7 0.4 collective-permute-start.8
  58.1 0.1 collective-permute-start.9
  58.2 2.0 %collective-permute-done.8.refs_3_ = f32[36,8,128]{2,1,0:T(8,128)S(1)} collective-permute-done((f32[36,8,128]{2,1,0:T(8,128)S(1)}, f32[36,8,128]{2,1,0:T(8,128)S(1)}, u32[]{:S(2)}, u32[]{:S(2)}) %collective-permute-start.8) | collective-permute-done | bytes 147488 | tf_op jit(solution)/shard_map/ppermute | solution.py:604
  60.2 0.0 copy-start
  60.2 2.8 %collective-permute-done.9.refs_4_ = f32[36,8,128]{2,1,0:T(8,128)S(1)} collective-permute-done((f32[36,8,128]{2,1,0:T(8,128)S(1)}, f32[36,8,128]{2,1,0:T(8,128)S(1)}, u32[]{:S(2)}, u32[]{:S(2)}) %collective-permute-start.9) | collective-permute-done | bytes 147488 | tf_op jit(solution)/shard_map/ppermute | solution.py:604
  63.0 0.0 copy-start.1
  63.0 3.9 %all-to-all-done.1.got = f32[8,4,8,128]{3,2,1,0:T(8,128)S(1)} async-done(((f32[8,4,8,128]{3,2,1,0:T(8,128)}), f32[8,4,8,128]{3,2,1,0:T(8,128)S(1)}, u32[]{:S(2)}, u32[]{:S(2)}) %all-to-all-start.1) | async-done | bytes 131104 | tf_op jit(solution)/shard_map/all_to_all | solution.py:651
  66.9 0.0 copy-done
  66.9 0.0 copy-done.1
  66.9 8.3 %up.1 = (f32[16,16,128]{2,1,0:T(8,128)}, f32[16,16,128]{2,1,0:T(8,128)}) custom-call(f32[8,4,8,128]{3,2,1,0:T(8,128)S(1)} %all-to-all-done.1.got, f32[16,8,128]{2,1,0:T(8,128)} %get-tuple-element.43.refs_0_, f32[16,8,128]{2,1,0:T(8,128)} %get-tuple-element.44.refs_1_, f32[16,8,128]{2,1,0:T(8,128)} %get-tuple-element.45.refs_2_, f32[36,8,128]{2,1,0:T(8,128)} %copy-done, ...), custom_call_target="tpu_custom_call" | custom-call | tf_op jit(solution)/shard_map/up/pallas_call | solution.py:585
  (2 shorter events, 0.1 us)
Async XLA Ops:
  1.8 7.8 %collective-permute-start = (f32[8,16,128]{2,1,0:T(8,128)S(1)}, f32[8,16,128]{2,1,0:T(8,128)S(1)}, u32[]{:S(2)}, u32[]{:S(2)}) collective-permute-start(f32[8,16,128]{2,1,0:T(8,128)S(1)} %get-tuple-element.32), channel_id=1, source_target_pairs={{0,224},{32,0},{64,32},{96,64},{128,96},{160,128},{192,160},{224,1... | collective-permute-start | bytes 196616 | tf_op jit(solution)/shard_map/ppermute | solution.py:604
  8.3 4.3 %collective-permute-start.1 = (f32[8,16,128]{2,1,0:T(8,128)S(1)}, f32[8,16,128]{2,1,0:T(8,128)S(1)}, u32[]{:S(2)}, u32[]{:S(2)}) collective-permute-start(f32[8,16,128]{2,1,0:T(8,128)S(1)} %get-tuple-element.33), channel_id=1, source_target_pairs={{0,32},{32,64},{64,96},{96,128},{128,160},{160,192},{192,224},{224... | collective-permute-start | bytes 196616 | tf_op jit(solution)/shard_map/ppermute | solution.py:604
  12.7 5.8 %collective-permute-start.2 = (f32[3,16,8,128]{3,2,1,0:T(8,128)S(1)}, f32[3,16,8,128]{3,2,1,0:T(8,128)S(1)}, u32[]{:S(2)}, u32[]{:S(2)}) collective-permute-start(f32[3,16,8,128]{3,2,1,0:T(8,128)S(1)} %get-tuple-element.35), channel_id=1, source_target_pairs={{0,8},{8,16},{16,24},{24,0},{1,9},{9,17},{17,25},{25,1},{2,10},{10... | collective-permute-start | bytes 589832 | tf_op jit(solution)/shard_map/ppermute | solution.py:604
  14.0 4.5 %collective-permute-start.3 = (f32[3,16,8,128]{3,2,1,0:T(8,128)S(1)}, f32[3,16,8,128]{3,2,1,0:T(8,128)S(1)}, u32[]{:S(2)}, u32[]{:S(2)}) collective-permute-start(f32[3,16,8,128]{3,2,1,0:T(8,128)S(1)} %get-tuple-element.36), channel_id=1, source_target_pairs={{0,24},{8,0},{16,8},{24,16},{1,25},{9,1},{17,9},{25,17},{2,26},{10... | collective-permute-start | bytes 589832 | tf_op jit(solution)/shard_map/ppermute | solution.py:604
  18.6 8.9 %collective-permute-start.4 = (f32[3,7,32,128]{3,2,1,0:T(8,128)S(1)}, f32[3,7,32,128]{3,2,1,0:T(8,128)S(1)}, u32[]{:S(2)}, u32[]{:S(2)}) collective-permute-start(f32[3,7,32,128]{3,2,1,0:T(8,128)S(1)} %get-tuple-element.37), channel_id=1, source_target_pairs={{0,1},{1,2},{2,3},{3,4},{4,5},{5,6},{6,7},{7,0},{8,9},{9,10},{10,1... | collective-permute-start | bytes 1032200 | tf_op jit(solution)/shard_map/ppermute | solution.py:604
  23.3 6.7 %collective-permute-start.5 = (f32[3,7,32,128]{3,2,1,0:T(8,128)S(1)}, f32[3,7,32,128]{3,2,1,0:T(8,128)S(1)}, u32[]{:S(2)}, u32[]{:S(2)}) collective-permute-start(f32[3,7,32,128]{3,2,1,0:T(8,128)S(1)} %get-tuple-element.38), channel_id=1, source_target_pairs={{0,7},{1,0},{2,1},{3,2},{4,3},{5,4},{6,5},{7,6},{8,15},{9,8},{10,9... | collective-permute-start | bytes 1032200 | tf_op jit(solution)/shard_map/ppermute | solution.py:604
  35.3 16.1 %all-to-all-start = ((f32[32,16,128]{2,1,0:T(8,128)}), f32[32,16,128]{2,1,0:T(8,128)S(1)}, u32[]{:S(2)}, u32[]{:S(2)}) async-start(f32[32,16,128]{2,1,0:T(8,128)} %down_one.1), calls=%async_computation | async-start | bytes 524288 | tf_op jit(solution)/shard_map/all_to_all | solution.py:640
  42.1 7.8 %collective-permute-start.6 = (f32[16,8,128]{2,1,0:T(8,128)S(1)}, f32[16,8,128]{2,1,0:T(8,128)S(1)}, u32[]{:S(2)}, u32[]{:S(2)}) collective-permute-start(f32[16,8,128]{2,1,0:T(8,128)S(1)} %get-tuple-element.41.own), channel_id=1, source_target_pairs={{0,8},{8,16},{16,24},{24,0},{1,9},{9,17},{17,25},{25,1},{2,10},{10... | collective-permute-start | bytes 196616 | tf_op jit(solution)/shard_map/ppermute | solution.py:604
  43.6 6.3 %collective-permute-start.7 = (f32[16,8,128]{2,1,0:T(8,128)S(1)}, f32[16,8,128]{2,1,0:T(8,128)S(1)}, u32[]{:S(2)}, u32[]{:S(2)}) collective-permute-start(f32[16,8,128]{2,1,0:T(8,128)S(1)} %get-tuple-element.41.own), channel_id=1, source_target_pairs={{0,24},{8,0},{16,8},{24,16},{1,25},{9,1},{17,9},{25,17},{2,26},{10... | collective-permute-start | bytes 196616 | tf_op jit(solution)/shard_map/ppermute | solution.py:604
  54.1 12.8 %all-to-all-start.1 = ((f32[8,4,8,128]{3,2,1,0:T(8,128)}), f32[8,4,8,128]{3,2,1,0:T(8,128)S(1)}, u32[]{:S(2)}, u32[]{:S(2)}) async-start(f32[8,4,8,128]{3,2,1,0:T(8,128)} %get-tuple-element.42), calls=%async_computation.1 | async-start | bytes 262144 | tf_op jit(solution)/shard_map/all_to_all | solution.py:651
  57.7 2.5 %collective-permute-start.8 = (f32[36,8,128]{2,1,0:T(8,128)S(1)}, f32[36,8,128]{2,1,0:T(8,128)S(1)}, u32[]{:S(2)}, u32[]{:S(2)}) collective-permute-start(f32[36,8,128]{2,1,0:T(8,128)S(1)} %get-tuple-element.46), channel_id=1, source_target_pairs={{0,1},{1,2},{2,3},{3,4},{4,5},{5,6},{6,7},{7,0},{8,9},{9,10},{10,1... | collective-permute-start | bytes 442376 | tf_op jit(solution)/shard_map/ppermute | solution.py:604
  58.1 4.9 %collective-permute-start.9 = (f32[36,8,128]{2,1,0:T(8,128)S(1)}, f32[36,8,128]{2,1,0:T(8,128)S(1)}, u32[]{:S(2)}, u32[]{:S(2)}) collective-permute-start(f32[36,8,128]{2,1,0:T(8,128)S(1)} %get-tuple-element.47), channel_id=1, source_target_pairs={{0,7},{1,0},{2,1},{3,2},{4,3},{5,4},{6,5},{7,6},{8,15},{9,8},{10,9... | collective-permute-start | bytes 442376 | tf_op jit(solution)/shard_map/ppermute | solution.py:604
  60.2 6.7 %copy-start = (f32[36,8,128]{2,1,0:T(8,128)}, f32[36,8,128]{2,1,0:T(8,128)S(1)}, u32[]{:S(2)}) copy-start(f32[36,8,128]{2,1,0:T(8,128)S(1)} %collective-permute-done.8.refs_3_) | copy-start | bytes 442372
  63.0 3.9 %copy-start.1 = (f32[36,8,128]{2,1,0:T(8,128)}, f32[36,8,128]{2,1,0:T(8,128)S(1)}, u32[]{:S(2)}) copy-start(f32[36,8,128]{2,1,0:T(8,128)S(1)} %collective-permute-done.9.refs_4_) | copy-start | bytes 442372

commit v4 on v3

--- a/solution.py
+++ b/solution.py
@@ -85,11 +85,14 @@
 
         planes(lo, hi, plane, unroll)
 
-    def apply(self, q, p):
+    def near(self, q, p):
         c, wx, wy = q[p], self.wx[p], self.wy[p]
-        near = wx * ahead(c, 1) + behind(wx * c, 1) + wy * ahead(c, 0) + behind(wy * c, 0)
-        near = near + self.wz[p] * q[p + 1] + self.wz[p - 1] * q[p - 1]
-        return c, self.diag[p] * c - near
+        total = wx * ahead(c, 1) + behind(wx * c, 1) + wy * ahead(c, 0) + behind(wy * c, 0)
+        return c, total + self.wz[p] * q[p + 1] + self.wz[p - 1] * q[p - 1]
+
+    def residual(self, q, rhs, p):
+        c, near = self.near(q, p)
+        return c, rhs[p] + near - self.diag[p] * c
 
     def first(self, rhs, out, lo, hi, unroll=10):
         def plane(p):
@@ -99,16 +102,16 @@
 
     def sweep(self, q, rhs, out, lo, hi, unroll=10):
         def plane(p):
-            c, applied = self.apply(q, p)
-            out[p] = c + self.inv[p] * (rhs[p] - applied)
+            c, near = self.near(q, p)
+            out[p] = (1.0 - RELAXATION) * c + self.inv[p] * (rhs[p] + near)
 
         planes(lo, hi, plane, unroll)
 
     def halved_residual(self, q, rhs, out, lo, hi, unroll=4):
         def pair(j):
-            _, one = self.apply(q, lo + 2 * j)
-            _, two = self.apply(q, lo + 2 * j + 1)
-            out[j] = (rhs[lo + 2 * j] - one) + (rhs[lo + 2 * j + 1] - two)
+            _, one = self.residual(q, rhs, lo + 2 * j)
+            _, two = self.residual(q, rhs, lo + 2 * j + 1)
+            out[j] = one + two
 
         planes(0, (hi - lo) // 2, pair, unroll)
 
@@ -151,7 +154,8 @@
 
 
 def pack_x_kernel(source, fraction, s, f, to_left, to_right, sems):
-    for copy in copies(((source, s), (fraction, f)), sems):
+    quarters = [slice(4 * k, 4 * k + 4) for k in range(4)]
+    for copy in copies([(a.at[k], b.at[k]) for a, b in ((source, s), (fraction, f)) for k in quarters], sems):
         copy.wait()
     lane = index_of((16, 128), 1)
     for z in range(8):
@@ -195,96 +199,154 @@
                 out[k, j, 24:32, :] = y_high[k, z] * high
 
 
-def down_kernel(s, f, halo, y_low, y_high, z_low, z_high, *refs):
-    kept, own1, f1, F1 = refs[:7], refs[7], refs[8], refs[9]
-    F, Q, T, U, V, S, D0, *w0, sems = refs[10:]
-    iz, iy = lax.axis_index("gz"), lax.axis_index("gy")
-    nz, ny = lax.axis_size("gz"), lax.axis_size("gy")
+def put(S, F, z0, y0, depth, height, scale, plane):
+    edge = index_of((height, 128), 1)
+    edge = (edge < 32) | (edge >= 96)
+
+    def body(k):
+        a, b, h = plane(k)
+        if scale is not None:
+            a, b, h = a * scale, b * scale, h * scale
+        rows = pl.ds(y0, height)
+        S[z0 + k, rows, 0:128] = a
+        F[z0 + k, rows, 0:128] = b
+        S[z0 + k, rows, 128:256] = jnp.where(edge, h, 0.0)
+        F[z0 + k, rows, 128:256] = jnp.where(edge, turn(h, 64, 1), 0.0)
+
+    planes(0, depth, body, 4)
+
+
+SOURCE, DIAG, WEIGHTS, RESULT = (0, 1), (1, 2), (2, 6), (6, 7)
+INNER = {SOURCE: ((8, 24),), DIAG: ((9, 23),), WEIGHTS: ((9, 23),), RESULT: ((10, 22),)}
+OUTER = {
+    SOURCE: ((6, 8), (24, 26)),
+    DIAG: ((8, 9), (23, 24)),
+    WEIGHTS: ((5, 9), (23, 27)),
+    RESULT: ((5, 10), (22, 27)),
+}
+
+
+def layers_of(source, target, spans, which):
+    return [
+        (source.at[a:b, lo:hi], target.at[a:b, lo:hi]) for a, b in which for lo, hi in spans[(a, b)]
+    ]
+
+
+def split(fine):
+    return fine.at[0], fine.at[6], [fine.at[k] for k in (2, 3, 4, 1, 5)]
+
+
+def coarse_rows(T, U, V, count):
+    for j in range(count):
+        for half in range(2):
+            lanes = slice(128 * half, 128 * half + 128)
+            V[j, half] = T[j, :, lanes]
+            U[j, :, lanes] = V[j, half, pl.ds(0, 16, 2), :] + V[j, half, pl.ds(1, 16, 2), :]
+    return matmul(rows_of(U, count), gather_pairs(256, 128, 0, 0, 128)).reshape(count, 16, 128)
+
+
+def inner_kernel(s, f, halo, y_low, y_high, *refs):
+    fine, F, Q, f1, F1, kept, T, U, V, sems = refs
+    S, D0, w0 = split(fine)
+    iy, ny = lax.axis_index("gy"), lax.axis_size("gy")
+    put(S, F, 8, 8, 16, 16, None, lambda k: (s[k], f[k], halo[k]))
+    for ref, y0, okay in ((y_low, 0, iy > 0), (y_high, 24, iy < ny - 1)):
+        put(S, F, 8, y0, 16, 8, inside(okay), lambda k, ref=ref: (ref[0, k], ref[1, k], ref[2, k]))
+    level = Level(w0)
+    level.build(F, 1.0, 9, 23, (False, False), 7)
+    level.first(S, Q, 9, 23, 14)
+    level.sweep(Q, S, D0, 10, 22, 6)
+    started = copies(layers_of(fine, kept, INNER, INNER), sems)
+    level.halved_residual(D0, S, T, 12, 20)
+    halved(F, T.at[4:12], 8, 24)
+    both = coarse_rows(T, U, V, 12)
+    f1[5:9] = both[0:4]
+    F1[3:11] = both[4:12]
+    for copy in started:
+        copy.wait()
+
+
+def down_kernel(z_low, z_high, *refs):
+    fine, F, Q, f1, F1, kept, own1, payload = refs[5:13]
+    T, U, V, V1, q1, d1, *w1, sems = refs[13:]
+    S, D0, w0 = split(fine)
+    iz, nz = lax.axis_index("gz"), lax.axis_size("gz")
     for p in (0, 31):
         S[p] = jnp.zeros((32, 256), F32)
         F[p] = jnp.zeros((32, 256), F32)
-
-    def put(z0, y0, depth, height, scale, plane):
-        edge = index_of((height, 128), 1)
-        edge = (edge < 32) | (edge >= 96)
-
-        def body(k):
-            a, b, h = plane(k)
-            if scale is not None:
-                a, b, h = a * scale, b * scale, h * scale
-            rows = pl.ds(y0, height)
-            S[z0 + k, rows, 0:128] = a
-            F[z0 + k, rows, 0:128] = b
-            S[z0 + k, rows, 128:256] = jnp.where(edge, h, 0.0)
-            F[z0 + k, rows, 128:256] = jnp.where(edge, turn(h, 64, 1), 0.0)
-
-        planes(0, depth, body, 4)
-
-    put(8, 8, 16, 16, None, lambda k: (s[k], f[k], halo[k]))
-    for ref, y0, okay in ((y_low, 0, iy > 0), (y_high, 24, iy < ny - 1)):
-        put(8, y0, 16, 8, inside(okay), lambda k, ref=ref: (ref[0, k], ref[1, k], ref[2, k]))
     for ref, z0, okay in ((z_low, 1, iz > 0), (z_high, 24, iz < nz - 1)):
-        put(z0, 0, 7, 32, inside(okay), lambda k, ref=ref: (ref[0, k], ref[1, k], ref[2, k]))
-
-    started = copies(((S.at[5:27], kept[0].at[5:27]),), sems)
+        put(S, F, z0, 0, 7, 32, inside(okay), lambda k, ref=ref: (ref[0, k], ref[1, k], ref[2, k]))
+
     level = Level(w0)
-    level.build(F, 1.0, 2, 30, (False, False))
-    started += copies(tuple((a.at[5:27], b.at[5:27]) for a, b in zip(w0, kept[2:])), sems.at[1:6])
-    level.first(S, Q, 2, 30)
-    level.sweep(Q, S, D0, 3, 29)
-    started += copies(((D0.at[5:27], kept[1].at[5:27]),), sems.at[6:7])
-    level.halved_residual(D0, S, T, 4, 28)
-    C = gather_pairs(256, 128, 0, 0, 128)
-
-    def coarse(count, out, start):
-        for j in range(count):
-            for half in range(2):
-                lanes = slice(128 * half, 128 * half + 128)
-                V[j, half] = T[j, :, lanes]
-                U[j, :, lanes] = V[j, half, pl.ds(0, 16, 2), :] + V[j, half, pl.ds(1, 16, 2), :]
-        out[start : start + count] = matmul(rows_of(U, count), C).reshape(count, 16, 128)
-
-    coarse(12, f1, 1)
-    halved(F, T, 2, 30)
-    coarse(14, F1, 0)
+    for lo, hi in ((2, 9), (23, 30)):
+        level.build(F, 1.0, lo, hi, (False, False), 7)
+        level.first(S, Q, lo, hi, 7)
+    started = copies(layers_of(fine, kept, OUTER, (SOURCE, DIAG, WEIGHTS)), sems)
+    level.sweep(Q, S, D0, 3, 10, 7)
+    level.sweep(Q, S, D0, 22, 29, 7)
+    started += copies(layers_of(fine, kept, OUTER, (RESULT,)), sems.at[6:8])
+    level.halved_residual(D0, S, T, 4, 12)
+    level.halved_residual(D0, S, T.at[4:8], 20, 28)
+    halved(F, T.at[8:11], 2, 8)
+    halved(F, T.at[11:14], 24, 30)
+    both = coarse_rows(T, U, V, 14)
+    f1[1:5] = both[0:4]
+    f1[9:13] = both[4:8]
+    F1[0:3] = both[8:11]
+    F1[11:14] = both[11:14]
     for j in range(8):
         own1[j] = f1[3 + j, 4:12, :]
         own1[8 + j] = F1[3 + j, 4:12, :]
-    for copy in started:
-        copy.wait()
-
-
-def down_one_kernel(f1, F1, payload, V, q1, d1, *w1):
+
     level = Level(w1)
     level.build(F1, 0.25, 1, 13, (False, False))
     level.first(f1, q1, 1, 13)
     level.sweep(q1, f1, d1, 2, 12)
-    level.halved_residual(d1, f1, V, 3, 11)
-    first = matmul(rows_of(V, 4), gather_pairs(128, 128, 112, 0, 48))
-    halved(F1, V, 3, 11)
-    both = first + matmul(rows_of(V, 4), gather_pairs(128, 128, 112, 64, 48))
-    V[0:4] = both.reshape(4, 16, 128)
+    level.halved_residual(d1, f1, V1, 3, 11)
+    first = matmul(rows_of(V1, 4), gather_pairs(128, 128, 112, 0, 48))
+    halved(F1, V1, 3, 11)
+    both = first + matmul(rows_of(V1, 4), gather_pairs(128, 128, 112, 64, 48))
+    V1[0:4] = both.reshape(4, 16, 128)
     for j in range(4):
-        rows = V[j, pl.ds(4, 4, 2), :] + V[j, pl.ds(5, 4, 2), :]
+        rows = V1[j, pl.ds(4, 4, 2), :] + V1[j, pl.ds(5, 4, 2), :]
         for d in range(32):
             payload[d, 4 * j : 4 * j + 4, :] = rows
-
-
-def spread_y_kernel(own, y_low, y_high, to_low, to_high):
+    for copy in started:
+        copy.wait()
+
+
+def spread_y_kernel(own, y_low, y_high, to_low, to_high, rows):
     iy, ny = lax.axis_index("gy"), lax.axis_size("gy")
     low, high = inside(iy > 0), inside(iy < ny - 1)
-    for out, start in ((to_low, 0), (to_high, 2)):
+    for out, start, depth in ((to_low, 0, 6), (to_high, 2, 6), (rows, 0, 8)):
         for k in range(2):
-            for j in range(6):
-                at, z = (6 * k + j) * 3, 8 * k + start + j
+            for j in range(depth):
+                at, z = (depth * k + j) * 3, 8 * k + start + j
                 out[at] = y_low[z] * low
                 out[at + 1] = own[z]
                 out[at + 2] = y_high[z] * high
 
 
-def middle_kernel(got, own, y_low, y_high, payload, f2h, F2h, d2h, own_h, y_low_h, y_high_h, *refs):
+def wide_kernel(rows, z_low, z_high, f1, d1, *refs):
+    w1, F1, q1 = refs[:5], refs[5], refs[6]
+    iz, nz = lax.axis_index("gz"), lax.axis_size("gz")
+    under, over = inside(iz > 0), inside(iz < nz - 1)
+    for k, ref in enumerate((f1, F1)):
+        for t in range(3):
+            at = slice(8 * t, 8 * t + 8)
+            for z in range(8):
+                ref[8 + z, at, :] = rows[(8 * k + z) * 3 + t]
+            for j in range(6):
+                ref[2 + j, at, :] = z_low[(6 * k + j) * 3 + t] * under
+                ref[16 + j, at, :] = z_high[(6 * k + j) * 3 + t] * over
+    one = Level(w1)
+    one.build(F1, 0.25, 3, 21, (False, False), 9)
+    one.first(f1, q1, 3, 21, 18)
+    one.sweep(q1, f1, d1, 4, 20, 8)
+
+
+def middle_kernel(got, after, payload, f2h, F2h, d2h, *refs):
     f2, F2, d2, q2, T, U, *w2, sems = refs
-    started = copies(((own, own_h), (y_low, y_low_h), (y_high, y_high_h)), sems)
     keep = index_of((16, 128), 1) < 48
     zero = jnp.zeros((16, 128), F32)
     for ref in (f2, F2, q2, d2):
@@ -297,12 +359,12 @@
             for j in range(4):
                 f2[1 + gz * 4 + j, 4 * gy : 4 * gy + 4, :] = rhs[4 * j : 4 * j + 4]
                 F2[1 + gz * 4 + j, 4 * gy : 4 * gy + 4, :] = frac[4 * j : 4 * j + 4]
-    started += copies(((f2, f2h), (F2, F2h)), sems.at[3:5])
+    started = copies(((f2, f2h), (F2, F2h)), sems)
     level = Level(w2)
     level.build(F2, 0.25**2, 1, 33, (True, False), 16)
     level.first(f2, q2, 1, 33, 16)
     level.sweep(q2, f2, d2, 1, 33, 16)
-    started += copies(((d2, d2h),), sems.at[5:6])
+    started += copies(((d2, d2h),), sems.at[2:3])
     C = gather_pairs(128, 128, 8, 0, 16)
     for field in range(2):
         if field == 0:
@@ -394,26 +456,25 @@
 
 
 def up_kernel(got, *refs):
-    far, refs = refs[:15], refs[15:]
+    f1, qb1, *w1 = refs[:7]
+    refs = refs[7:]
+    far, refs = refs[:5], refs[5:]
     pressure, residual, refs = refs[0], refs[1], refs[2:]
-    near, sems = refs[:15], refs[15]
+    near, sems = refs[:4], refs[4]
     iz, iy, ix = lax.axis_index("gz"), lax.axis_index("gy"), lax.axis_index("gx")
     nz, ny = lax.axis_size("gz"), lax.axis_size("gy")
     start = jnp.clip(4 * iz - 4, 0, 20)
 
-    def part(a, b):
-        if b.shape == BIG:
-            return a.at[5:27], b.at[5:27]
-        if b.shape == WINDOW:
-            return a.at[pl.ds(start, 14)], b
-        return a, b
-
-    started = copies(tuple(part(a, b) for a, b in zip(far, near)), sems)
-    own1, y_low, y_high, z_low, z_high, f2, F2, d2, S, D0, wx0, wy0, wz0, g0, i0 = near
-    refs = refs[16:]
+    pairs = [(a.at[pl.ds(start, 14)], b) for a, b in zip(far[:3], near)]
+    for which in ((WEIGHTS, RESULT, SOURCE), (DIAG,)):
+        pairs += layers_of(far[3], near[3], INNER, which) + layers_of(far[4], near[3], OUTER, which)
+    started = copies(pairs, sems)
+    f2, F2, d2, fine = near
+    S, D0, w0 = split(fine)
+    refs = refs[5:]
     f3, F3, q3, d3, f4, F4, q4, d4 = refs[:8]
-    w3, w4, w2, w1 = refs[8:13], refs[13:18], refs[18:23], refs[23:28]
-    T3, g5, F5, qa2, qb2, T2, T2y, f1, F1, qa1, qb1, T1, U1, T0, U0, qa0, qb0, kept_p, kept_r, out_sems = refs[28:]
+    w3, w4, w2 = refs[8:13], refs[13:18], refs[18:23]
+    T3, g5, F5, qa2, qb2, T2, T2y, qa1, qc1, T1, U1, T0, U0, qa0, qb0, kept_p, kept_r, out_sems = refs[23:]
     lane = index_of((8, 128), 1)
     row = index_of((8, 128), 0)
     zero = jnp.zeros((8, 128), F32)
@@ -484,7 +545,7 @@
     three.sweep(q3, f3, d3, 1, 17, 16)
     three.sweep(d3, f3, q3, 1, 17, 16)
 
-    for copy in started[5:8]:
+    for copy in started[:3]:
         copy.wait()
     two = Level(w2)
     two.build(F2, 0.25**2, 1, 13, (True, False), 12)
@@ -507,23 +568,7 @@
     two.sweep(qa2, f2, qb2, 1, 13, 12)
     two.sweep(qb2, f2, qa2, 1, 13, 12)
 
-    for copy in started[:5]:
-        copy.wait()
-    low, high, under, over = inside(iy > 0), inside(iy < ny - 1), inside(iz > 0), inside(iz < nz - 1)
-    for k, ref in enumerate((f1, F1)):
-        for z in range(8):
-            ref[8 + z, 0:8, :] = y_low[8 * k + z] * low
-            ref[8 + z, 8:16, :] = own1[8 * k + z]
-            ref[8 + z, 16:24, :] = y_high[8 * k + z] * high
-        for j in range(6):
-            for t in range(3):
-                at = (6 * k + j) * 3 + t
-                ref[2 + j, 8 * t : 8 * t + 8, :] = z_low[at] * under
-                ref[16 + j, 8 * t : 8 * t + 8, :] = z_high[at] * over
     one = Level(w1)
-    one.build(F1, 0.25, 3, 21, (False, False))
-    one.first(f1, qa1, 3, 21)
-    one.sweep(qa1, f1, qb1, 4, 20)
     shift = jnp.remainder(4 - 4 * iy, 16)
     for j in range(8):
         at = jnp.clip(4 * iz - 2 + j, 0, 31) - start
@@ -536,13 +581,13 @@
         plane = T1[j]
         for k in (0, 1):
             p = 4 + 2 * j + k
-            qa1[p] = qb1[p] + jnp.where(F1[p] > 0.0, plane, 0.0)
-    one.sweep(qa1, f1, qb1, 5, 19)
-    one.sweep(qb1, f1, qa1, 6, 18)
-
-    for copy in started[8:]:
+            qa1[p] = qb1[p] + jnp.where(one.inv[p] > 0.0, plane, 0.0)
+    one.sweep(qa1, f1, qc1, 5, 19, 7)
+    one.sweep(qc1, f1, qa1, 6, 18, 6)
+
+    for copy in started[3:12]:
         copy.wait()
-    zero_level = Level((wx0, wy0, wz0, g0, i0))
+    zero_level = Level(w0)
     T0[...] = matmul(qa1[6:18].reshape(288, 128), spread_pairs(128, 256, 0, 0, 128)).reshape(12, 24, 256)
 
     def refine(j):
@@ -553,17 +598,19 @@
         plane = jnp.concatenate([U0[0, j], U0[1, j]], axis=1)
         for k in (0, 1):
             p = 4 + 2 * j + k
-            qa0[p] = D0[p] + jnp.where(i0[p] > 0.0, plane, 0.0)
+            qa0[p] = D0[p] + jnp.where(zero_level.inv[p] > 0.0, plane, 0.0)
 
     planes(0, 12, refine, 4)
     zero_level.sweep(qa0, S, qb0, 6, 26)
     zero_level.sweep(qb0, S, qa0, 7, 25)
 
     def finish(p):
-        c, applied = zero_level.apply(qa0, p)
+        c, rest = zero_level.residual(qa0, S, p)
         kept_p[p - 8] = c[8:24, 0:128]
-        kept_r[p - 8] = (S[p] - applied)[8:24, 0:128]
-
+        kept_r[p - 8] = rest[8:24, 0:128]
+
+    for copy in started[12:]:
+        copy.wait()
     started = []
     for k in (0, 8):
         planes(8 + k, 16 + k, finish, 8)
@@ -574,7 +621,7 @@
         copy.wait()
 
 
-def call(kernel, name, ins, outs, scratch=()):
+def call(kernel, name, ins, outs, scratch=(), aliases=()):
     anywhere = pl.BlockSpec(memory_space=pl.ANY)
     spec = {"v": pl.BlockSpec(memory_space=pltpu.VMEM), "n": pl.BlockSpec(memory_space=pltpu.VMEM), "h": anywhere}
     kind = {"v": pltpu.VMEM, "h": pltpu.HBM, "n": jax.ShapeDtypeStruct}
@@ -589,6 +636,7 @@
             out_specs=[spec[k] for k, _ in outs],
             scratch_shapes=[pltpu.VMEM(shape, F32) if isinstance(shape, tuple) else shape for shape in scratch],
             compiler_params=pltpu.CompilerParams(vmem_limit_bytes=VMEM_LIMIT),
+            input_output_aliases=dict(aliases),
             name=name,
         )(*args)
 
@@ -604,7 +652,7 @@
     return lax.ppermute(to_high, axis, ring(axis, reach)), lax.ppermute(to_low, axis, ring(axis, -reach))
 
 
-BIG, MID, MID2, WIDE1 = (32, 32, 256), (14, 16, 128), (34, 16, 128), (24, 24, 128)
+FINE, BIG, MID, MID2, WIDE1 = (7, 32, 32, 256), (32, 32, 256), (14, 16, 128), (34, 16, 128), (24, 24, 128)
 WINDOW = (14, 16, 128)
 THREE, FOUR = (18, 8, 128), (10, 8, 128)
 
@@ -615,62 +663,67 @@
 
     own, strip = (16, 16, 128), (8, 16, 128)
     s, f, to_left, to_right = call(
-        pack_x_kernel, "pack_x", "hh", [("v", own)] * 2 + [("v", strip)] * 2, [dma(2)]
+        pack_x_kernel, "pack_x", "hh", [("v", own)] * 2 + [("v", strip)] * 2, [dma(8)]
     )(source, fraction)
     from_left, from_right = exchange(to_left, to_right, "gx")
     rows = (3, 16, 8, 128)
     halo, to_low, to_high = call(pack_y_kernel, "pack_y", "vvvv", [("v", own), ("v", rows), ("v", rows)])(
         s, f, from_right, from_left
     )
-    y_low, y_high = exchange(to_low, to_high, "gy")
+    y_halos = exchange(to_low, to_high, "gy")
     layers = (3, 7, 32, 128)
-    to_low, to_high = call(pack_z_kernel, "pack_z", "vvvvv", [("v", layers)] * 2)(s, f, halo, y_low, y_high)
+    to_low, to_high = call(pack_z_kernel, "pack_z", "vvvvv", [("v", layers)] * 2)(s, f, halo, *y_halos)
     z_low, z_high = exchange(to_low, to_high, "gz")
-    *fine, own1, f1, F1 = call(
+    coarse = [(14, 32, 256), (14, 16, 256), (14, 2, 32, 128)]
+    *inner, fine_inner = call(
+        inner_kernel,
+        "inner",
+        "vvvvv",
+        [("v", FINE), ("v", BIG), ("v", BIG), ("v", MID), ("v", MID), ("h", FINE)],
+        [*coarse, dma(4)],
+    )(s, f, halo, *y_halos)
+    fine, own1, payload = call(
         down_kernel,
         "down",
-        "vvvvvvv",
-        [("h", BIG)] * 7 + [("v", (16, 8, 128)), ("v", MID), ("v", MID)],
-        [BIG, BIG, (14, 32, 256), (14, 16, 256), (14, 2, 32, 128)] + [BIG] * 7 + [dma(7)],
-    )(s, f, halo, y_low, y_high, z_low, z_high)
+        "v" * 7,
+        [("v", FINE), ("v", BIG), ("v", BIG), ("v", MID), ("v", MID), ("h", FINE)]
+        + [("v", (16, 8, 128)), ("v", (32, 16, 128))],
+        [*coarse, (4, 16, 128)] + [MID] * 7 + [dma(8)],
+        [(2 + i, i) for i in range(5)],
+    )(z_low, z_high, *inner)[5:]
     y_low, y_high = exchange(own1, own1, "gy")
-    (payload,) = call(
-        down_one_kernel, "down_one", "vv", [("v", (32, 16, 128))], [(4, 16, 128)] + [MID] * 7
-    )(f1, F1)
     got = lax.all_to_all(payload, ("gy", "gz"), 0, 0)
     layers = (36, 8, 128)
-    to_low, to_high = call(spread_y_kernel, "spread_y", "vvv", [("v", layers)] * 2)(own1, y_low, y_high)
+    to_low, to_high, rows = call(
+        spread_y_kernel, "spread_y", "vvv", [("v", layers)] * 2 + [("v", (48, 8, 128))]
+    )(own1, y_low, y_high)
     z_low, z_high = exchange(to_low, to_high, "gz")
+    one = call(wide_kernel, "wide", "vvv", [("v", WIDE1)] * 7, [WIDE1] * 2)(rows, z_low, z_high)
     payload, *kept = call(
         middle_kernel,
         "middle",
-        "vvvv",
-        [("v", (8, 4, 8, 128))] + [("h", MID2)] * 3 + [("h", (16, 8, 128))] * 3,
-        [MID2] * 4 + [(16, 16, 128), (16, 16, 128)] + [MID2] * 5 + [dma(6)],
-    )(got, own1, y_low, y_high)
+        "vv",
+        [("v", (8, 4, 8, 128))] + [("h", MID2)] * 3,
+        [MID2] * 4 + [(16, 16, 128), (16, 16, 128)] + [MID2] * 5 + [dma(3)],
+    )(got, rows)
     got = lax.all_to_all(payload, "gx", 0, 0)
-    f2, F2, d2, own1, y_low, y_high = kept
-    kept = [own1, y_low, y_high, z_low, z_high, f2, F2, d2, *fine]
     pressure, residual = call(
         up_kernel,
         "up",
-        "v" + "h" * 15,
+        "v" * 8 + "h" * 5,
         [("h", own)] * 2,
-        [(16, 8, 128)] * 3
-        + [layers] * 2
-        + [WINDOW] * 3
-        + [BIG] * 7
+        [WINDOW] * 3
+        + [FINE]
         + [dma(15)]
         + [THREE] * 4
         + [FOUR] * 4
         + [THREE] * 5
         + [FOUR] * 5
         + [WINDOW] * 5
-        + [WIDE1] * 5
         + [(9, 8, 128), (8, 128), (8, 128), WINDOW, WINDOW, (2, 6, 8, 128), (6, 16, 128)]
-        + [WIDE1] * 4
+        + [WIDE1] * 2
         + [(8, 24, 128), (8, 16, 128), (12, 24, 256), (2, 12, 32, 128), BIG, BIG, own, own, dma(4)],
-    )(got, *kept)
+    )(got, *one, *kept, fine_inner, fine)
     return (pressure, residual)
 
 

time: 75.6 us -> 72.8 us (0.963)
  waiting for transfers between devices: 29.2 us -> 24.9 us
  Pallas kernels: 17.6 us -> 18.9 us
    ppermute x5, waiting for transfers between devices: 17.2 us -> 9.94 us  [exchange(): lax.ppermute(to_high, axis, ring(axis, reach))]
    ppermute x5, waiting for transfers between devices: 6.57 us -> 10.3 us  [exchange(): lax.ppermute(to_low, axis, ring(axis, -reach))]
    pallas_call x8 -> x9, Pallas kernels: 17.6 us -> 18.9 us  [run(): pl.pallas_call(kernel, out_shape=[kind[k](shape, F32) for k, shape in out...]
    ppermute x5, starting transfers between devices: 9.41 us -> 10.7 us  [exchange(): lax.ppermute(to_low, axis, ring(axis, -reach))]
    ppermute x5, starting transfers between devices: 7.88 us -> 6.71 us  [exchange(): lax.ppermute(to_high, axis, ring(axis, reach))]
    all_to_all x1, waiting for transfers between devices: 3.9 us -> 3.02 us  [local(): got = lax.all_to_all(payload, 'gx', 0, 0)]
  transfers between devices with their start and end apart: 12 -> 12, of which waited for: 10 -> 11; matrix products, arithmetic and copies ran while one was open for 0% -> 0% of each run, Pallas kernels for 0% -> 6%
where the time goes in v4:
time: 72.8 us; the launch traced here: 72.5 us
  starting transfers between devices  27.8 us (38%)
  waiting for transfers between devices  24.9 us (34%)
  Pallas kernels  18.9 us (26%)
  between operations  0.87 us (1%)
    pallas_call x9, Pallas kernels, run(): pl.pallas_call(kernel, out_shape=[kind[k](shape, F32) for k, shape in out...  18.9 us
    ppermute x5, starting transfers between devices, exchange(): lax.ppermute(to_low, axis, ring(axis, -reach))  10.7 us
    ppermute x5, waiting for transfers between devices, exchange(): lax.ppermute(to_low, axis, ring(axis, -reach))  10.3 us
    ppermute x5, waiting for transfers between devices, exchange(): lax.ppermute(to_high, axis, ring(axis, reach))  9.94 us
    all_to_all x1, starting transfers between devices, local(): got = lax.all_to_all(payload, ('gy', 'gz'), 0, 0)  6.85 us
    ppermute x5, starting transfers between devices, exchange(): lax.ppermute(to_high, axis, ring(axis, reach))  6.71 us
    all_to_all x1, starting transfers between devices, local(): got = lax.all_to_all(payload, 'gx', 0, 0)  3.56 us
    all_to_all x1, waiting for transfers between devices, local(): got = lax.all_to_all(payload, 'gx', 0, 0)  3.02 us
  transfers between devices with their start and end apart: 12, of which 11 were waited for; matrix products, arithmetic and copies ran while one was open for 0% of the time, Pallas kernels for 6%

profile of v4, /device:TPU:1, one launch (start us, length us, event | category | flops | bytes accessed | tf_op | source)
XLA Modules:
  0.0 72.5 jit_solution(5081615465415498946)
XLA Ops:
  0.6 1.1 %pack_x.1 = (f32[16,16,128]{2,1,0:T(8,128)S(1)}, f32[16,16,128]{2,1,0:T(8,128)S(1)}, f32[8,16,128]{2,1,0:T(8,128)S(1)}, f32[8,16,128]{2,1,0:T(8,128)S(1)}) custom-call(f32[16,16,128]{2,1,0:T(8,128)} %source.1, f32[16,16,128]{2,1,0:T(8,128)} %fraction.1), custom_call_target="tpu_custom_call" | custom-call | tf_op jit(solution)/shard_map/pack_x/pallas_call | solution.py:632
  1.7 6.5 %collective-permute-start = (f32[8,16,128]{2,1,0:T(8,128)S(1)}, f32[8,16,128]{2,1,0:T(8,128)S(1)}, u32[]{:S(2)}, u32[]{:S(2)}) collective-permute-start(f32[8,16,128]{2,1,0:T(8,128)S(1)} %get-tuple-element.36), channel_id=1, source_target_pairs={{0,224},{32,0},{64,32},{96,64},{128,96},{160,128},{192,160},{224,1... | collective-permute-start | bytes 196616 | tf_op jit(solution)/shard_map/ppermute | solution.py:652
  8.2 0.0 collective-permute-start.1
  8.2 1.3 %collective-permute-done.from_right = f32[8,16,128]{2,1,0:T(8,128)S(1)} collective-permute-done((f32[8,16,128]{2,1,0:T(8,128)S(1)}, f32[8,16,128]{2,1,0:T(8,128)S(1)}, u32[]{:S(2)}, u32[]{:S(2)}) %collective-permute-start) | collective-permute-done | bytes 65568 | tf_op jit(solution)/shard_map/ppermute | solution.py:652
  9.5 3.0 %collective-permute-done.1.from_left = f32[8,16,128]{2,1,0:T(8,128)S(1)} collective-permute-done((f32[8,16,128]{2,1,0:T(8,128)S(1)}, f32[8,16,128]{2,1,0:T(8,128)S(1)}, u32[]{:S(2)}, u32[]{:S(2)}) %collective-permute-start.1) | collective-permute-done | bytes 65568 | tf_op jit(solution)/shard_map/ppermute | solution.py:652
  12.5 0.1 pack_y.1
  12.7 1.3 %collective-permute-start.2 = (f32[3,16,8,128]{3,2,1,0:T(8,128)S(1)}, f32[3,16,8,128]{3,2,1,0:T(8,128)S(1)}, u32[]{:S(2)}, u32[]{:S(2)}) collective-permute-start(f32[3,16,8,128]{3,2,1,0:T(8,128)S(1)} %get-tuple-element.39), channel_id=1, source_target_pairs={{0,8},{8,16},{16,24},{24,0},{1,9},{9,17},{17,25},{25,1},{2,10},{10... | collective-permute-start | bytes 589832 | tf_op jit(solution)/shard_map/ppermute | solution.py:652
  14.0 1.5 %collective-permute-start.3 = (f32[3,16,8,128]{3,2,1,0:T(8,128)S(1)}, f32[3,16,8,128]{3,2,1,0:T(8,128)S(1)}, u32[]{:S(2)}, u32[]{:S(2)}) collective-permute-start(f32[3,16,8,128]{3,2,1,0:T(8,128)S(1)} %get-tuple-element.40), channel_id=1, source_target_pairs={{0,24},{8,0},{16,8},{24,16},{1,25},{9,1},{17,9},{25,17},{2,26},{10... | collective-permute-start | bytes 589832 | tf_op jit(solution)/shard_map/ppermute | solution.py:652
  15.4 3.1 %collective-permute-done.2.y_low = f32[3,16,8,128]{3,2,1,0:T(8,128)S(1)} collective-permute-done((f32[3,16,8,128]{3,2,1,0:T(8,128)S(1)}, f32[3,16,8,128]{3,2,1,0:T(8,128)S(1)}, u32[]{:S(2)}, u32[]{:S(2)}) %collective-permute-start.2) | collective-permute-done | bytes 196640 | tf_op jit(solution)/shard_map/ppermute | solution.py:652
  18.5 0.0 collective-permute-done.3.y_high
  18.5 4.7 %collective-permute-start.4 = (f32[3,7,32,128]{3,2,1,0:T(8,128)S(1)}, f32[3,7,32,128]{3,2,1,0:T(8,128)S(1)}, u32[]{:S(2)}, u32[]{:S(2)}) collective-permute-start(f32[3,7,32,128]{3,2,1,0:T(8,128)S(1)} %get-tuple-element.41), channel_id=1, source_target_pairs={{0,1},{1,2},{2,3},{3,4},{4,5},{5,6},{6,7},{7,0},{8,9},{9,10},{10,1... | collective-permute-start | bytes 1032200 | tf_op jit(solution)/shard_map/ppermute | solution.py:652
  23.3 0.0 collective-permute-start.5
  23.3 3.5 %inner.1 = (f32[7,32,32,256]{3,2,1,0:T(8,128)S(1)}, f32[32,32,256]{2,1,0:T(8,128)S(1)}, f32[32,32,256]{2,1,0:T(8,128)S(1)}, f32[14,16,128]{2,1,0:T(8,128)S(1)}, ...) custom-call(f32[16,16,128]{2,1,0:T(8,128)S(1)} %get-tuple-element.34.s, f32[16,16,128]{2,1,0:T(8,128)S(1)} %get-tuple-element.35.f, ...), custom_call_target="tpu_custom_call" | custom-call | tf_op jit(solution)/shard_map/inner/pallas_call | solution.py:632
  26.8 0.7 collective-permute-done.4.z_low
  27.5 2.5 %collective-permute-done.5.z_high = f32[3,7,32,128]{3,2,1,0:T(8,128)S(1)} collective-permute-done((f32[3,7,32,128]{3,2,1,0:T(8,128)S(1)}, f32[3,7,32,128]{3,2,1,0:T(8,128)S(1)}, u32[]{:S(2)}, u32[]{:S(2)}) %collective-permute-start.5) | collective-permute-done | bytes 344096 | tf_op jit(solution)/shard_map/ppermute | solution.py:652
  29.9 2.9 %down.1 = (f32[7,32,32,256]{3,2,1,0:T(8,128)S(1)}, f32[32,32,256]{2,1,0:T(8,128)S(1)}, f32[32,32,256]{2,1,0:T(8,128)S(1)}, f32[14,16,128]{2,1,0:T(8,128)S(1)}, f...) custom-call(f32[3,7,32,128]{3,2,1,0:T(8,128)S(1)} %collective-permut, ...), custom_call_target="tpu_custom_call", output_to_operand_aliasing={{0}: (2, {}), {1}: (3, {}), {2}: (4, {}), {3}: (5, {}), {4}... | custom-call | tf_op jit(solution)/shard_map/down/pallas_call | solution.py:632
  32.8 6.9 %all-to-all-start = ((f32[32,16,128]{2,1,0:T(8,128)}), f32[32,16,128]{2,1,0:T(8,128)S(1)}, u32[]{:S(2)}, u32[]{:S(2)}) async-start(f32[32,16,128]{2,1,0:T(8,128)} %get-tuple-element.48), calls=%async_computation | async-start | bytes 524288 | tf_op jit(solution)/shard_map/all_to_all | solution.py:695
  39.7 2.7 %collective-permute-start.7 = (f32[16,8,128]{2,1,0:T(8,128)S(1)}, f32[16,8,128]{2,1,0:T(8,128)S(1)}, u32[]{:S(2)}, u32[]{:S(2)}) collective-permute-start(f32[16,8,128]{2,1,0:T(8,128)S(1)} %get-tuple-element.49.own), channel_id=1, source_target_pairs={{0,24},{8,0},{16,8},{24,16},{1,25},{9,1},{17,9},{25,17},{2,26},{10... | collective-permute-start | bytes 196616 | tf_op jit(solution)/shard_map/ppermute | solution.py:652
  42.4 0.0 collective-permute-start.6
  42.4 3.7 %collective-permute-done.7.y_high = f32[16,8,128]{2,1,0:T(8,128)S(1)} collective-permute-done((f32[16,8,128]{2,1,0:T(8,128)S(1)}, f32[16,8,128]{2,1,0:T(8,128)S(1)}, u32[]{:S(2)}, u32[]{:S(2)}) %collective-permute-start.7) | collective-permute-done | bytes 65568 | tf_op jit(solution)/shard_map/ppermute | solution.py:652
  46.1 1.1 %collective-permute-done.6.y_low = f32[16,8,128]{2,1,0:T(8,128)S(1)} collective-permute-done((f32[16,8,128]{2,1,0:T(8,128)S(1)}, f32[16,8,128]{2,1,0:T(8,128)S(1)}, u32[]{:S(2)}, u32[]{:S(2)}) %collective-permute-start.6) | collective-permute-done | bytes 65568 | tf_op jit(solution)/shard_map/ppermute | solution.py:652
  47.3 1.6 %all-to-all-done.got = f32[32,16,128]{2,1,0:T(8,128)S(1)} async-done(((f32[32,16,128]{2,1,0:T(8,128)}), f32[32,16,128]{2,1,0:T(8,128)S(1)}, u32[]{:S(2)}, u32[]{:S(2)}) %all-to-all-start) | async-done | bytes 262176 | tf_op jit(solution)/shard_map/all_to_all | solution.py:695
  49.0 2.6 %middle.1 = (f32[8,4,8,128]{3,2,1,0:T(8,128)}, f32[34,16,128]{2,1,0:T(8,128)}, f32[34,16,128]{2,1,0:T(8,128)}, f32[34,16,128]{2,1,0:T(8,128)}) custom-call(f32[32,16,128]{2,1,0:T(8,128)S(1)} %all-to-all-done.got, f32[48,8,128]{2,1,0:T(8,128)S(1)} %get-tuple-element.50.after.rows), custom_call_target="tpu_custom_call" | custom-call | tf_op jit(solution)/shard_map/middle/pallas_call | solution.py:632
  51.6 3.6 %all-to-all-start.1 = ((f32[8,4,8,128]{3,2,1,0:T(8,128)}), f32[8,4,8,128]{3,2,1,0:T(8,128)S(1)}, u32[]{:S(2)}, u32[]{:S(2)}) async-start(f32[8,4,8,128]{3,2,1,0:T(8,128)} %get-tuple-element.51), calls=%async_computation.1 | async-start | bytes 262144 | tf_op jit(solution)/shard_map/all_to_all | solution.py:709
  55.1 0.7 collective-permute-start.8
  55.8 0.0 collective-permute-start.9
  55.8 2.1 %collective-permute-done.8.z_low = f32[36,8,128]{2,1,0:T(8,128)S(1)} collective-permute-done((f32[36,8,128]{2,1,0:T(8,128)S(1)}, f32[36,8,128]{2,1,0:T(8,128)S(1)}, u32[]{:S(2)}, u32[]{:S(2)}) %collective-permute-start.8) | collective-permute-done | bytes 147488 | tf_op jit(solution)/shard_map/ppermute | solution.py:652
  57.9 2.8 %collective-permute-done.9.z_high = f32[36,8,128]{2,1,0:T(8,128)S(1)} collective-permute-done((f32[36,8,128]{2,1,0:T(8,128)S(1)}, f32[36,8,128]{2,1,0:T(8,128)S(1)}, u32[]{:S(2)}, u32[]{:S(2)}) %collective-permute-start.9) | collective-permute-done | bytes 147488 | tf_op jit(solution)/shard_map/ppermute | solution.py:652
  60.7 0.6 wide.1
  61.3 3.0 %all-to-all-done.1.got = f32[8,4,8,128]{3,2,1,0:T(8,128)S(1)} async-done(((f32[8,4,8,128]{3,2,1,0:T(8,128)}), f32[8,4,8,128]{3,2,1,0:T(8,128)S(1)}, u32[]{:S(2)}, u32[]{:S(2)}) %all-to-all-start.1) | async-done | bytes 131104 | tf_op jit(solution)/shard_map/all_to_all | solution.py:709
  64.3 8.0 %up.1 = (f32[16,16,128]{2,1,0:T(8,128)}, f32[16,16,128]{2,1,0:T(8,128)}) custom-call(f32[8,4,8,128]{3,2,1,0:T(8,128)S(1)} %all-to-all-done.1.got, f32[24,24,128]{2,1,0:T(8,128)S(1)} %get-tuple-element.54.refs_0_, f32[24,24,128]{2,1,0:T(8,128)S(1)} %get-tuple-element.55.refs_1_, f32[24,24,128]{2,1,0:T(8,128)S(1)} %get-tuple-element.56.refs_2_, ...), custom_call_target="tpu_custom_call" | custom-call | tf_op jit(solution)/shard_map/up/pallas_call | solution.py:632
  (2 shorter events, 0.1 us)
Async XLA Ops:
  1.7 7.8 %collective-permute-start = (f32[8,16,128]{2,1,0:T(8,128)S(1)}, f32[8,16,128]{2,1,0:T(8,128)S(1)}, u32[]{:S(2)}, u32[]{:S(2)}) collective-permute-start(f32[8,16,128]{2,1,0:T(8,128)S(1)} %get-tuple-element.36), channel_id=1, source_target_pairs={{0,224},{32,0},{64,32},{96,64},{128,96},{160,128},{192,160},{224,1... | collective-permute-start | bytes 196616 | tf_op jit(solution)/shard_map/ppermute | solution.py:652
  8.2 4.3 %collective-permute-start.1 = (f32[8,16,128]{2,1,0:T(8,128)S(1)}, f32[8,16,128]{2,1,0:T(8,128)S(1)}, u32[]{:S(2)}, u32[]{:S(2)}) collective-permute-start(f32[8,16,128]{2,1,0:T(8,128)S(1)} %get-tuple-element.37), channel_id=1, source_target_pairs={{0,32},{32,64},{64,96},{96,128},{128,160},{160,192},{192,224},{224... | collective-permute-start | bytes 196616 | tf_op jit(solution)/shard_map/ppermute | solution.py:652
  12.7 5.8 %collective-permute-start.2 = (f32[3,16,8,128]{3,2,1,0:T(8,128)S(1)}, f32[3,16,8,128]{3,2,1,0:T(8,128)S(1)}, u32[]{:S(2)}, u32[]{:S(2)}) collective-permute-start(f32[3,16,8,128]{3,2,1,0:T(8,128)S(1)} %get-tuple-element.39), channel_id=1, source_target_pairs={{0,8},{8,16},{16,24},{24,0},{1,9},{9,17},{17,25},{25,1},{2,10},{10... | collective-permute-start | bytes 589832 | tf_op jit(solution)/shard_map/ppermute | solution.py:652
  14.0 4.5 %collective-permute-start.3 = (f32[3,16,8,128]{3,2,1,0:T(8,128)S(1)}, f32[3,16,8,128]{3,2,1,0:T(8,128)S(1)}, u32[]{:S(2)}, u32[]{:S(2)}) collective-permute-start(f32[3,16,8,128]{3,2,1,0:T(8,128)S(1)} %get-tuple-element.40), channel_id=1, source_target_pairs={{0,24},{8,0},{16,8},{24,16},{1,25},{9,1},{17,9},{25,17},{2,26},{10... | collective-permute-start | bytes 589832 | tf_op jit(solution)/shard_map/ppermute | solution.py:652
  18.5 8.9 %collective-permute-start.4 = (f32[3,7,32,128]{3,2,1,0:T(8,128)S(1)}, f32[3,7,32,128]{3,2,1,0:T(8,128)S(1)}, u32[]{:S(2)}, u32[]{:S(2)}) collective-permute-start(f32[3,7,32,128]{3,2,1,0:T(8,128)S(1)} %get-tuple-element.41), channel_id=1, source_target_pairs={{0,1},{1,2},{2,3},{3,4},{4,5},{5,6},{6,7},{7,0},{8,9},{9,10},{10,1... | collective-permute-start | bytes 1032200 | tf_op jit(solution)/shard_map/ppermute | solution.py:652
  23.3 6.7 %collective-permute-start.5 = (f32[3,7,32,128]{3,2,1,0:T(8,128)S(1)}, f32[3,7,32,128]{3,2,1,0:T(8,128)S(1)}, u32[]{:S(2)}, u32[]{:S(2)}) collective-permute-start(f32[3,7,32,128]{3,2,1,0:T(8,128)S(1)} %get-tuple-element.42), channel_id=1, source_target_pairs={{0,7},{1,0},{2,1},{3,2},{4,3},{5,4},{6,5},{7,6},{8,15},{9,8},{10,9... | collective-permute-start | bytes 1032200 | tf_op jit(solution)/shard_map/ppermute | solution.py:652
  32.8 16.1 %all-to-all-start = ((f32[32,16,128]{2,1,0:T(8,128)}), f32[32,16,128]{2,1,0:T(8,128)S(1)}, u32[]{:S(2)}, u32[]{:S(2)}) async-start(f32[32,16,128]{2,1,0:T(8,128)} %get-tuple-element.48), calls=%async_computation | async-start | bytes 524288 | tf_op jit(solution)/shard_map/all_to_all | solution.py:695
  39.7 6.5 %collective-permute-start.7 = (f32[16,8,128]{2,1,0:T(8,128)S(1)}, f32[16,8,128]{2,1,0:T(8,128)S(1)}, u32[]{:S(2)}, u32[]{:S(2)}) collective-permute-start(f32[16,8,128]{2,1,0:T(8,128)S(1)} %get-tuple-element.49.own), channel_id=1, source_target_pairs={{0,24},{8,0},{16,8},{24,16},{1,25},{9,1},{17,9},{25,17},{2,26},{10... | collective-permute-start | bytes 196616 | tf_op jit(solution)/shard_map/ppermute | solution.py:652
  42.4 4.9 %collective-permute-start.6 = (f32[16,8,128]{2,1,0:T(8,128)S(1)}, f32[16,8,128]{2,1,0:T(8,128)S(1)}, u32[]{:S(2)}, u32[]{:S(2)}) collective-permute-start(f32[16,8,128]{2,1,0:T(8,128)S(1)} %get-tuple-element.49.own), channel_id=1, source_target_pairs={{0,8},{8,16},{16,24},{24,0},{1,9},{9,17},{17,25},{25,1},{2,10},{10... | collective-permute-start | bytes 196616 | tf_op jit(solution)/shard_map/ppermute | solution.py:652
  51.6 12.8 %all-to-all-start.1 = ((f32[8,4,8,128]{3,2,1,0:T(8,128)}), f32[8,4,8,128]{3,2,1,0:T(8,128)S(1)}, u32[]{:S(2)}, u32[]{:S(2)}) async-start(f32[8,4,8,128]{3,2,1,0:T(8,128)} %get-tuple-element.51), calls=%async_computation.1 | async-start | bytes 262144 | tf_op jit(solution)/shard_map/all_to_all | solution.py:709
  55.1 2.8 %collective-permute-start.8 = (f32[36,8,128]{2,1,0:T(8,128)S(1)}, f32[36,8,128]{2,1,0:T(8,128)S(1)}, u32[]{:S(2)}, u32[]{:S(2)}) collective-permute-start(f32[36,8,128]{2,1,0:T(8,128)S(1)} %get-tuple-element.52), channel_id=1, source_target_pairs={{0,1},{1,2},{2,3},{3,4},{4,5},{5,6},{6,7},{7,0},{8,9},{9,10},{10,1... | collective-permute-start | bytes 442376 | tf_op jit(solution)/shard_map/ppermute | solution.py:652
  55.8 4.9 %collective-permute-start.9 = (f32[36,8,128]{2,1,0:T(8,128)S(1)}, f32[36,8,128]{2,1,0:T(8,128)S(1)}, u32[]{:S(2)}, u32[]{:S(2)}) collective-permute-start(f32[36,8,128]{2,1,0:T(8,128)S(1)} %get-tuple-element.53), channel_id=1, source_target_pairs={{0,7},{1,0},{2,1},{3,2},{4,3},{5,4},{6,5},{7,6},{8,15},{9,8},{10,9... | collective-permute-start | bytes 442376 | tf_op jit(solution)/shard_map/ppermute | solution.py:652

commit v5 on v4

--- a/solution.py
+++ b/solution.py
@@ -172,6 +172,35 @@
         )
 
 
+ROWS = (6, 7, 7)
+ROWS_ONE = (5, 6)
+
+
+def tiles_of(rows, own):
+    return [
+        (k, depth, t)
+        for k in range(len(rows))
+        for depth in range(1, rows[k] + 1)
+        for t in range(own + 2)
+        if 0 < t <= own or depth < rows[k]
+    ]
+
+
+TILES, TILES_ONE = tiles_of(ROWS, 2), tiles_of(ROWS_ONE, 1)
+
+
+def unpack_y(message, out, rows, low):
+    at = 0
+    for k, count in enumerate(rows):
+        for j in range(8):
+            source = j - (8 - count) if low else j
+            if 0 <= source < count:
+                out[k, :, j, :] = message[at + source]
+            else:
+                out[k, :, j, :] = jnp.zeros(message.shape[1:], F32)
+        at += count
+
+
 def pack_y_kernel(s, f, from_right, from_left, halo, to_low, to_high):
     ix = lax.axis_index("gx")
     left = inside(ix > 0)
@@ -182,21 +211,27 @@
         r, l = from_right[z] * right, from_left[z] * left
         halo[z] = jnp.where(is_right, r, l)
         halo[z + 8] = jnp.where(is_right, turn(r, 96, 1), turn(l, 32, 1))
-    for k, ref in enumerate((s, f, halo)):
-        to_low[k] = ref[:, 0:8, :]
-        to_high[k] = ref[:, 8:16, :]
-
-
-def pack_z_kernel(s, f, halo, y_low, y_high, to_low, to_high):
+    at = 0
+    for count, ref in zip(ROWS, (s, f, halo)):
+        for j in range(count):
+            to_low[at + j] = ref[:, j, :]
+            to_high[at + j] = ref[:, 16 - count + j, :]
+        at += count
+
+
+def pack_z_kernel(s, f, halo, from_low, from_high, to_low, to_high, y_low, y_high):
+    unpack_y(from_low, y_low, ROWS, True)
+    unpack_y(from_high, y_high, ROWS, False)
     iy, ny = lax.axis_index("gy"), lax.axis_size("gy")
     low, high = inside(iy > 0), inside(iy < ny - 1)
-    for out, start in ((to_low, 0), (to_high, 9)):
-        for k, ref in enumerate((s, f, halo)):
-            for j in range(7):
-                z = start + j
-                out[k, j, 0:8, :] = y_low[k, z] * low
-                out[k, j, 8:24, :] = ref[z]
-                out[k, j, 24:32, :] = y_high[k, z] * high
+    for i, (k, depth, t) in enumerate(TILES):
+        for out, z in ((to_low, depth - 1), (to_high, 16 - depth)):
+            if t == 0:
+                out[i] = y_low[k, z] * low
+            elif t == 3:
+                out[i] = y_high[k, z] * high
+            else:
+                out[i] = (s, f, halo)[k][z, 8 * t - 8 : 8 * t, :]
 
 
 def put(S, F, z0, y0, depth, height, scale, plane):
@@ -216,12 +251,13 @@
     planes(0, depth, body, 4)
 
 
-SOURCE, DIAG, WEIGHTS, RESULT = (0, 1), (1, 2), (2, 6), (6, 7)
-INNER = {SOURCE: ((8, 24),), DIAG: ((9, 23),), WEIGHTS: ((9, 23),), RESULT: ((10, 22),)}
+SOURCE, DIAG, WEIGHTS, INVERSE, RESULT = (0, 1), (1, 2), (2, 5), (5, 6), (6, 7)
+INNER = {SOURCE: ((8, 24),), DIAG: ((9, 23),), WEIGHTS: ((9, 23),), INVERSE: ((9, 23),), RESULT: ((10, 22),)}
 OUTER = {
     SOURCE: ((6, 8), (24, 26)),
     DIAG: ((8, 9), (23, 24)),
-    WEIGHTS: ((5, 9), (23, 27)),
+    WEIGHTS: ((5, 9), (23, 26)),
+    INVERSE: ((5, 9), (23, 27)),
     RESULT: ((5, 10), (22, 27)),
 }
 
@@ -245,8 +281,10 @@
     return matmul(rows_of(U, count), gather_pairs(256, 128, 0, 0, 128)).reshape(count, 16, 128)
 
 
-def inner_kernel(s, f, halo, y_low, y_high, *refs):
-    fine, F, Q, f1, F1, kept, T, U, V, sems = refs
+def inner_kernel(s, f, halo, from_low, from_high, *refs):
+    fine, F, Q, f1, F1, kept, T, U, V, y_low, y_high, sems = refs
+    unpack_y(from_low, y_low, ROWS, True)
+    unpack_y(from_high, y_high, ROWS, False)
     S, D0, w0 = split(fine)
     iy, ny = lax.axis_index("gy"), lax.axis_size("gy")
     put(S, F, 8, 8, 16, 16, None, lambda k: (s[k], f[k], halo[k]))
@@ -267,24 +305,30 @@
 
 
 def down_kernel(z_low, z_high, *refs):
-    fine, F, Q, f1, F1, kept, own1, payload = refs[5:13]
-    T, U, V, V1, q1, d1, *w1, sems = refs[13:]
+    fine, F, Q, f1, F1, kept, own1, to_low, to_high, payload = refs[5:15]
+    T, U, V, V1, q1, d1, *w1, sems = refs[15:]
     S, D0, w0 = split(fine)
     iz, nz = lax.axis_index("gz"), lax.axis_size("gz")
     for p in (0, 31):
         S[p] = jnp.zeros((32, 256), F32)
         F[p] = jnp.zeros((32, 256), F32)
+    zero = jnp.zeros((8, 128), F32)
+
+    def layer(ref, depth):
+        tiles = [[ref[TILES.index((k, depth, t))] if (k, depth, t) in TILES else zero for t in range(4)] for k in range(3)]
+        return [jnp.concatenate(four, axis=0) for four in tiles]
+
     for ref, z0, okay in ((z_low, 1, iz > 0), (z_high, 24, iz < nz - 1)):
-        put(S, F, z0, 0, 7, 32, inside(okay), lambda k, ref=ref: (ref[0, k], ref[1, k], ref[2, k]))
+        put(S, F, z0, 0, 7, 32, inside(okay), lambda k, ref=ref, z0=z0: layer(ref, 7 - k if z0 == 1 else 1 + k))
 
     level = Level(w0)
     for lo, hi in ((2, 9), (23, 30)):
         level.build(F, 1.0, lo, hi, (False, False), 7)
         level.first(S, Q, lo, hi, 7)
-    started = copies(layers_of(fine, kept, OUTER, (SOURCE, DIAG, WEIGHTS)), sems)
+    started = copies(layers_of(fine, kept, OUTER, (SOURCE, DIAG, WEIGHTS, INVERSE)), sems)
     level.sweep(Q, S, D0, 3, 10, 7)
     level.sweep(Q, S, D0, 22, 29, 7)
-    started += copies(layers_of(fine, kept, OUTER, (RESULT,)), sems.at[6:8])
+    started += copies(layers_of(fine, kept, OUTER, (RESULT,)), sems.at[8:10])
     level.halved_residual(D0, S, T, 4, 12)
     level.halved_residual(D0, S, T.at[4:8], 20, 28)
     halved(F, T.at[8:11], 2, 8)
@@ -297,6 +341,12 @@
     for j in range(8):
         own1[j] = f1[3 + j, 4:12, :]
         own1[8 + j] = F1[3 + j, 4:12, :]
+    at = 0
+    for ref, count in zip((f1, F1), ROWS_ONE):
+        for j in range(count):
+            to_low[at + j] = ref[3:11, 4 + j, :]
+            to_high[at + j] = ref[3:11, 12 - count + j, :]
+        at += count
 
     level = Level(w1)
     level.build(F1, 0.25, 1, 13, (False, False))
@@ -315,37 +365,49 @@
         copy.wait()
 
 
-def spread_y_kernel(own, y_low, y_high, to_low, to_high, rows):
+def spread_y_kernel(own, from_low, from_high, to_low, to_high, rows, y_low, y_high):
+    unpack_y(from_low, y_low, ROWS_ONE, True)
+    unpack_y(from_high, y_high, ROWS_ONE, False)
     iy, ny = lax.axis_index("gy"), lax.axis_size("gy")
     low, high = inside(iy > 0), inside(iy < ny - 1)
-    for out, start, depth in ((to_low, 0, 6), (to_high, 2, 6), (rows, 0, 8)):
-        for k in range(2):
-            for j in range(depth):
-                at, z = (depth * k + j) * 3, 8 * k + start + j
-                out[at] = y_low[z] * low
-                out[at + 1] = own[z]
-                out[at + 2] = y_high[z] * high
+    for k in range(2):
+        for z in range(8):
+            at = (8 * k + z) * 3
+            rows[at] = y_low[k, z] * low
+            rows[at + 1] = own[8 * k + z]
+            rows[at + 2] = y_high[k, z] * high
+    for i, (k, depth, t) in enumerate(TILES_ONE):
+        to_low[i] = rows[(8 * k + depth - 1) * 3 + t]
+        to_high[i] = rows[(8 * k + 8 - depth) * 3 + t]
 
 
 def wide_kernel(rows, z_low, z_high, f1, d1, *refs):
     w1, F1, q1 = refs[:5], refs[5], refs[6]
     iz, nz = lax.axis_index("gz"), lax.axis_size("gz")
     under, over = inside(iz > 0), inside(iz < nz - 1)
+    zero = jnp.zeros((8, 128), F32)
     for k, ref in enumerate((f1, F1)):
         for t in range(3):
             at = slice(8 * t, 8 * t + 8)
             for z in range(8):
                 ref[8 + z, at, :] = rows[(8 * k + z) * 3 + t]
-            for j in range(6):
-                ref[2 + j, at, :] = z_low[(6 * k + j) * 3 + t] * under
-                ref[16 + j, at, :] = z_high[(6 * k + j) * 3 + t] * over
+            for depth in range(1, 7):
+                there = (k, depth, t) in TILES_ONE
+                i = TILES_ONE.index((k, depth, t)) if there else 0
+                ref[8 - depth, at, :] = z_low[i] * under if there else zero
+                ref[15 + depth, at, :] = z_high[i] * over if there else zero
     one = Level(w1)
     one.build(F1, 0.25, 3, 21, (False, False), 9)
     one.first(f1, q1, 3, 21, 18)
     one.sweep(q1, f1, d1, 4, 20, 8)
 
 
+def window_start():
+    return jnp.clip(4 * lax.axis_index("gz") - 4, 0, 20)
+
+
 def middle_kernel(got, after, payload, f2h, F2h, d2h, *refs):
+    *refs, part, part_sems = refs
     f2, F2, d2, q2, T, U, *w2, sems = refs
     keep = index_of((16, 128), 1) < 48
     zero = jnp.zeros((16, 128), F32)
@@ -359,28 +421,32 @@
             for j in range(4):
                 f2[1 + gz * 4 + j, 4 * gy : 4 * gy + 4, :] = rhs[4 * j : 4 * j + 4]
                 F2[1 + gz * 4 + j, 4 * gy : 4 * gy + 4, :] = frac[4 * j : 4 * j + 4]
-    started = copies(((f2, f2h), (F2, F2h)), sems)
+    at = pl.ds(window_start(), 14)
+    started = copies(((f2.at[at], f2h), (F2.at[at], F2h)), sems)
     level = Level(w2)
-    level.build(F2, 0.25**2, 1, 33, (True, False), 16)
-    level.first(f2, q2, 1, 33, 16)
-    level.sweep(q2, f2, d2, 1, 33, 16)
-    started += copies(((d2, d2h),), sems.at[2:3])
     C = gather_pairs(128, 128, 8, 0, 16)
-    for field in range(2):
-        if field == 0:
-            level.halved_residual(d2, f2, T, 1, 33, 2)
-        else:
-            halved(F2, T, 1, 33)
+
+    def send(field):
         U[...] = matmul(rows_of(T, 16), C).reshape(16, 16, 128)
         for zh in range(2):
             total = None
             for zl in range(8):
                 z = zh * 8 + zl
-                part = U[z, pl.ds(0, 8, 2), :] + U[z, pl.ds(1, 8, 2), :]
-                part = turn(part, 16 * zl, 1)
-                total = part if total is None else total + part
-            for d in range(8):
-                payload[d, 2 * field + zh] = total
+                rows = U[z, pl.ds(0, 8, 2), :] + U[z, pl.ds(1, 8, 2), :]
+                rows = turn(rows, 16 * zl, 1)
+                total = rows if total is None else total + rows
+            part[2 * field + zh] = total
+        at = slice(2 * field, 2 * field + 2)
+        return copies([(part.at[at], payload.at[d, at]) for d in range(8)], part_sems.at[8 * field : 8 * field + 8])
+
+    halved(F2, T, 1, 33)
+    started += send(1)
+    level.build(F2, 0.25**2, 1, 33, (True, False), 16)
+    level.first(f2, q2, 1, 33, 16)
+    level.sweep(q2, f2, d2, 1, 33, 16)
+    started += copies(((d2.at[at], d2h),), sems.at[2:3])
+    level.halved_residual(d2, f2, T, 1, 33, 8)
+    started += send(0)
     for copy in started:
         copy.wait()
 
@@ -436,7 +502,7 @@
         nA, nC, nD, ng = [], [], [], []
         for i in range(8):
             d, a, c, r = D[i], None, None, g[i]
-            for k in range(8):
+            for k in (i,) if step == 1 else range(8):
                 pa, pc = pick(A[i], k), pick(C[i], k)
                 d = d - (pa * Yl[k] + pc * Xr[k])
                 r = r - (pa * hl[k] + pc * hr[k])
@@ -463,10 +529,9 @@
     near, sems = refs[:4], refs[4]
     iz, iy, ix = lax.axis_index("gz"), lax.axis_index("gy"), lax.axis_index("gx")
     nz, ny = lax.axis_size("gz"), lax.axis_size("gy")
-    start = jnp.clip(4 * iz - 4, 0, 20)
-
-    pairs = [(a.at[pl.ds(start, 14)], b) for a, b in zip(far[:3], near)]
-    for which in ((WEIGHTS, RESULT, SOURCE), (DIAG,)):
+    start = window_start()
+    pairs = list(zip(far[:3], near))
+    for which in ((RESULT, INVERSE), (WEIGHTS, SOURCE), (DIAG,)):
         pairs += layers_of(far[3], near[3], INNER, which) + layers_of(far[4], near[3], OUTER, which)
     started = copies(pairs, sems)
     f2, F2, d2, fine = near
@@ -585,8 +650,6 @@
     one.sweep(qa1, f1, qc1, 5, 19, 7)
     one.sweep(qc1, f1, qa1, 6, 18, 6)
 
-    for copy in started[3:12]:
-        copy.wait()
     zero_level = Level(w0)
     T0[...] = matmul(qa1[6:18].reshape(288, 128), spread_pairs(128, 256, 0, 0, 128)).reshape(12, 24, 256)
 
@@ -600,7 +663,11 @@
             p = 4 + 2 * j + k
             qa0[p] = D0[p] + jnp.where(zero_level.inv[p] > 0.0, plane, 0.0)
 
+    for copy in started[3:9]:
+        copy.wait()
     planes(0, 12, refine, 4)
+    for copy in started[9:15]:
+        copy.wait()
     zero_level.sweep(qa0, S, qb0, 6, 26)
     zero_level.sweep(qb0, S, qa0, 7, 25)
 
@@ -609,7 +676,7 @@
         kept_p[p - 8] = c[8:24, 0:128]
         kept_r[p - 8] = rest[8:24, 0:128]
 
-    for copy in started[12:]:
+    for copy in started[15:]:
         copy.wait()
     started = []
     for k in (0, 8):
@@ -666,13 +733,15 @@
         pack_x_kernel, "pack_x", "hh", [("v", own)] * 2 + [("v", strip)] * 2, [dma(8)]
     )(source, fraction)
     from_left, from_right = exchange(to_left, to_right, "gx")
-    rows = (3, 16, 8, 128)
+    rows = (sum(ROWS), 16, 128)
     halo, to_low, to_high = call(pack_y_kernel, "pack_y", "vvvv", [("v", own), ("v", rows), ("v", rows)])(
         s, f, from_right, from_left
     )
     y_halos = exchange(to_low, to_high, "gy")
-    layers = (3, 7, 32, 128)
-    to_low, to_high = call(pack_z_kernel, "pack_z", "vvvvv", [("v", layers)] * 2)(s, f, halo, *y_halos)
+    layers = (len(TILES), 8, 128)
+    to_low, to_high = call(pack_z_kernel, "pack_z", "vvvvv", [("v", layers)] * 2, [(3, 16, 8, 128)] * 2)(
+        s, f, halo, *y_halos
+    )
     z_low, z_high = exchange(to_low, to_high, "gz")
     coarse = [(14, 32, 256), (14, 16, 256), (14, 2, 32, 128)]
     *inner, fine_inner = call(
@@ -680,22 +749,27 @@
         "inner",
         "vvvvv",
         [("v", FINE), ("v", BIG), ("v", BIG), ("v", MID), ("v", MID), ("h", FINE)],
-        [*coarse, dma(4)],
+        [*coarse, (3, 16, 8, 128), (3, 16, 8, 128), dma(5)],
     )(s, f, halo, *y_halos)
-    fine, own1, payload = call(
+    rows = (sum(ROWS_ONE), 8, 128)
+    fine, own1, to_low, to_high, payload = call(
         down_kernel,
         "down",
         "v" * 7,
         [("v", FINE), ("v", BIG), ("v", BIG), ("v", MID), ("v", MID), ("h", FINE)]
-        + [("v", (16, 8, 128)), ("v", (32, 16, 128))],
-        [*coarse, (4, 16, 128)] + [MID] * 7 + [dma(8)],
+        + [("v", (16, 8, 128)), ("v", rows), ("v", rows), ("v", (32, 16, 128))],
+        [*coarse, (4, 16, 128)] + [MID] * 7 + [dma(10)],
         [(2 + i, i) for i in range(5)],
     )(z_low, z_high, *inner)[5:]
-    y_low, y_high = exchange(own1, own1, "gy")
+    y_low, y_high = exchange(to_low, to_high, "gy")
     got = lax.all_to_all(payload, ("gy", "gz"), 0, 0)
-    layers = (36, 8, 128)
+    layers = (len(TILES_ONE), 8, 128)
     to_low, to_high, rows = call(
-        spread_y_kernel, "spread_y", "vvv", [("v", layers)] * 2 + [("v", (48, 8, 128))]
+        spread_y_kernel,
+        "spread_y",
+        "vvv",
+        [("v", layers)] * 2 + [("v", (48, 8, 128))],
+        [(2, 8, 8, 128)] * 2,
     )(own1, y_low, y_high)
     z_low, z_high = exchange(to_low, to_high, "gz")
     one = call(wide_kernel, "wide", "vvv", [("v", WIDE1)] * 7, [WIDE1] * 2)(rows, z_low, z_high)
@@ -703,8 +777,8 @@
         middle_kernel,
         "middle",
         "vv",
-        [("v", (8, 4, 8, 128))] + [("h", MID2)] * 3,
-        [MID2] * 4 + [(16, 16, 128), (16, 16, 128)] + [MID2] * 5 + [dma(3)],
+        [("h", (8, 4, 8, 128))] + [("h", WINDOW)] * 3,
+        [MID2] * 4 + [(16, 16, 128), (16, 16, 128)] + [MID2] * 5 + [dma(3), (4, 8, 128), dma(16)],
     )(got, rows)
     got = lax.all_to_all(payload, "gx", 0, 0)
     pressure, residual = call(
@@ -714,7 +788,7 @@
         [("h", own)] * 2,
         [WINDOW] * 3
         + [FINE]
-        + [dma(15)]
+        + [dma(18)]
         + [THREE] * 4
         + [FOUR] * 4
         + [THREE] * 5

time: 72.8 us -> 71.6 us (0.984)
  waiting for transfers between devices: 24.9 us -> 23.9 us
    ppermute x5, waiting for transfers between devices: 10.3 us -> 6.53 us  [exchange(): lax.ppermute(to_low, axis, ring(axis, -reach))]
    ppermute x5, waiting for transfers between devices: 9.94 us -> 11.5 us  [exchange(): lax.ppermute(to_high, axis, ring(axis, reach))]
    all_to_all x1, waiting for transfers between devices: 3.02 us -> 3.96 us  [local(): got = lax.all_to_all(payload, 'gx', 0, 0)]
    ppermute x5, starting transfers between devices: 10.7 us -> 9.74 us  [exchange(): lax.ppermute(to_low, axis, ring(axis, -reach))]
    ppermute x5, starting transfers between devices: 6.71 us -> 7.56 us  [exchange(): lax.ppermute(to_high, axis, ring(axis, reach))]
  transfers between devices with their start and end apart: 12 -> 12, of which waited for: 11 -> 9; matrix products, arithmetic and copies ran while one was open for 0% -> 0% of each run, Pallas kernels for 6% -> 6%
where the time goes in v5:
time: 71.6 us; the launch traced here: 71.3 us
  starting transfers between devices  27.7 us (39%)
  waiting for transfers between devices  23.9 us (33%)
  Pallas kernels  18.8 us (26%)
  between operations  0.88 us (1%)
    pallas_call x9, Pallas kernels, run(): pl.pallas_call(kernel, out_shape=[kind[k](shape, F32) for k, shape in out...  18.8 us
    ppermute x5, waiting for transfers between devices, exchange(): lax.ppermute(to_high, axis, ring(axis, reach))  11.5 us
    ppermute x5, starting transfers between devices, exchange(): lax.ppermute(to_low, axis, ring(axis, -reach))  9.74 us
    ppermute x5, starting transfers between devices, exchange(): lax.ppermute(to_high, axis, ring(axis, reach))  7.56 us
    all_to_all x1, starting transfers between devices, local(): got = lax.all_to_all(payload, ('gy', 'gz'), 0, 0)  6.85 us
    ppermute x5, waiting for transfers between devices, exchange(): lax.ppermute(to_low, axis, ring(axis, -reach))  6.53 us
    all_to_all x1, waiting for transfers between devices, local(): got = lax.all_to_all(payload, 'gx', 0, 0)  3.96 us
    all_to_all x1, starting transfers between devices, local(): got = lax.all_to_all(payload, 'gx', 0, 0)  3.56 us
  transfers between devices with their start and end apart: 12, of which 9 were waited for; matrix products, arithmetic and copies ran while one was open for 0% of the time, Pallas kernels for 6%

profile of v5, /device:TPU:1, one launch (start us, length us, event | category | flops | bytes accessed | tf_op | source)
XLA Modules:
  0.0 71.3 jit_solution(8812527101814378026)
XLA Ops:
  0.6 1.1 %pack_x.1 = (f32[16,16,128]{2,1,0:T(8,128)S(1)}, f32[16,16,128]{2,1,0:T(8,128)S(1)}, f32[8,16,128]{2,1,0:T(8,128)S(1)}, f32[8,16,128]{2,1,0:T(8,128)S(1)}) custom-call(f32[16,16,128]{2,1,0:T(8,128)} %source.1, f32[16,16,128]{2,1,0:T(8,128)} %fraction.1), custom_call_target="tpu_custom_call" | custom-call | tf_op jit(solution)/shard_map/pack_x/pallas_call | solution.py:699
  1.7 6.5 %collective-permute-start = (f32[8,16,128]{2,1,0:T(8,128)S(1)}, f32[8,16,128]{2,1,0:T(8,128)S(1)}, u32[]{:S(2)}, u32[]{:S(2)}) collective-permute-start(f32[8,16,128]{2,1,0:T(8,128)S(1)} %get-tuple-element.38), channel_id=1, source_target_pairs={{0,224},{32,0},{64,32},{96,64},{128,96},{160,128},{192,160},{224,1... | collective-permute-start | bytes 196616 | tf_op jit(solution)/shard_map/ppermute | solution.py:719
  8.2 0.0 collective-permute-start.1
  8.2 1.3 %collective-permute-done.from_right = f32[8,16,128]{2,1,0:T(8,128)S(1)} collective-permute-done((f32[8,16,128]{2,1,0:T(8,128)S(1)}, f32[8,16,128]{2,1,0:T(8,128)S(1)}, u32[]{:S(2)}, u32[]{:S(2)}) %collective-permute-start) | collective-permute-done | bytes 65568 | tf_op jit(solution)/shard_map/ppermute | solution.py:719
  9.5 3.0 %collective-permute-done.1.from_left = f32[8,16,128]{2,1,0:T(8,128)S(1)} collective-permute-done((f32[8,16,128]{2,1,0:T(8,128)S(1)}, f32[8,16,128]{2,1,0:T(8,128)S(1)}, u32[]{:S(2)}, u32[]{:S(2)}) %collective-permute-start.1) | collective-permute-done | bytes 65568 | tf_op jit(solution)/shard_map/ppermute | solution.py:719
  12.5 0.2 pack_y.1
  12.7 1.3 %collective-permute-start.2 = (f32[20,16,128]{2,1,0:T(8,128)S(1)}, f32[20,16,128]{2,1,0:T(8,128)S(1)}, u32[]{:S(2)}, u32[]{:S(2)}) collective-permute-start(f32[20,16,128]{2,1,0:T(8,128)S(1)} %get-tuple-element.41), channel_id=1, source_target_pairs={{0,8},{8,16},{16,24},{24,0},{1,9},{9,17},{17,25},{25,1},{2,10},{10... | collective-permute-start | bytes 491528 | tf_op jit(solution)/shard_map/ppermute | solution.py:719
  14.0 1.5 %collective-permute-start.3 = (f32[20,16,128]{2,1,0:T(8,128)S(1)}, f32[20,16,128]{2,1,0:T(8,128)S(1)}, u32[]{:S(2)}, u32[]{:S(2)}) collective-permute-start(f32[20,16,128]{2,1,0:T(8,128)S(1)} %get-tuple-element.42), channel_id=1, source_target_pairs={{0,24},{8,0},{16,8},{24,16},{1,25},{9,1},{17,9},{25,17},{2,26},{10... | collective-permute-start | bytes 491528 | tf_op jit(solution)/shard_map/ppermute | solution.py:719
  15.5 2.7 %collective-permute-done.2.from_low = f32[20,16,128]{2,1,0:T(8,128)S(1)} collective-permute-done((f32[20,16,128]{2,1,0:T(8,128)S(1)}, f32[20,16,128]{2,1,0:T(8,128)S(1)}, u32[]{:S(2)}, u32[]{:S(2)}) %collective-permute-start.2) | collective-permute-done | bytes 163872 | tf_op jit(solution)/shard_map/ppermute | solution.py:719
  18.2 0.0 collective-permute-done.3.from_high
  18.2 0.2 pack_z.1
  18.4 4.7 %collective-permute-start.4 = (f32[74,8,128]{2,1,0:T(8,128)S(1)}, f32[74,8,128]{2,1,0:T(8,128)S(1)}, u32[]{:S(2)}, u32[]{:S(2)}) collective-permute-start(f32[74,8,128]{2,1,0:T(8,128)S(1)} %get-tuple-element.43), channel_id=1, source_target_pairs={{0,1},{1,2},{2,3},{3,4},{4,5},{5,6},{6,7},{7,0},{8,9},{9,10},{10,1... | collective-permute-start | bytes 909320 | tf_op jit(solution)/shard_map/ppermute | solution.py:719
  23.1 0.0 collective-permute-start.5
  23.1 3.7 %inner.1 = (f32[7,32,32,256]{3,2,1,0:T(8,128)S(1)}, f32[32,32,256]{2,1,0:T(8,128)S(1)}, f32[32,32,256]{2,1,0:T(8,128)S(1)}, f32[14,16,128]{2,1,0:T(8,128)S(1)}, ...) custom-call(f32[16,16,128]{2,1,0:T(8,128)S(1)} %get-tuple-element.36.s, f32[16,16,128]{2,1,0:T(8,128)S(1)} %get-tuple-element.37.f, ...), custom_call_target="tpu_custom_call" | custom-call | tf_op jit(solution)/shard_map/inner/pallas_call | solution.py:699
  26.9 0.0 collective-permute-done.4.z_low
  26.9 2.5 %collective-permute-done.5.z_high = f32[74,8,128]{2,1,0:T(8,128)S(1)} collective-permute-done((f32[74,8,128]{2,1,0:T(8,128)S(1)}, f32[74,8,128]{2,1,0:T(8,128)S(1)}, u32[]{:S(2)}, u32[]{:S(2)}) %collective-permute-start.5) | collective-permute-done | bytes 303136 | tf_op jit(solution)/shard_map/ppermute | solution.py:719
  29.4 3.1 %down.1 = (f32[7,32,32,256]{3,2,1,0:T(8,128)S(1)}, f32[32,32,256]{2,1,0:T(8,128)S(1)}, f32[32,32,256]{2,1,0:T(8,128)S(1)}, f32[14,16,128]{2,1,0:T(8,128)S(1)}, f...) custom-call(f32[74,8,128]{2,1,0:T(8,128)S(1)} %collective-permute-do, ...), custom_call_target="tpu_custom_call", output_to_operand_aliasing={{0}: (2, {}), {1}: (3, {}), {2}: (4, {}), {3}: (5, {}), {4}... | custom-call | tf_op jit(solution)/shard_map/down/pallas_call | solution.py:699
  32.5 6.8 %all-to-all-start = ((f32[32,16,128]{2,1,0:T(8,128)}), f32[32,16,128]{2,1,0:T(8,128)S(1)}, u32[]{:S(2)}, u32[]{:S(2)}) async-start(f32[32,16,128]{2,1,0:T(8,128)} %get-tuple-element.50), calls=%async_computation | async-start | bytes 524288 | tf_op jit(solution)/shard_map/all_to_all | solution.py:765
  39.3 1.5 %collective-permute-start.6 = (f32[11,8,128]{2,1,0:T(8,128)S(1)}, f32[11,8,128]{2,1,0:T(8,128)S(1)}, u32[]{:S(2)}, u32[]{:S(2)}) collective-permute-start(f32[11,8,128]{2,1,0:T(8,128)S(1)} %get-tuple-element.52), channel_id=1, source_target_pairs={{0,8},{8,16},{16,24},{24,0},{1,9},{9,17},{17,25},{25,1},{2,10},{10... | collective-permute-start | bytes 135176 | tf_op jit(solution)/shard_map/ppermute | solution.py:719
  40.8 1.3 %collective-permute-start.7 = (f32[11,8,128]{2,1,0:T(8,128)S(1)}, f32[11,8,128]{2,1,0:T(8,128)S(1)}, u32[]{:S(2)}, u32[]{:S(2)}) collective-permute-start(f32[11,8,128]{2,1,0:T(8,128)S(1)} %get-tuple-element.53), channel_id=1, source_target_pairs={{0,24},{8,0},{16,8},{24,16},{1,25},{9,1},{17,9},{25,17},{2,26},{10... | collective-permute-start | bytes 135176 | tf_op jit(solution)/shard_map/ppermute | solution.py:719
  42.1 4.4 %collective-permute-done.6.from_low = f32[11,8,128]{2,1,0:T(8,128)S(1)} collective-permute-done((f32[11,8,128]{2,1,0:T(8,128)S(1)}, f32[11,8,128]{2,1,0:T(8,128)S(1)}, u32[]{:S(2)}, u32[]{:S(2)}) %collective-permute-start.6) | collective-permute-done | bytes 45088 | tf_op jit(solution)/shard_map/ppermute | solution.py:719
  46.5 0.0 collective-permute-done.7.from_high
  46.5 0.1 spread_y.1
  46.6 2.0 %all-to-all-done.got = f32[32,16,128]{2,1,0:T(8,128)S(1)} async-done(((f32[32,16,128]{2,1,0:T(8,128)}), f32[32,16,128]{2,1,0:T(8,128)S(1)}, u32[]{:S(2)}, u32[]{:S(2)}) %all-to-all-start) | async-done | bytes 262176 | tf_op jit(solution)/shard_map/all_to_all | solution.py:765
  48.6 2.5 %middle.1 = (f32[8,4,8,128]{3,2,1,0:T(8,128)}, f32[14,16,128]{2,1,0:T(8,128)}, f32[14,16,128]{2,1,0:T(8,128)}, f32[14,16,128]{2,1,0:T(8,128)}) custom-call(f32[32,16,128]{2,1,0:T(8,128)S(1)} %all-to-all-done.got, f32[48,8,128]{2,1,0:T(8,128)S(1)} %get-tuple-element.54.after.rows), custom_call_target="tpu_custom_call" | custom-call | tf_op jit(solution)/shard_map/middle/pallas_call | solution.py:699
  51.1 3.6 %all-to-all-start.1 = ((f32[8,4,8,128]{3,2,1,0:T(8,128)}), f32[8,4,8,128]{3,2,1,0:T(8,128)S(1)}, u32[]{:S(2)}, u32[]{:S(2)}) async-start(f32[8,4,8,128]{3,2,1,0:T(8,128)} %get-tuple-element.55), calls=%async_computation.1 | async-start | bytes 262144 | tf_op jit(solution)/shard_map/all_to_all | solution.py:783
  54.7 0.1 collective-permute-start.8
  54.8 0.4 collective-permute-start.9
  55.2 1.4 %collective-permute-done.8.z_low = f32[29,8,128]{2,1,0:T(8,128)S(1)} collective-permute-done((f32[29,8,128]{2,1,0:T(8,128)S(1)}, f32[29,8,128]{2,1,0:T(8,128)S(1)}, u32[]{:S(2)}, u32[]{:S(2)}) %collective-permute-start.8) | collective-permute-done | bytes 118816 | tf_op jit(solution)/shard_map/ppermute | solution.py:719
  56.6 2.7 %collective-permute-done.9.z_high = f32[29,8,128]{2,1,0:T(8,128)S(1)} collective-permute-done((f32[29,8,128]{2,1,0:T(8,128)S(1)}, f32[29,8,128]{2,1,0:T(8,128)S(1)}, u32[]{:S(2)}, u32[]{:S(2)}) %collective-permute-start.9) | collective-permute-done | bytes 118816 | tf_op jit(solution)/shard_map/ppermute | solution.py:719
  59.3 0.6 wide.1
  59.9 4.0 %all-to-all-done.1.got = f32[8,4,8,128]{3,2,1,0:T(8,128)S(1)} async-done(((f32[8,4,8,128]{3,2,1,0:T(8,128)}), f32[8,4,8,128]{3,2,1,0:T(8,128)S(1)}, u32[]{:S(2)}, u32[]{:S(2)}) %all-to-all-start.1) | async-done | bytes 131104 | tf_op jit(solution)/shard_map/all_to_all | solution.py:783
  63.9 7.2 %up.1 = (f32[16,16,128]{2,1,0:T(8,128)}, f32[16,16,128]{2,1,0:T(8,128)}) custom-call(f32[8,4,8,128]{3,2,1,0:T(8,128)S(1)} %all-to-all-done.1.got, f32[24,24,128]{2,1,0:T(8,128)S(1)} %get-tuple-element.58.refs_0_, f32[24,24,128]{2,1,0:T(8,128)S(1)} %get-tuple-element.59.refs_1_, f32[24,24,128]{2,1,0:T(8,128)S(1)} %get-tuple-element.60.refs_2_, ...), custom_call_target="tpu_custom_call" | custom-call | tf_op jit(solution)/shard_map/up/pallas_call | solution.py:699
Async XLA Ops:
  1.7 7.8 %collective-permute-start = (f32[8,16,128]{2,1,0:T(8,128)S(1)}, f32[8,16,128]{2,1,0:T(8,128)S(1)}, u32[]{:S(2)}, u32[]{:S(2)}) collective-permute-start(f32[8,16,128]{2,1,0:T(8,128)S(1)} %get-tuple-element.38), channel_id=1, source_target_pairs={{0,224},{32,0},{64,32},{96,64},{128,96},{160,128},{192,160},{224,1... | collective-permute-start | bytes 196616 | tf_op jit(solution)/shard_map/ppermute | solution.py:719
  8.2 4.3 %collective-permute-start.1 = (f32[8,16,128]{2,1,0:T(8,128)S(1)}, f32[8,16,128]{2,1,0:T(8,128)S(1)}, u32[]{:S(2)}, u32[]{:S(2)}) collective-permute-start(f32[8,16,128]{2,1,0:T(8,128)S(1)} %get-tuple-element.39), channel_id=1, source_target_pairs={{0,32},{32,64},{64,96},{96,128},{128,160},{160,192},{192,224},{224... | collective-permute-start | bytes 196616 | tf_op jit(solution)/shard_map/ppermute | solution.py:719
  12.7 5.5 %collective-permute-start.2 = (f32[20,16,128]{2,1,0:T(8,128)S(1)}, f32[20,16,128]{2,1,0:T(8,128)S(1)}, u32[]{:S(2)}, u32[]{:S(2)}) collective-permute-start(f32[20,16,128]{2,1,0:T(8,128)S(1)} %get-tuple-element.41), channel_id=1, source_target_pairs={{0,8},{8,16},{16,24},{24,0},{1,9},{9,17},{17,25},{25,1},{2,10},{10... | collective-permute-start | bytes 491528 | tf_op jit(solution)/shard_map/ppermute | solution.py:719
  14.0 4.2 %collective-permute-start.3 = (f32[20,16,128]{2,1,0:T(8,128)S(1)}, f32[20,16,128]{2,1,0:T(8,128)S(1)}, u32[]{:S(2)}, u32[]{:S(2)}) collective-permute-start(f32[20,16,128]{2,1,0:T(8,128)S(1)} %get-tuple-element.42), channel_id=1, source_target_pairs={{0,24},{8,0},{16,8},{24,16},{1,25},{9,1},{17,9},{25,17},{2,26},{10... | collective-permute-start | bytes 491528 | tf_op jit(solution)/shard_map/ppermute | solution.py:719
  18.4 8.5 %collective-permute-start.4 = (f32[74,8,128]{2,1,0:T(8,128)S(1)}, f32[74,8,128]{2,1,0:T(8,128)S(1)}, u32[]{:S(2)}, u32[]{:S(2)}) collective-permute-start(f32[74,8,128]{2,1,0:T(8,128)S(1)} %get-tuple-element.43), channel_id=1, source_target_pairs={{0,1},{1,2},{2,3},{3,4},{4,5},{5,6},{6,7},{7,0},{8,9},{9,10},{10,1... | collective-permute-start | bytes 909320 | tf_op jit(solution)/shard_map/ppermute | solution.py:719
  23.1 6.2 %collective-permute-start.5 = (f32[74,8,128]{2,1,0:T(8,128)S(1)}, f32[74,8,128]{2,1,0:T(8,128)S(1)}, u32[]{:S(2)}, u32[]{:S(2)}) collective-permute-start(f32[74,8,128]{2,1,0:T(8,128)S(1)} %get-tuple-element.44), channel_id=1, source_target_pairs={{0,7},{1,0},{2,1},{3,2},{4,3},{5,4},{6,5},{7,6},{8,15},{9,8},{10,9... | collective-permute-start | bytes 909320 | tf_op jit(solution)/shard_map/ppermute | solution.py:719
  32.5 16.1 %all-to-all-start = ((f32[32,16,128]{2,1,0:T(8,128)}), f32[32,16,128]{2,1,0:T(8,128)S(1)}, u32[]{:S(2)}, u32[]{:S(2)}) async-start(f32[32,16,128]{2,1,0:T(8,128)} %get-tuple-element.50), calls=%async_computation | async-start | bytes 524288 | tf_op jit(solution)/shard_map/all_to_all | solution.py:765
  39.3 7.2 %collective-permute-start.6 = (f32[11,8,128]{2,1,0:T(8,128)S(1)}, f32[11,8,128]{2,1,0:T(8,128)S(1)}, u32[]{:S(2)}, u32[]{:S(2)}) collective-permute-start(f32[11,8,128]{2,1,0:T(8,128)S(1)} %get-tuple-element.52), channel_id=1, source_target_pairs={{0,8},{8,16},{16,24},{24,0},{1,9},{9,17},{17,25},{25,1},{2,10},{10... | collective-permute-start | bytes 135176 | tf_op jit(solution)/shard_map/ppermute | solution.py:719
  40.8 5.7 %collective-permute-start.7 = (f32[11,8,128]{2,1,0:T(8,128)S(1)}, f32[11,8,128]{2,1,0:T(8,128)S(1)}, u32[]{:S(2)}, u32[]{:S(2)}) collective-permute-start(f32[11,8,128]{2,1,0:T(8,128)S(1)} %get-tuple-element.53), channel_id=1, source_target_pairs={{0,24},{8,0},{16,8},{24,16},{1,25},{9,1},{17,9},{25,17},{2,26},{10... | collective-permute-start | bytes 135176 | tf_op jit(solution)/shard_map/ppermute | solution.py:719
  51.1 12.8 %all-to-all-start.1 = ((f32[8,4,8,128]{3,2,1,0:T(8,128)}), f32[8,4,8,128]{3,2,1,0:T(8,128)S(1)}, u32[]{:S(2)}, u32[]{:S(2)}) async-start(f32[8,4,8,128]{3,2,1,0:T(8,128)} %get-tuple-element.55), calls=%async_computation.1 | async-start | bytes 262144 | tf_op jit(solution)/shard_map/all_to_all | solution.py:783
  54.7 1.9 %collective-permute-start.8 = (f32[29,8,128]{2,1,0:T(8,128)S(1)}, f32[29,8,128]{2,1,0:T(8,128)S(1)}, u32[]{:S(2)}, u32[]{:S(2)}) collective-permute-start(f32[29,8,128]{2,1,0:T(8,128)S(1)} %get-tuple-element.56), channel_id=1, source_target_pairs={{0,1},{1,2},{2,3},{3,4},{4,5},{5,6},{6,7},{7,0},{8,9},{9,10},{10,1... | collective-permute-start | bytes 356360 | tf_op jit(solution)/shard_map/ppermute | solution.py:719
  54.8 4.6 %collective-permute-start.9 = (f32[29,8,128]{2,1,0:T(8,128)S(1)}, f32[29,8,128]{2,1,0:T(8,128)S(1)}, u32[]{:S(2)}, u32[]{:S(2)}) collective-permute-start(f32[29,8,128]{2,1,0:T(8,128)S(1)} %get-tuple-element.57), channel_id=1, source_target_pairs={{0,7},{1,0},{2,1},{3,2},{4,3},{5,4},{6,5},{7,6},{8,15},{9,8},{10,9... | collective-permute-start | bytes 356360 | tf_op jit(solution)/shard_map/ppermute | solution.py:719

commit v6 on v5

--- a/solution.py
+++ b/solution.py
@@ -306,7 +306,7 @@
 
 def down_kernel(z_low, z_high, *refs):
     fine, F, Q, f1, F1, kept, own1, to_low, to_high, payload = refs[5:15]
-    T, U, V, V1, q1, d1, *w1, sems = refs[15:]
+    T, U, V, V1, q1, d1, *w1, sems, sent, sent_sem = refs[15:]
     S, D0, w0 = split(fine)
     iz, nz = lax.axis_index("gz"), lax.axis_size("gz")
     for p in (0, 31):
@@ -360,7 +360,8 @@
     for j in range(4):
         rows = V1[j, pl.ds(4, 4, 2), :] + V1[j, pl.ds(5, 4, 2), :]
         for d in range(32):
-            payload[d, 4 * j : 4 * j + 4, :] = rows
+            sent[d, 4 * j : 4 * j + 4, :] = rows
+    started += copies(((sent, payload),), sent_sem)
     for copy in started:
         copy.wait()
 
@@ -539,7 +540,7 @@
     refs = refs[5:]
     f3, F3, q3, d3, f4, F4, q4, d4 = refs[:8]
     w3, w4, w2 = refs[8:13], refs[13:18], refs[18:23]
-    T3, g5, F5, qa2, qb2, T2, T2y, qa1, qc1, T1, U1, T0, U0, qa0, qb0, kept_p, kept_r, out_sems = refs[23:]
+    T3, T4, TF3, TF4, g5, F5, qa2, qb2, T2, T2y, qa1, qc1, T1, U1, T0, U0, qa0, qb0, kept_p, kept_r, out_sems = refs[23:]
     lane = index_of((8, 128), 1)
     row = index_of((8, 128), 0)
     zero = jnp.zeros((8, 128), F32)
@@ -550,7 +551,7 @@
     for ref in (f4, F4, q4, d4):
         ref[0] = zero
         ref[9] = zero
-    for field, ref in enumerate((f3, F3)):
+    for field, ref in ((1, F3), (0, f3)):
         for zh in range(2):
             blocks = [got[d, 2 * field + zh] for d in range(8)]
             for zl in range(8):
@@ -560,32 +561,33 @@
                 ref[1 + zh * 8 + zl] = total
 
     three, four = Level(w3), Level(w4)
+    C = gather_pairs(128, 128, 0, 0, 64)
+
+    def to_four(T, out):
+        T[0:8] = matmul(rows_of(T, 8), C).reshape(8, 8, 128)
+        for j in range(8):
+            out[1 + j] = zero
+            out[1 + j, 0:4, :] = T[j, pl.ds(0, 4, 2), :] + T[j, pl.ds(1, 4, 2), :]
+
+    def to_five(T, out):
+        T[0:4] = matmul(rows_of(T, 4), C).reshape(4, 8, 128)
+        for j in range(4):
+            out[2 * j : 2 * j + 2, :] = T[j, pl.ds(0, 2, 2), :] + T[j, pl.ds(1, 2, 2), :]
+
+    halved(F3, TF3, 1, 17)
+    to_four(TF3, F4)
+    halved(F4, TF4, 1, 9)
+    to_five(TF4, F5)
     three.build(F3, 0.25**3, 1, 17, (True, True), 16)
     three.first(f3, q3, 1, 17, 16)
     three.sweep(q3, f3, d3, 1, 17, 16)
-    C = gather_pairs(128, 128, 0, 0, 64)
-    for field in range(2):
-        if field == 0:
-            three.halved_residual(d3, f3, T3, 1, 17, 8)
-        else:
-            halved(F3, T3, 1, 17)
-        T3[0:8] = matmul(rows_of(T3, 8), C).reshape(8, 8, 128)
-        out = (f4, F4)[field]
-        for j in range(8):
-            out[1 + j] = zero
-            out[1 + j, 0:4, :] = T3[j, pl.ds(0, 4, 2), :] + T3[j, pl.ds(1, 4, 2), :]
+    three.halved_residual(d3, f3, T3, 1, 17, 8)
+    to_four(T3, f4)
     four.build(F4, 0.25**4, 1, 9, (False, False), 8)
     four.first(f4, q4, 1, 9, 8)
     four.sweep(q4, f4, d4, 1, 9, 8)
-    for field in range(2):
-        if field == 0:
-            four.halved_residual(d4, f4, T3, 1, 9, 4)
-        else:
-            halved(F4, T3, 1, 9)
-        T3[0:4] = matmul(rows_of(T3, 4), C).reshape(4, 8, 128)
-        out = (g5, F5)[field]
-        for j in range(4):
-            out[2 * j : 2 * j + 2, :] = T3[j, pl.ds(0, 2, 2), :] + T3[j, pl.ds(1, 2, 2), :]
+    four.halved_residual(d4, f4, T4, 1, 9, 4)
+    to_five(T4, g5)
     corr5 = bottom(F5[...], g5[...], 0.5 * 0.25**5)
 
     double = spread_pairs(128, 128, 0, 0, 64)
@@ -757,8 +759,8 @@
         "down",
         "v" * 7,
         [("v", FINE), ("v", BIG), ("v", BIG), ("v", MID), ("v", MID), ("h", FINE)]
-        + [("v", (16, 8, 128)), ("v", rows), ("v", rows), ("v", (32, 16, 128))],
-        [*coarse, (4, 16, 128)] + [MID] * 7 + [dma(10)],
+        + [("v", (16, 8, 128)), ("v", rows), ("v", rows), ("h", (32, 16, 128))],
+        [*coarse, (4, 16, 128)] + [MID] * 7 + [dma(10), (32, 16, 128), dma(1)],
         [(2 + i, i) for i in range(5)],
     )(z_low, z_high, *inner)[5:]
     y_low, y_high = exchange(to_low, to_high, "gy")
@@ -794,7 +796,7 @@
         + [THREE] * 5
         + [FOUR] * 5
         + [WINDOW] * 5
-        + [(9, 8, 128), (8, 128), (8, 128), WINDOW, WINDOW, (2, 6, 8, 128), (6, 16, 128)]
+        + [(9, 8, 128), (4, 8, 128), (8, 8, 128), (4, 8, 128), (8, 128), (8, 128), WINDOW, WINDOW, (2, 6, 8, 128), (6, 16, 128)]
         + [WIDE1] * 2
         + [(8, 24, 128), (8, 16, 128), (12, 24, 256), (2, 12, 32, 128), BIG, BIG, own, own, dma(4)],
     )(got, *one, *kept, fine_inner, fine)

time: 71.6 us -> 70.9 us (level)
  Pallas kernels: 18.8 us -> 18 us
    pallas_call x9, Pallas kernels: 18.8 us -> 18 us  [run(): pl.pallas_call(kernel, out_shape=[kind[k](shape, F32) for k, shape in out...]
where the time goes in v6:
time: 70.9 us; the launch traced here: 70.6 us
  starting transfers between devices  27.7 us (39%)
  waiting for transfers between devices  23.9 us (34%)
  Pallas kernels  18 us (25%)
  between operations  0.88 us (1%)
    pallas_call x9, Pallas kernels, run(): pl.pallas_call(kernel, out_shape=[kind[k](shape, F32) for k, shape in out...  18 us
    ppermute x5, waiting for transfers between devices, exchange(): lax.ppermute(to_high, axis, ring(axis, reach))  11.5 us
    ppermute x5, starting transfers between devices, exchange(): lax.ppermute(to_low, axis, ring(axis, -reach))  9.74 us
    ppermute x5, starting transfers between devices, exchange(): lax.ppermute(to_high, axis, ring(axis, reach))  7.56 us
    all_to_all x1, starting transfers between devices, local(): got = lax.all_to_all(payload, ('gy', 'gz'), 0, 0)  6.85 us
    ppermute x5, waiting for transfers between devices, exchange(): lax.ppermute(to_low, axis, ring(axis, -reach))  6.53 us
    all_to_all x1, waiting for transfers between devices, local(): got = lax.all_to_all(payload, 'gx', 0, 0)  3.96 us
    all_to_all x1, starting transfers between devices, local(): got = lax.all_to_all(payload, 'gx', 0, 0)  3.56 us
  transfers between devices with their start and end apart: 12, of which 9 were waited for; matrix products, arithmetic and copies ran while one was open for 0% of the time, Pallas kernels for 6%

profile of v6, /device:TPU:1, one launch (start us, length us, event | category | flops | bytes accessed | tf_op | source)
XLA Modules:
  0.0 70.6 jit_solution(5436941999109137058)
XLA Ops:
  0.6 1.1 %pack_x.1 = (f32[16,16,128]{2,1,0:T(8,128)S(1)}, f32[16,16,128]{2,1,0:T(8,128)S(1)}, f32[8,16,128]{2,1,0:T(8,128)S(1)}, f32[8,16,128]{2,1,0:T(8,128)S(1)}) custom-call(f32[16,16,128]{2,1,0:T(8,128)} %source.1, f32[16,16,128]{2,1,0:T(8,128)} %fraction.1), custom_call_target="tpu_custom_call" | custom-call | tf_op jit(solution)/shard_map/pack_x/pallas_call | solution.py:701
  1.7 6.5 %collective-permute-start = (f32[8,16,128]{2,1,0:T(8,128)S(1)}, f32[8,16,128]{2,1,0:T(8,128)S(1)}, u32[]{:S(2)}, u32[]{:S(2)}) collective-permute-start(f32[8,16,128]{2,1,0:T(8,128)S(1)} %get-tuple-element.38), channel_id=1, source_target_pairs={{0,224},{32,0},{64,32},{96,64},{128,96},{160,128},{192,160},{224,1... | collective-permute-start | bytes 196616 | tf_op jit(solution)/shard_map/ppermute | solution.py:721
  8.2 0.0 collective-permute-start.1
  8.2 1.3 %collective-permute-done.from_right = f32[8,16,128]{2,1,0:T(8,128)S(1)} collective-permute-done((f32[8,16,128]{2,1,0:T(8,128)S(1)}, f32[8,16,128]{2,1,0:T(8,128)S(1)}, u32[]{:S(2)}, u32[]{:S(2)}) %collective-permute-start) | collective-permute-done | bytes 65568 | tf_op jit(solution)/shard_map/ppermute | solution.py:721
  9.5 3.0 %collective-permute-done.1.from_left = f32[8,16,128]{2,1,0:T(8,128)S(1)} collective-permute-done((f32[8,16,128]{2,1,0:T(8,128)S(1)}, f32[8,16,128]{2,1,0:T(8,128)S(1)}, u32[]{:S(2)}, u32[]{:S(2)}) %collective-permute-start.1) | collective-permute-done | bytes 65568 | tf_op jit(solution)/shard_map/ppermute | solution.py:721
  12.5 0.2 pack_y.1
  12.7 1.3 %collective-permute-start.2 = (f32[20,16,128]{2,1,0:T(8,128)S(1)}, f32[20,16,128]{2,1,0:T(8,128)S(1)}, u32[]{:S(2)}, u32[]{:S(2)}) collective-permute-start(f32[20,16,128]{2,1,0:T(8,128)S(1)} %get-tuple-element.41), channel_id=1, source_target_pairs={{0,8},{8,16},{16,24},{24,0},{1,9},{9,17},{17,25},{25,1},{2,10},{10... | collective-permute-start | bytes 491528 | tf_op jit(solution)/shard_map/ppermute | solution.py:721
  14.0 1.5 %collective-permute-start.3 = (f32[20,16,128]{2,1,0:T(8,128)S(1)}, f32[20,16,128]{2,1,0:T(8,128)S(1)}, u32[]{:S(2)}, u32[]{:S(2)}) collective-permute-start(f32[20,16,128]{2,1,0:T(8,128)S(1)} %get-tuple-element.42), channel_id=1, source_target_pairs={{0,24},{8,0},{16,8},{24,16},{1,25},{9,1},{17,9},{25,17},{2,26},{10... | collective-permute-start | bytes 491528 | tf_op jit(solution)/shard_map/ppermute | solution.py:721
  15.5 2.7 %collective-permute-done.2.from_low = f32[20,16,128]{2,1,0:T(8,128)S(1)} collective-permute-done((f32[20,16,128]{2,1,0:T(8,128)S(1)}, f32[20,16,128]{2,1,0:T(8,128)S(1)}, u32[]{:S(2)}, u32[]{:S(2)}) %collective-permute-start.2) | collective-permute-done | bytes 163872 | tf_op jit(solution)/shard_map/ppermute | solution.py:721
  18.2 0.0 collective-permute-done.3.from_high
  18.2 0.2 pack_z.1
  18.4 4.7 %collective-permute-start.4 = (f32[74,8,128]{2,1,0:T(8,128)S(1)}, f32[74,8,128]{2,1,0:T(8,128)S(1)}, u32[]{:S(2)}, u32[]{:S(2)}) collective-permute-start(f32[74,8,128]{2,1,0:T(8,128)S(1)} %get-tuple-element.43), channel_id=1, source_target_pairs={{0,1},{1,2},{2,3},{3,4},{4,5},{5,6},{6,7},{7,0},{8,9},{9,10},{10,1... | collective-permute-start | bytes 909320 | tf_op jit(solution)/shard_map/ppermute | solution.py:721
  23.1 0.0 collective-permute-start.5
  23.1 3.7 %inner.1 = (f32[7,32,32,256]{3,2,1,0:T(8,128)S(1)}, f32[32,32,256]{2,1,0:T(8,128)S(1)}, f32[32,32,256]{2,1,0:T(8,128)S(1)}, f32[14,16,128]{2,1,0:T(8,128)S(1)}, ...) custom-call(f32[16,16,128]{2,1,0:T(8,128)S(1)} %get-tuple-element.36.s, f32[16,16,128]{2,1,0:T(8,128)S(1)} %get-tuple-element.37.f, ...), custom_call_target="tpu_custom_call" | custom-call | tf_op jit(solution)/shard_map/inner/pallas_call | solution.py:701
  26.9 0.0 collective-permute-done.4.z_low
  26.9 2.5 %collective-permute-done.5.z_high = f32[74,8,128]{2,1,0:T(8,128)S(1)} collective-permute-done((f32[74,8,128]{2,1,0:T(8,128)S(1)}, f32[74,8,128]{2,1,0:T(8,128)S(1)}, u32[]{:S(2)}, u32[]{:S(2)}) %collective-permute-start.5) | collective-permute-done | bytes 303136 | tf_op jit(solution)/shard_map/ppermute | solution.py:721
  29.4 2.9 %down.1 = (f32[7,32,32,256]{3,2,1,0:T(8,128)S(1)}, f32[32,32,256]{2,1,0:T(8,128)S(1)}, f32[32,32,256]{2,1,0:T(8,128)S(1)}, f32[14,16,128]{2,1,0:T(8,128)S(1)}, f...) custom-call(f32[74,8,128]{2,1,0:T(8,128)S(1)} %collective-permute-do, ...), custom_call_target="tpu_custom_call", output_to_operand_aliasing={{0}: (2, {}), {1}: (3, {}), {2}: (4, {}), {3}: (5, {}), {4}... | custom-call | tf_op jit(solution)/shard_map/down/pallas_call | solution.py:701
  32.3 6.8 %all-to-all-start = ((f32[32,16,128]{2,1,0:T(8,128)}), f32[32,16,128]{2,1,0:T(8,128)S(1)}, u32[]{:S(2)}, u32[]{:S(2)}) async-start(f32[32,16,128]{2,1,0:T(8,128)} %get-tuple-element.50), calls=%async_computation | async-start | bytes 524288 | tf_op jit(solution)/shard_map/all_to_all | solution.py:767
  39.1 1.5 %collective-permute-start.6 = (f32[11,8,128]{2,1,0:T(8,128)S(1)}, f32[11,8,128]{2,1,0:T(8,128)S(1)}, u32[]{:S(2)}, u32[]{:S(2)}) collective-permute-start(f32[11,8,128]{2,1,0:T(8,128)S(1)} %get-tuple-element.52), channel_id=1, source_target_pairs={{0,8},{8,16},{16,24},{24,0},{1,9},{9,17},{17,25},{25,1},{2,10},{10... | collective-permute-start | bytes 135176 | tf_op jit(solution)/shard_map/ppermute | solution.py:721
  40.6 1.3 %collective-permute-start.7 = (f32[11,8,128]{2,1,0:T(8,128)S(1)}, f32[11,8,128]{2,1,0:T(8,128)S(1)}, u32[]{:S(2)}, u32[]{:S(2)}) collective-permute-start(f32[11,8,128]{2,1,0:T(8,128)S(1)} %get-tuple-element.53), channel_id=1, source_target_pairs={{0,24},{8,0},{16,8},{24,16},{1,25},{9,1},{17,9},{25,17},{2,26},{10... | collective-permute-start | bytes 135176 | tf_op jit(solution)/shard_map/ppermute | solution.py:721
  41.9 4.4 %collective-permute-done.6.from_low = f32[11,8,128]{2,1,0:T(8,128)S(1)} collective-permute-done((f32[11,8,128]{2,1,0:T(8,128)S(1)}, f32[11,8,128]{2,1,0:T(8,128)S(1)}, u32[]{:S(2)}, u32[]{:S(2)}) %collective-permute-start.6) | collective-permute-done | bytes 45088 | tf_op jit(solution)/shard_map/ppermute | solution.py:721
  46.3 0.0 collective-permute-done.7.from_high
  46.3 0.1 spread_y.1
  46.4 2.0 %all-to-all-done.got = f32[32,16,128]{2,1,0:T(8,128)S(1)} async-done(((f32[32,16,128]{2,1,0:T(8,128)}), f32[32,16,128]{2,1,0:T(8,128)S(1)}, u32[]{:S(2)}, u32[]{:S(2)}) %all-to-all-start) | async-done | bytes 262176 | tf_op jit(solution)/shard_map/all_to_all | solution.py:767
  48.4 2.5 %middle.1 = (f32[8,4,8,128]{3,2,1,0:T(8,128)}, f32[14,16,128]{2,1,0:T(8,128)}, f32[14,16,128]{2,1,0:T(8,128)}, f32[14,16,128]{2,1,0:T(8,128)}) custom-call(f32[32,16,128]{2,1,0:T(8,128)S(1)} %all-to-all-done.got, f32[48,8,128]{2,1,0:T(8,128)S(1)} %get-tuple-element.54.after.rows), custom_call_target="tpu_custom_call" | custom-call | tf_op jit(solution)/shard_map/middle/pallas_call | solution.py:701
  50.9 3.6 %all-to-all-start.1 = ((f32[8,4,8,128]{3,2,1,0:T(8,128)}), f32[8,4,8,128]{3,2,1,0:T(8,128)S(1)}, u32[]{:S(2)}, u32[]{:S(2)}) async-start(f32[8,4,8,128]{3,2,1,0:T(8,128)} %get-tuple-element.55), calls=%async_computation.1 | async-start | bytes 262144 | tf_op jit(solution)/shard_map/all_to_all | solution.py:785
  54.5 0.1 collective-permute-start.8
  54.5 0.4 collective-permute-start.9
  55.0 1.4 %collective-permute-done.8.z_low = f32[29,8,128]{2,1,0:T(8,128)S(1)} collective-permute-done((f32[29,8,128]{2,1,0:T(8,128)S(1)}, f32[29,8,128]{2,1,0:T(8,128)S(1)}, u32[]{:S(2)}, u32[]{:S(2)}) %collective-permute-start.8) | collective-permute-done | bytes 118816 | tf_op jit(solution)/shard_map/ppermute | solution.py:721
  56.4 2.7 %collective-permute-done.9.z_high = f32[29,8,128]{2,1,0:T(8,128)S(1)} collective-permute-done((f32[29,8,128]{2,1,0:T(8,128)S(1)}, f32[29,8,128]{2,1,0:T(8,128)S(1)}, u32[]{:S(2)}, u32[]{:S(2)}) %collective-permute-start.9) | collective-permute-done | bytes 118816 | tf_op jit(solution)/shard_map/ppermute | solution.py:721
  59.1 0.6 wide.1
  59.7 4.0 %all-to-all-done.1.got = f32[8,4,8,128]{3,2,1,0:T(8,128)S(1)} async-done(((f32[8,4,8,128]{3,2,1,0:T(8,128)}), f32[8,4,8,128]{3,2,1,0:T(8,128)S(1)}, u32[]{:S(2)}, u32[]{:S(2)}) %all-to-all-start.1) | async-done | bytes 131104 | tf_op jit(solution)/shard_map/all_to_all | solution.py:785
  63.7 6.7 %up.1 = (f32[16,16,128]{2,1,0:T(8,128)}, f32[16,16,128]{2,1,0:T(8,128)}) custom-call(f32[8,4,8,128]{3,2,1,0:T(8,128)S(1)} %all-to-all-done.1.got, f32[24,24,128]{2,1,0:T(8,128)S(1)} %get-tuple-element.58.refs_0_, f32[24,24,128]{2,1,0:T(8,128)S(1)} %get-tuple-element.59.refs_1_, f32[24,24,128]{2,1,0:T(8,128)S(1)} %get-tuple-element.60.refs_2_, ...), custom_call_target="tpu_custom_call" | custom-call | tf_op jit(solution)/shard_map/up/pallas_call | solution.py:701
Async XLA Ops:
  1.7 7.8 %collective-permute-start = (f32[8,16,128]{2,1,0:T(8,128)S(1)}, f32[8,16,128]{2,1,0:T(8,128)S(1)}, u32[]{:S(2)}, u32[]{:S(2)}) collective-permute-start(f32[8,16,128]{2,1,0:T(8,128)S(1)} %get-tuple-element.38), channel_id=1, source_target_pairs={{0,224},{32,0},{64,32},{96,64},{128,96},{160,128},{192,160},{224,1... | collective-permute-start | bytes 196616 | tf_op jit(solution)/shard_map/ppermute | solution.py:721
  8.2 4.3 %collective-permute-start.1 = (f32[8,16,128]{2,1,0:T(8,128)S(1)}, f32[8,16,128]{2,1,0:T(8,128)S(1)}, u32[]{:S(2)}, u32[]{:S(2)}) collective-permute-start(f32[8,16,128]{2,1,0:T(8,128)S(1)} %get-tuple-element.39), channel_id=1, source_target_pairs={{0,32},{32,64},{64,96},{96,128},{128,160},{160,192},{192,224},{224... | collective-permute-start | bytes 196616 | tf_op jit(solution)/shard_map/ppermute | solution.py:721
  12.7 5.5 %collective-permute-start.2 = (f32[20,16,128]{2,1,0:T(8,128)S(1)}, f32[20,16,128]{2,1,0:T(8,128)S(1)}, u32[]{:S(2)}, u32[]{:S(2)}) collective-permute-start(f32[20,16,128]{2,1,0:T(8,128)S(1)} %get-tuple-element.41), channel_id=1, source_target_pairs={{0,8},{8,16},{16,24},{24,0},{1,9},{9,17},{17,25},{25,1},{2,10},{10... | collective-permute-start | bytes 491528 | tf_op jit(solution)/shard_map/ppermute | solution.py:721
  14.0 4.2 %collective-permute-start.3 = (f32[20,16,128]{2,1,0:T(8,128)S(1)}, f32[20,16,128]{2,1,0:T(8,128)S(1)}, u32[]{:S(2)}, u32[]{:S(2)}) collective-permute-start(f32[20,16,128]{2,1,0:T(8,128)S(1)} %get-tuple-element.42), channel_id=1, source_target_pairs={{0,24},{8,0},{16,8},{24,16},{1,25},{9,1},{17,9},{25,17},{2,26},{10... | collective-permute-start | bytes 491528 | tf_op jit(solution)/shard_map/ppermute | solution.py:721
  18.4 8.5 %collective-permute-start.4 = (f32[74,8,128]{2,1,0:T(8,128)S(1)}, f32[74,8,128]{2,1,0:T(8,128)S(1)}, u32[]{:S(2)}, u32[]{:S(2)}) collective-permute-start(f32[74,8,128]{2,1,0:T(8,128)S(1)} %get-tuple-element.43), channel_id=1, source_target_pairs={{0,1},{1,2},{2,3},{3,4},{4,5},{5,6},{6,7},{7,0},{8,9},{9,10},{10,1... | collective-permute-start | bytes 909320 | tf_op jit(solution)/shard_map/ppermute | solution.py:721
  23.1 6.2 %collective-permute-start.5 = (f32[74,8,128]{2,1,0:T(8,128)S(1)}, f32[74,8,128]{2,1,0:T(8,128)S(1)}, u32[]{:S(2)}, u32[]{:S(2)}) collective-permute-start(f32[74,8,128]{2,1,0:T(8,128)S(1)} %get-tuple-element.44), channel_id=1, source_target_pairs={{0,7},{1,0},{2,1},{3,2},{4,3},{5,4},{6,5},{7,6},{8,15},{9,8},{10,9... | collective-permute-start | bytes 909320 | tf_op jit(solution)/shard_map/ppermute | solution.py:721
  32.3 16.1 %all-to-all-start = ((f32[32,16,128]{2,1,0:T(8,128)}), f32[32,16,128]{2,1,0:T(8,128)S(1)}, u32[]{:S(2)}, u32[]{:S(2)}) async-start(f32[32,16,128]{2,1,0:T(8,128)} %get-tuple-element.50), calls=%async_computation | async-start | bytes 524288 | tf_op jit(solution)/shard_map/all_to_all | solution.py:767
  39.1 7.2 %collective-permute-start.6 = (f32[11,8,128]{2,1,0:T(8,128)S(1)}, f32[11,8,128]{2,1,0:T(8,128)S(1)}, u32[]{:S(2)}, u32[]{:S(2)}) collective-permute-start(f32[11,8,128]{2,1,0:T(8,128)S(1)} %get-tuple-element.52), channel_id=1, source_target_pairs={{0,8},{8,16},{16,24},{24,0},{1,9},{9,17},{17,25},{25,1},{2,10},{10... | collective-permute-start | bytes 135176 | tf_op jit(solution)/shard_map/ppermute | solution.py:721
  40.6 5.7 %collective-permute-start.7 = (f32[11,8,128]{2,1,0:T(8,128)S(1)}, f32[11,8,128]{2,1,0:T(8,128)S(1)}, u32[]{:S(2)}, u32[]{:S(2)}) collective-permute-start(f32[11,8,128]{2,1,0:T(8,128)S(1)} %get-tuple-element.53), channel_id=1, source_target_pairs={{0,24},{8,0},{16,8},{24,16},{1,25},{9,1},{17,9},{25,17},{2,26},{10... | collective-permute-start | bytes 135176 | tf_op jit(solution)/shard_map/ppermute | solution.py:721
  50.9 12.8 %all-to-all-start.1 = ((f32[8,4,8,128]{3,2,1,0:T(8,128)}), f32[8,4,8,128]{3,2,1,0:T(8,128)S(1)}, u32[]{:S(2)}, u32[]{:S(2)}) async-start(f32[8,4,8,128]{3,2,1,0:T(8,128)} %get-tuple-element.55), calls=%async_computation.1 | async-start | bytes 262144 | tf_op jit(solution)/shard_map/all_to_all | solution.py:785
  54.5 1.9 %collective-permute-start.8 = (f32[29,8,128]{2,1,0:T(8,128)S(1)}, f32[29,8,128]{2,1,0:T(8,128)S(1)}, u32[]{:S(2)}, u32[]{:S(2)}) collective-permute-start(f32[29,8,128]{2,1,0:T(8,128)S(1)} %get-tuple-element.56), channel_id=1, source_target_pairs={{0,1},{1,2},{2,3},{3,4},{4,5},{5,6},{6,7},{7,0},{8,9},{9,10},{10,1... | collective-permute-start | bytes 356360 | tf_op jit(solution)/shard_map/ppermute | solution.py:721
  54.5 4.6 %collective-permute-start.9 = (f32[29,8,128]{2,1,0:T(8,128)S(1)}, f32[29,8,128]{2,1,0:T(8,128)S(1)}, u32[]{:S(2)}, u32[]{:S(2)}) collective-permute-start(f32[29,8,128]{2,1,0:T(8,128)S(1)} %get-tuple-element.57), channel_id=1, source_target_pairs={{0,7},{1,0},{2,1},{3,2},{4,3},{5,4},{6,5},{7,6},{8,15},{9,8},{10,9... | collective-permute-start | bytes 356360 | tf_op jit(solution)/shard_map/ppermute | solution.py:721

commit v7 on v6

--- a/solution.py
+++ b/solution.py
@@ -201,7 +201,20 @@
         at += count
 
 
-def pack_y_kernel(s, f, from_right, from_left, halo, to_low, to_high):
+def pack_rows(arrays, first, to_low, to_high):
+    at = sum(ROWS[:first])
+    for count, ref in zip(ROWS[first:], arrays):
+        for j in range(count):
+            to_low[at + j] = ref[:, j, :]
+            to_high[at + j] = ref[:, 16 - count + j, :]
+        at += count
+
+
+def pack_own_kernel(s, f, to_low, to_high):
+    pack_rows((s, f), 0, to_low, to_high)
+
+
+def pack_y_kernel(from_right, from_left, low_in, high_in, halo, to_low, to_high):
     ix = lax.axis_index("gx")
     left = inside(ix > 0)
     right = inside(ix < lax.axis_size("gx") - 1)
@@ -211,12 +224,7 @@
         r, l = from_right[z] * right, from_left[z] * left
         halo[z] = jnp.where(is_right, r, l)
         halo[z + 8] = jnp.where(is_right, turn(r, 96, 1), turn(l, 32, 1))
-    at = 0
-    for count, ref in zip(ROWS, (s, f, halo)):
-        for j in range(count):
-            to_low[at + j] = ref[:, j, :]
-            to_high[at + j] = ref[:, 16 - count + j, :]
-        at += count
+    pack_rows((halo,), 2, to_low, to_high)
 
 
 def pack_z_kernel(s, f, halo, from_low, from_high, to_low, to_high, y_low, y_high):
@@ -736,9 +744,10 @@
     )(source, fraction)
     from_left, from_right = exchange(to_left, to_right, "gx")
     rows = (sum(ROWS), 16, 128)
-    halo, to_low, to_high = call(pack_y_kernel, "pack_y", "vvvv", [("v", own), ("v", rows), ("v", rows)])(
-        s, f, from_right, from_left
-    )
+    started = call(pack_own_kernel, "pack_own", "vv", [("v", rows), ("v", rows)])(s, f)
+    halo, to_low, to_high = call(
+        pack_y_kernel, "pack_y", "vvvv", [("v", own), ("v", rows), ("v", rows)], (), [(2, 1), (3, 2)]
+    )(from_right, from_left, *started)
     y_halos = exchange(to_low, to_high, "gy")
     layers = (len(TILES), 8, 128)
     to_low, to_high = call(pack_z_kernel, "pack_z", "vvvvv", [("v", layers)] * 2, [(3, 16, 8, 128)] * 2)(

time: 70.9 us -> 70.8 us (level)
    pallas_call x9 -> x10, Pallas kernels: 18 us -> 18.1 us  [run(): pl.pallas_call(kernel, out_shape=[kind[k](shape, F32) for k, shape in out...]
where the time goes in v7:
time: 70.8 us; the launch traced here: 70.5 us
  starting transfers between devices  27.7 us (39%)
  waiting for transfers between devices  23.8 us (34%)
  Pallas kernels  18.1 us (26%)
  between operations  0.88 us (1%)
    pallas_call x10, Pallas kernels, run(): pl.pallas_call(kernel, out_shape=[kind[k](shape, F32) for k, shape in out...  18.1 us
    ppermute x5, waiting for transfers between devices, exchange(): lax.ppermute(to_high, axis, ring(axis, reach))  11.5 us
    ppermute x5, starting transfers between devices, exchange(): lax.ppermute(to_low, axis, ring(axis, -reach))  9.74 us
    ppermute x5, starting transfers between devices, exchange(): lax.ppermute(to_high, axis, ring(axis, reach))  7.56 us
    all_to_all x1, starting transfers between devices, local(): got = lax.all_to_all(payload, ('gy', 'gz'), 0, 0)  6.85 us
    ppermute x5, waiting for transfers between devices, exchange(): lax.ppermute(to_low, axis, ring(axis, -reach))  6.41 us
    all_to_all x1, waiting for transfers between devices, local(): got = lax.all_to_all(payload, 'gx', 0, 0)  3.96 us
    all_to_all x1, starting transfers between devices, local(): got = lax.all_to_all(payload, 'gx', 0, 0)  3.56 us
  transfers between devices with their start and end apart: 12, of which 9 were waited for; matrix products, arithmetic and copies ran while one was open for 0% of the time, Pallas kernels for 6%

profile of v7, /device:TPU:1, one launch (start us, length us, event | category | flops | bytes accessed | tf_op | source)
XLA Modules:
  0.0 70.5 jit_solution(3017680254661641867)
XLA Ops:
  0.6 1.1 %pack_x.1 = (f32[16,16,128]{2,1,0:T(8,128)S(1)}, f32[16,16,128]{2,1,0:T(8,128)S(1)}, f32[8,16,128]{2,1,0:T(8,128)S(1)}, f32[8,16,128]{2,1,0:T(8,128)S(1)}) custom-call(f32[16,16,128]{2,1,0:T(8,128)} %source.1, f32[16,16,128]{2,1,0:T(8,128)} %fraction.1), custom_call_target="tpu_custom_call" | custom-call | tf_op jit(solution)/shard_map/pack_x/pallas_call | solution.py:709
  1.7 6.5 %collective-permute-start = (f32[8,16,128]{2,1,0:T(8,128)S(1)}, f32[8,16,128]{2,1,0:T(8,128)S(1)}, u32[]{:S(2)}, u32[]{:S(2)}) collective-permute-start(f32[8,16,128]{2,1,0:T(8,128)S(1)} %get-tuple-element.40), channel_id=1, source_target_pairs={{0,224},{32,0},{64,32},{96,64},{128,96},{160,128},{192,160},{224,1... | collective-permute-start | bytes 196616 | tf_op jit(solution)/shard_map/ppermute | solution.py:729
  8.2 0.0 collective-permute-start.1
  8.2 0.1 pack_own.1
  8.3 1.2 %collective-permute-done.from_right = f32[8,16,128]{2,1,0:T(8,128)S(1)} collective-permute-done((f32[8,16,128]{2,1,0:T(8,128)S(1)}, f32[8,16,128]{2,1,0:T(8,128)S(1)}, u32[]{:S(2)}, u32[]{:S(2)}) %collective-permute-start) | collective-permute-done | bytes 65568 | tf_op jit(solution)/shard_map/ppermute | solution.py:729
  9.5 3.0 %collective-permute-done.1.from_left = f32[8,16,128]{2,1,0:T(8,128)S(1)} collective-permute-done((f32[8,16,128]{2,1,0:T(8,128)S(1)}, f32[8,16,128]{2,1,0:T(8,128)S(1)}, u32[]{:S(2)}, u32[]{:S(2)}) %collective-permute-start.1) | collective-permute-done | bytes 65568 | tf_op jit(solution)/shard_map/ppermute | solution.py:729
  12.5 0.1 pack_y.1
  12.7 1.3 %collective-permute-start.2 = (f32[20,16,128]{2,1,0:T(8,128)S(1)}, f32[20,16,128]{2,1,0:T(8,128)S(1)}, u32[]{:S(2)}, u32[]{:S(2)}) collective-permute-start(f32[20,16,128]{2,1,0:T(8,128)S(1)} %get-tuple-element.45), channel_id=1, source_target_pairs={{0,8},{8,16},{16,24},{24,0},{1,9},{9,17},{17,25},{25,1},{2,10},{10... | collective-permute-start | bytes 491528 | tf_op jit(solution)/shard_map/ppermute | solution.py:729
  14.0 1.5 %collective-permute-start.3 = (f32[20,16,128]{2,1,0:T(8,128)S(1)}, f32[20,16,128]{2,1,0:T(8,128)S(1)}, u32[]{:S(2)}, u32[]{:S(2)}) collective-permute-start(f32[20,16,128]{2,1,0:T(8,128)S(1)} %get-tuple-element.46), channel_id=1, source_target_pairs={{0,24},{8,0},{16,8},{24,16},{1,25},{9,1},{17,9},{25,17},{2,26},{10... | collective-permute-start | bytes 491528 | tf_op jit(solution)/shard_map/ppermute | solution.py:729
  15.4 2.7 %collective-permute-done.2.from_low = f32[20,16,128]{2,1,0:T(8,128)S(1)} collective-permute-done((f32[20,16,128]{2,1,0:T(8,128)S(1)}, f32[20,16,128]{2,1,0:T(8,128)S(1)}, u32[]{:S(2)}, u32[]{:S(2)}) %collective-permute-start.2) | collective-permute-done | bytes 163872 | tf_op jit(solution)/shard_map/ppermute | solution.py:729
  18.1 0.0 collective-permute-done.3.from_high
  18.1 0.2 pack_z.1
  18.3 4.7 %collective-permute-start.4 = (f32[74,8,128]{2,1,0:T(8,128)S(1)}, f32[74,8,128]{2,1,0:T(8,128)S(1)}, u32[]{:S(2)}, u32[]{:S(2)}) collective-permute-start(f32[74,8,128]{2,1,0:T(8,128)S(1)} %get-tuple-element.47), channel_id=1, source_target_pairs={{0,1},{1,2},{2,3},{3,4},{4,5},{5,6},{6,7},{7,0},{8,9},{9,10},{10,1... | collective-permute-start | bytes 909320 | tf_op jit(solution)/shard_map/ppermute | solution.py:729
  23.1 0.0 collective-permute-start.5
  23.1 3.7 %inner.1 = (f32[7,32,32,256]{3,2,1,0:T(8,128)S(1)}, f32[32,32,256]{2,1,0:T(8,128)S(1)}, f32[32,32,256]{2,1,0:T(8,128)S(1)}, f32[14,16,128]{2,1,0:T(8,128)S(1)}, ...) custom-call(f32[16,16,128]{2,1,0:T(8,128)S(1)} %get-tuple-element.38.s, f32[16,16,128]{2,1,0:T(8,128)S(1)} %get-tuple-element.39.f, ...), custom_call_target="tpu_custom_call" | custom-call | tf_op jit(solution)/shard_map/inner/pallas_call | solution.py:709
  26.8 0.0 collective-permute-done.4.z_low
  26.8 2.5 %collective-permute-done.5.z_high = f32[74,8,128]{2,1,0:T(8,128)S(1)} collective-permute-done((f32[74,8,128]{2,1,0:T(8,128)S(1)}, f32[74,8,128]{2,1,0:T(8,128)S(1)}, u32[]{:S(2)}, u32[]{:S(2)}) %collective-permute-start.5) | collective-permute-done | bytes 303136 | tf_op jit(solution)/shard_map/ppermute | solution.py:729
  29.3 2.9 %down.1 = (f32[7,32,32,256]{3,2,1,0:T(8,128)S(1)}, f32[32,32,256]{2,1,0:T(8,128)S(1)}, f32[32,32,256]{2,1,0:T(8,128)S(1)}, f32[14,16,128]{2,1,0:T(8,128)S(1)}, f...) custom-call(f32[74,8,128]{2,1,0:T(8,128)S(1)} %collective-permute-do, ...), custom_call_target="tpu_custom_call", output_to_operand_aliasing={{0}: (2, {}), {1}: (3, {}), {2}: (4, {}), {3}: (5, {}), {4}... | custom-call | tf_op jit(solution)/shard_map/down/pallas_call | solution.py:709
  32.2 6.9 %all-to-all-start = ((f32[32,16,128]{2,1,0:T(8,128)}), f32[32,16,128]{2,1,0:T(8,128)S(1)}, u32[]{:S(2)}, u32[]{:S(2)}) async-start(f32[32,16,128]{2,1,0:T(8,128)} %get-tuple-element.54), calls=%async_computation | async-start | bytes 524288 | tf_op jit(solution)/shard_map/all_to_all | solution.py:776
  39.0 1.5 %collective-permute-start.6 = (f32[11,8,128]{2,1,0:T(8,128)S(1)}, f32[11,8,128]{2,1,0:T(8,128)S(1)}, u32[]{:S(2)}, u32[]{:S(2)}) collective-permute-start(f32[11,8,128]{2,1,0:T(8,128)S(1)} %get-tuple-element.56), channel_id=1, source_target_pairs={{0,8},{8,16},{16,24},{24,0},{1,9},{9,17},{17,25},{25,1},{2,10},{10... | collective-permute-start | bytes 135176 | tf_op jit(solution)/shard_map/ppermute | solution.py:729
  40.5 1.3 %collective-permute-start.7 = (f32[11,8,128]{2,1,0:T(8,128)S(1)}, f32[11,8,128]{2,1,0:T(8,128)S(1)}, u32[]{:S(2)}, u32[]{:S(2)}) collective-permute-start(f32[11,8,128]{2,1,0:T(8,128)S(1)} %get-tuple-element.57), channel_id=1, source_target_pairs={{0,24},{8,0},{16,8},{24,16},{1,25},{9,1},{17,9},{25,17},{2,26},{10... | collective-permute-start | bytes 135176 | tf_op jit(solution)/shard_map/ppermute | solution.py:729
  41.9 4.4 %collective-permute-done.6.from_low = f32[11,8,128]{2,1,0:T(8,128)S(1)} collective-permute-done((f32[11,8,128]{2,1,0:T(8,128)S(1)}, f32[11,8,128]{2,1,0:T(8,128)S(1)}, u32[]{:S(2)}, u32[]{:S(2)}) %collective-permute-start.6) | collective-permute-done | bytes 45088 | tf_op jit(solution)/shard_map/ppermute | solution.py:729
  46.2 0.0 collective-permute-done.7.from_high
  46.3 0.1 spread_y.1
  46.4 2.0 %all-to-all-done.got = f32[32,16,128]{2,1,0:T(8,128)S(1)} async-done(((f32[32,16,128]{2,1,0:T(8,128)}), f32[32,16,128]{2,1,0:T(8,128)S(1)}, u32[]{:S(2)}, u32[]{:S(2)}) %all-to-all-start) | async-done | bytes 262176 | tf_op jit(solution)/shard_map/all_to_all | solution.py:776
  48.3 2.5 %middle.1 = (f32[8,4,8,128]{3,2,1,0:T(8,128)}, f32[14,16,128]{2,1,0:T(8,128)}, f32[14,16,128]{2,1,0:T(8,128)}, f32[14,16,128]{2,1,0:T(8,128)}) custom-call(f32[32,16,128]{2,1,0:T(8,128)S(1)} %all-to-all-done.got, f32[48,8,128]{2,1,0:T(8,128)S(1)} %get-tuple-element.58.after.rows), custom_call_target="tpu_custom_call" | custom-call | tf_op jit(solution)/shard_map/middle/pallas_call | solution.py:709
  50.8 3.6 %all-to-all-start.1 = ((f32[8,4,8,128]{3,2,1,0:T(8,128)}), f32[8,4,8,128]{3,2,1,0:T(8,128)S(1)}, u32[]{:S(2)}, u32[]{:S(2)}) async-start(f32[8,4,8,128]{3,2,1,0:T(8,128)} %get-tuple-element.59), calls=%async_computation.1 | async-start | bytes 262144 | tf_op jit(solution)/shard_map/all_to_all | solution.py:794
  54.4 0.1 collective-permute-start.8
  54.5 0.4 collective-permute-start.9
  54.9 1.4 %collective-permute-done.8.z_low = f32[29,8,128]{2,1,0:T(8,128)S(1)} collective-permute-done((f32[29,8,128]{2,1,0:T(8,128)S(1)}, f32[29,8,128]{2,1,0:T(8,128)S(1)}, u32[]{:S(2)}, u32[]{:S(2)}) %collective-permute-start.8) | collective-permute-done | bytes 118816 | tf_op jit(solution)/shard_map/ppermute | solution.py:729
  56.3 2.7 %collective-permute-done.9.z_high = f32[29,8,128]{2,1,0:T(8,128)S(1)} collective-permute-done((f32[29,8,128]{2,1,0:T(8,128)S(1)}, f32[29,8,128]{2,1,0:T(8,128)S(1)}, u32[]{:S(2)}, u32[]{:S(2)}) %collective-permute-start.9) | collective-permute-done | bytes 118816 | tf_op jit(solution)/shard_map/ppermute | solution.py:729
  59.0 0.6 wide.1
  59.6 4.0 %all-to-all-done.1.got = f32[8,4,8,128]{3,2,1,0:T(8,128)S(1)} async-done(((f32[8,4,8,128]{3,2,1,0:T(8,128)}), f32[8,4,8,128]{3,2,1,0:T(8,128)S(1)}, u32[]{:S(2)}, u32[]{:S(2)}) %all-to-all-start.1) | async-done | bytes 131104 | tf_op jit(solution)/shard_map/all_to_all | solution.py:794
  63.6 6.7 %up.1 = (f32[16,16,128]{2,1,0:T(8,128)}, f32[16,16,128]{2,1,0:T(8,128)}) custom-call(f32[8,4,8,128]{3,2,1,0:T(8,128)S(1)} %all-to-all-done.1.got, f32[24,24,128]{2,1,0:T(8,128)S(1)} %get-tuple-element.62.refs_0_, f32[24,24,128]{2,1,0:T(8,128)S(1)} %get-tuple-element.63.refs_1_, f32[24,24,128]{2,1,0:T(8,128)S(1)} %get-tuple-element.64.refs_2_, ...), custom_call_target="tpu_custom_call" | custom-call | tf_op jit(solution)/shard_map/up/pallas_call | solution.py:709
Async XLA Ops:
  1.7 7.8 %collective-permute-start = (f32[8,16,128]{2,1,0:T(8,128)S(1)}, f32[8,16,128]{2,1,0:T(8,128)S(1)}, u32[]{:S(2)}, u32[]{:S(2)}) collective-permute-start(f32[8,16,128]{2,1,0:T(8,128)S(1)} %get-tuple-element.40), channel_id=1, source_target_pairs={{0,224},{32,0},{64,32},{96,64},{128,96},{160,128},{192,160},{224,1... | collective-permute-start | bytes 196616 | tf_op jit(solution)/shard_map/ppermute | solution.py:729
  8.2 4.3 %collective-permute-start.1 = (f32[8,16,128]{2,1,0:T(8,128)S(1)}, f32[8,16,128]{2,1,0:T(8,128)S(1)}, u32[]{:S(2)}, u32[]{:S(2)}) collective-permute-start(f32[8,16,128]{2,1,0:T(8,128)S(1)} %get-tuple-element.41), channel_id=1, source_target_pairs={{0,32},{32,64},{64,96},{96,128},{128,160},{160,192},{192,224},{224... | collective-permute-start | bytes 196616 | tf_op jit(solution)/shard_map/ppermute | solution.py:729
  12.7 5.5 %collective-permute-start.2 = (f32[20,16,128]{2,1,0:T(8,128)S(1)}, f32[20,16,128]{2,1,0:T(8,128)S(1)}, u32[]{:S(2)}, u32[]{:S(2)}) collective-permute-start(f32[20,16,128]{2,1,0:T(8,128)S(1)} %get-tuple-element.45), channel_id=1, source_target_pairs={{0,8},{8,16},{16,24},{24,0},{1,9},{9,17},{17,25},{25,1},{2,10},{10... | collective-permute-start | bytes 491528 | tf_op jit(solution)/shard_map/ppermute | solution.py:729
  14.0 4.2 %collective-permute-start.3 = (f32[20,16,128]{2,1,0:T(8,128)S(1)}, f32[20,16,128]{2,1,0:T(8,128)S(1)}, u32[]{:S(2)}, u32[]{:S(2)}) collective-permute-start(f32[20,16,128]{2,1,0:T(8,128)S(1)} %get-tuple-element.46), channel_id=1, source_target_pairs={{0,24},{8,0},{16,8},{24,16},{1,25},{9,1},{17,9},{25,17},{2,26},{10... | collective-permute-start | bytes 491528 | tf_op jit(solution)/shard_map/ppermute | solution.py:729
  18.3 8.5 %collective-permute-start.4 = (f32[74,8,128]{2,1,0:T(8,128)S(1)}, f32[74,8,128]{2,1,0:T(8,128)S(1)}, u32[]{:S(2)}, u32[]{:S(2)}) collective-permute-start(f32[74,8,128]{2,1,0:T(8,128)S(1)} %get-tuple-element.47), channel_id=1, source_target_pairs={{0,1},{1,2},{2,3},{3,4},{4,5},{5,6},{6,7},{7,0},{8,9},{9,10},{10,1... | collective-permute-start | bytes 909320 | tf_op jit(solution)/shard_map/ppermute | solution.py:729
  23.1 6.2 %collective-permute-start.5 = (f32[74,8,128]{2,1,0:T(8,128)S(1)}, f32[74,8,128]{2,1,0:T(8,128)S(1)}, u32[]{:S(2)}, u32[]{:S(2)}) collective-permute-start(f32[74,8,128]{2,1,0:T(8,128)S(1)} %get-tuple-element.48), channel_id=1, source_target_pairs={{0,7},{1,0},{2,1},{3,2},{4,3},{5,4},{6,5},{7,6},{8,15},{9,8},{10,9... | collective-permute-start | bytes 909320 | tf_op jit(solution)/shard_map/ppermute | solution.py:729
  32.2 16.1 %all-to-all-start = ((f32[32,16,128]{2,1,0:T(8,128)}), f32[32,16,128]{2,1,0:T(8,128)S(1)}, u32[]{:S(2)}, u32[]{:S(2)}) async-start(f32[32,16,128]{2,1,0:T(8,128)} %get-tuple-element.54), calls=%async_computation | async-start | bytes 524288 | tf_op jit(solution)/shard_map/all_to_all | solution.py:776
  39.0 7.2 %collective-permute-start.6 = (f32[11,8,128]{2,1,0:T(8,128)S(1)}, f32[11,8,128]{2,1,0:T(8,128)S(1)}, u32[]{:S(2)}, u32[]{:S(2)}) collective-permute-start(f32[11,8,128]{2,1,0:T(8,128)S(1)} %get-tuple-element.56), channel_id=1, source_target_pairs={{0,8},{8,16},{16,24},{24,0},{1,9},{9,17},{17,25},{25,1},{2,10},{10... | collective-permute-start | bytes 135176 | tf_op jit(solution)/shard_map/ppermute | solution.py:729
  40.5 5.7 %collective-permute-start.7 = (f32[11,8,128]{2,1,0:T(8,128)S(1)}, f32[11,8,128]{2,1,0:T(8,128)S(1)}, u32[]{:S(2)}, u32[]{:S(2)}) collective-permute-start(f32[11,8,128]{2,1,0:T(8,128)S(1)} %get-tuple-element.57), channel_id=1, source_target_pairs={{0,24},{8,0},{16,8},{24,16},{1,25},{9,1},{17,9},{25,17},{2,26},{10... | collective-permute-start | bytes 135176 | tf_op jit(solution)/shard_map/ppermute | solution.py:729
  50.8 12.8 %all-to-all-start.1 = ((f32[8,4,8,128]{3,2,1,0:T(8,128)}), f32[8,4,8,128]{3,2,1,0:T(8,128)S(1)}, u32[]{:S(2)}, u32[]{:S(2)}) async-start(f32[8,4,8,128]{3,2,1,0:T(8,128)} %get-tuple-element.59), calls=%async_computation.1 | async-start | bytes 262144 | tf_op jit(solution)/shard_map/all_to_all | solution.py:794
  54.4 1.9 %collective-permute-start.8 = (f32[29,8,128]{2,1,0:T(8,128)S(1)}, f32[29,8,128]{2,1,0:T(8,128)S(1)}, u32[]{:S(2)}, u32[]{:S(2)}) collective-permute-start(f32[29,8,128]{2,1,0:T(8,128)S(1)} %get-tuple-element.60), channel_id=1, source_target_pairs={{0,1},{1,2},{2,3},{3,4},{4,5},{5,6},{6,7},{7,0},{8,9},{9,10},{10,1... | collective-permute-start | bytes 356360 | tf_op jit(solution)/shard_map/ppermute | solution.py:729
  54.5 4.6 %collective-permute-start.9 = (f32[29,8,128]{2,1,0:T(8,128)S(1)}, f32[29,8,128]{2,1,0:T(8,128)S(1)}, u32[]{:S(2)}, u32[]{:S(2)}) collective-permute-start(f32[29,8,128]{2,1,0:T(8,128)S(1)} %get-tuple-element.61), channel_id=1, source_target_pairs={{0,7},{1,0},{2,1},{3,2},{4,3},{5,4},{6,5},{7,6},{8,15},{9,8},{10,9... | collective-permute-start | bytes 356360 | tf_op jit(solution)/shard_map/ppermute | solution.py:729
